TPU v7x, 32 devices: a whole 2x2x4 slice. The times are simulated.
32 devices in a mesh: dp: 8 (over z, x), mp: 4 (over y, core).
Axes of the slice: x: 2, y: 2, z: 4, core: 2. Of those that a mesh axis runs over, the one named last changes fastest.
Arguments:
- hidden: bfloat16 [4096, 1536], P('dp'), may hold values from -6 to 6
- segment_ids: int32 [4096], replicated, may hold values from 0 to 2, as said below
- routes: int32 [4096, 6], P('dp'), may hold values from 0 to 63, all different within a row; in each aligned block of 512 rows (0 to 511, 512 to 1023, ...) at most 64 rows name the same one
- norm_gain: bfloat16 [1536], P('dp'), may hold values from 0.5 to 1.5
- mixer_in: bfloat16 [1536, 2, 3072], P('dp', None, 'mp'), may hold values from -0.15625 to 0.15625
- state_in: bfloat16 [1536, 256], P('dp'), may hold values from -0.15625 to 0.15625
- step_in: bfloat16 [1536, 48], P('dp', 'mp'), may hold values from -0.15625 to 0.15625
- conv_value: bfloat16 [4, 64, 48], P(None, 'dp', 'mp'), may hold values from -3 to 3
- conv_value_bias: bfloat16 [64, 48], P('dp', 'mp'), may hold values from -3 to 3
- conv_state: bfloat16 [4, 256], P(None, 'dp'), may hold values from -3 to 3
- conv_state_bias: bfloat16 [256], P('dp'), may hold values from -3 to 3
- head_params: bfloat16 [3, 48], P(None, 'mp')
- gated_gain: bfloat16 [64, 48], P('dp', 'mp'), may hold values from 0.5 to 1.5
- mixer_out: bfloat16 [3072, 1536], P('mp', 'dp'), may hold values from -0.109375 to 0.109375
- ffn_gain: bfloat16 [1536], P('dp'), may hold values from 0.5 to 1.5
- router: bfloat16 [1536, 64], P('dp'), may hold values from -0.078125 to 0.078125
- shared_in: bfloat16 [1536, 2, 1024], P('dp', None, 'mp'), may hold values from -0.15625 to 0.15625
- shared_out: bfloat16 [1024, 1536], P('mp', 'dp'), may hold values from -0.1875 to 0.1875
- expert_in: bfloat16 [64, 1536, 2, 512], P('dp', None, None, 'mp'), may hold values from -0.15625 to 0.15625
- expert_out: bfloat16 [64, 512, 1536], P('dp', 'mp'), may hold values from -0.25 to 0.25
- cotangent: bfloat16 [4096, 1536], P('dp'), may hold values from -6 to 6
Outputs:
- result: bfloat16 [4096, 1536], P('dp')
- grad_hidden: float32 [4096, 1536], P('dp')
- grad_norm_gain: float32 [1536], P('dp')
- grad_mixer_in: float32 [1536, 2, 3072], P('dp', None, 'mp')
- grad_state_in: float32 [1536, 256], P('dp')
- grad_step_in: float32 [1536, 48], P('dp', 'mp')
- grad_conv_value: float32 [4, 64, 48], P(None, 'dp', 'mp')
- grad_conv_value_bias: float32 [64, 48], P('dp', 'mp')
- grad_conv_state: float32 [4, 256], P(None, 'dp')
- grad_conv_state_bias: float32 [256], P('dp')
- grad_head_params: float32 [3, 48], P(None, 'mp')
- grad_gated_gain: float32 [64, 48], P('dp', 'mp')
- grad_mixer_out: float32 [3072, 1536], P('mp', 'dp')
- grad_ffn_gain: float32 [1536], P('dp')
- grad_router: float32 [1536, 64], P('dp')
- grad_shared_in: float32 [1536, 2, 1024], P('dp', None, 'mp')
- grad_shared_out: float32 [1024, 1536], P('mp', 'dp')
- grad_expert_in: float32 [64, 1536, 2, 512], P('dp', None, None, 'mp')
- grad_expert_out: float32 [64, 512, 1536], P('dp', 'mp')
Inputs may be any that keep to these rules, and one draw needn't show every extreme that they name: `segment_ids`: never falling; 0 up to a position inside the first 512 tokens, 2 from a position inside the last 512 tokens, 1 between. `routes`: in each aligned block of 512 rows no expert is named by more than 64 rows, a bound that some block reaches.
All inputs are finite; a program needn't handle non-finite values.
Results may differ from a plain program's by a relative error of at most 0.02.
The roundings to bfloat16 on the way count: a program that leaves them out, or rounds other values in their place, can miss the bound.
Values may be sent and summed in bfloat16 or wider, within the bound.
A program may use at most 320 MiB of HBM per device.

v0:
```python
from functools import partial

import jax
import jax.numpy as jnp
from jax import lax
from jax.experimental import pallas as pl
from jax.experimental.pallas import tpu as pltpu
from jax.sharding import PartitionSpec as P

MESH = pl.DeviceIdType.MESH
BLK = 128
EXPERTS = 64
TOPK = 6
DI = 3072
CAP = 64
LANES = 128

EPS = 1e-05
HIGH = lax.Precision.HIGHEST
MASKED = -1e30
BF = jnp.bfloat16
F32 = jnp.float32
ANY = pl.BlockSpec(memory_space=pl.ANY)
VM = pl.BlockSpec(memory_space=pltpu.VMEM)


def dot(a, b, dims=((1,), (0,)), precision=None):
    return lax.dot_general(
        a, b, (dims, ((), ())), precision=precision, preferred_element_type=F32
    )


def two_parts(a):
    high = a.astype(BF)
    return high, (a - high.astype(F32)).astype(BF)


def dot_three(a, b, over):
    a_high, a_low = two_parts(a)
    b_high, b_low = two_parts(b)
    left = jnp.concatenate([a_high, a_low, a_high], axis=over[0])
    right = jnp.concatenate([b_high, b_high, b_low], axis=over[1])
    return dot(left, right, ((over[0],), (over[1],)))


def silu_slope(argument):
    sigmoid_val = jax.nn.sigmoid(argument)
    return sigmoid_val * (1.0 + argument * (1.0 - sigmoid_val))


def chunk_rows(start, size):
    return [(start + i, min(32, size - i)) for i in range(0, size, 32)]


def ring_place(n, d):
    high, low = d // 2, d % 2
    return high * (1 - low) + (n - 1 - high) * low


def ring_device(n, p):
    back = p // (n // 2)
    return (2 * p) * (1 - back) + (2 * (n - 1 - p) + 1) * back


def greet(targets):
    barrier = pltpu.get_barrier_semaphore()
    for target in targets:
        pl.semaphore_signal(barrier, inc=1, device_id=target, device_id_type=MESH)
    pl.semaphore_wait(barrier, len(targets))


def remote(src, dst, send, recv, target):
    return pltpu.make_async_remote_copy(
        src_ref=src,
        dst_ref=dst,
        send_sem=send,
        recv_sem=recv,
        device_id=target,
        device_id_type=MESH,
    )


def mp_partners(m):
    return {"mp": m + 1 - 2 * (m % 2)}, {"mp": (m + 2) % 4}


def ring_neighbours(n):
    p = ring_place(n, lax.axis_index("dp"))
    nxt = {"dp": ring_device(n, (p + 1) % n)}
    prv = {"dp": ring_device(n, (p + n - 1) % n)}
    return p, nxt, prv


class RingGather:
    def __init__(self, n, ins, outs, sems):
        self.n, self.ins, self.outs = n, ins, outs
        self.local_sem, self.send_sem, self.recv_sem = sems
        self.p, self.nxt, self.prv = ring_neighbours(n)
        self.copies = {}

    @staticmethod
    def scratch(n, arrays):
        dma = pltpu.SemaphoreType.DMA
        most = max(len(chunk_rows(0, a.shape[0])) for a in arrays)
        shape = (n // 2, len(arrays), most, 2)
        return [dma((len(arrays),)), dma(shape), dma(shape)]

    def begin(self):
        d = lax.axis_index("dp")
        self.local = []
        for j, (a, out) in enumerate(zip(self.ins, self.outs)):
            copy = pltpu.make_async_copy(a, out.at[d], self.local_sem.at[j])
            copy.start()
            self.local.append(copy)

    def step(self, s):
        n, p = self.n, self.p
        for j, (a, out) in enumerate(zip(self.ins, self.outs)):
            for i, (start, rows) in enumerate(chunk_rows(0, a.shape[0])):
                part = pl.ds(start, rows)
                for way in range(2):
                    origin = ring_device(n, (p + n - s) % n if way == 0 else (p + s) % n)
                    if (s - 1, j, i, way) in self.copies:
                        self.copies[s - 1, j, i, way].wait_recv()
                    if s + 1 < n // 2 or (s + 1 == n // 2 and i % 2 == way):
                        copy = remote(
                            a.at[part] if s == 0 else out.at[origin, part],
                            out.at[origin, part],
                            self.send_sem.at[s, j, i, way],
                            self.recv_sem.at[s, j, i, way],
                            self.nxt if way == 0 else self.prv,
                        )
                        copy.start()
                        self.copies[s, j, i, way] = copy

    def end(self):
        for copy in self.copies.values():
            copy.wait_send()
        for copy in self.local:
            copy.wait()


def gather_kernel(n, k, *refs):
    ring = RingGather(n, refs[:k], refs[k : 2 * k], refs[2 * k :])
    greet([ring.nxt, ring.prv])
    ring.begin()
    for s in range(n // 2 + 1):
        ring.step(s)
    ring.end()


def gather_dp(arrays, cid):
    n, k = lax.axis_size("dp"), len(arrays)
    return pl.pallas_call(
        partial(gather_kernel, n, k),
        out_shape=[jax.ShapeDtypeStruct((n,) + a.shape, a.dtype) for a in arrays],
        in_specs=[ANY] * k,
        out_specs=[ANY] * k,
        scratch_shapes=RingGather.scratch(n, arrays),
        compiler_params=pltpu.CompilerParams(collective_id=cid, has_side_effects=True),
    )(*arrays)


def add_rows(dst, pieces, rows, dtype):
    def body(i, carry):
        sl = pl.ds(pl.multiple_of(i * 16, 16), 16)
        total = pieces[0][sl, :].astype(F32)
        for piece in pieces[1:]:
            total = total + piece[sl, :].astype(F32)
        dst[sl, :] = total.astype(dtype)
        return carry

    lax.fori_loop(0, rows // 16, body, 0)


class RingScatter:
    def __init__(self, n, ins, outs, slots, sems):
        self.n, self.ins, self.outs, self.slots = n, ins, outs, slots
        self.send_sem, self.recv_sem = sems
        self.p, self.nxt, self.prv = ring_neighbours(n)
        self.copies = {}

    @staticmethod
    def scratch(n, arrays):
        most = max(len(chunk_rows(0, a.shape[1])) for a in arrays)
        shape = (n // 2, len(arrays), most, 2)
        return [pltpu.VMEM((n // 2, 2) + a.shape[1:], a.dtype) for a in arrays] + [
            pltpu.SemaphoreType.DMA(shape),
            pltpu.SemaphoreType.DMA(shape),
        ]

    def step(self, s, j):
        n, p = self.n, self.p
        array, out, slots = self.ins[j], self.outs[j], self.slots[j]
        for i, (start, size) in enumerate(chunk_rows(0, array.shape[1])):
            part = pl.ds(start, size)
            if s == n // 2:
                for way in range(2):
                    self.copies[s - 1, j, i, way].wait_recv()
                mine = array.at[ring_device(n, p), part]
                add_rows(out.at[part], [mine, slots.at[s - 1, 0, part], slots.at[s - 1, 1, part]], size, F32)
                continue
            for way in range(2):
                if s == 0 and i % 2 != way:
                    continue
                away = n // 2 - s
                block = ring_device(n, (p + away) % n if way == 0 else (p + n - away) % n)
                source = array.at[block, part]
                if (s - 1, j, i, way) in self.copies:
                    self.copies[s - 1, j, i, way].wait_recv()
                    held = slots.at[s - 1, way, part]
                    add_rows(held, [held, source], size, array.dtype)
                    source = held
                copy = remote(
                    source,
                    slots.at[s, way, part],
                    self.send_sem.at[s, j, i, way],
                    self.recv_sem.at[s, j, i, way],
                    self.nxt if way == 0 else self.prv,
                )
                copy.start()
                self.copies[s, j, i, way] = copy

    def end(self):
        for copy in self.copies.values():
            copy.wait_send()


def last_kernel(
    n,
    grad_a,
    misc,
    gains,
    d_normed,
    extra,
    d_mixed,
    hidden,
    gain,
    result,
    out_a,
    out_misc,
    out_gains,
    all_hidden,
    all_result,
    gains_mine,
    gains_core,
    gains_chip,
    rows_core,
    rows_chip,
    rows_bf,
    slots_a,
    slots_misc,
    slots_gains,
    ring_send,
    ring_recv,
    mp_send,
    mp_recv,
    local_sem,
):
    m = lax.axis_index("mp")
    core, chip = mp_partners(m)
    far = (m + 2) % 4
    beside = m + 1 - 2 * (m % 2)
    ring = RingScatter(
        n,
        [grad_a, misc, gains_mine],
        [out_a, out_misc, out_gains],
        [slots_a, slots_misc, slots_gains],
        [ring_send, ring_recv],
    )
    greet([core, chip, ring.nxt, ring.prv])
    sent = []

    def over_mp(i, source, target, device):
        copy = remote(source, target, mp_send.at[i], mp_recv.at[i], device)
        copy.start()
        sent.append(copy)
        return copy

    ring.step(0, 0)
    ring.step(0, 1)
    gains_one = over_mp(0, gains, gains_core, core)
    rows_far = over_mp(1, d_normed.at[(beside + 2) % 4], rows_core.at[1], core)
    rows_near = over_mp(2, d_normed.at[beside], rows_core.at[0], core)
    own_result = pltpu.make_async_copy(result, all_result.at[m], local_sem.at[0])
    own_result.start()
    gains_one.wait_recv()
    for b in range(n):
        add_rows(gains_mine.at[b], [gains.at[b], gains_core.at[b]], 16, F32)
    gains_two = over_mp(3, gains_mine, gains_chip, chip)
    count = d_mixed.shape[0]
    rows_far.wait_recv()
    add_rows(rows_core.at[1], [rows_core.at[1], d_normed.at[far]], count, BF)
    rows_two = over_mp(4, rows_core.at[1], rows_chip, chip)
    result_chip = over_mp(5, result, all_result.at[m], chip)
    result_core = over_mp(6, result, all_result.at[m], core)
    ring.step(1, 0)
    ring.step(1, 1)
    gains_two.wait()
    for b in range(n):
        add_rows(gains_mine.at[b], [gains_mine.at[b], gains_chip.at[b]], 16, F32)
    ring.step(0, 2)
    rows_near.wait_recv()
    rows_two.wait_recv()

    def body(i, carry):
        sl = pl.ds(pl.multiple_of(i * 16, 16), 16)
        d_n = d_normed[m, sl, :].astype(F32) + rows_core[0, sl, :].astype(F32)
        d_n = d_n + rows_chip[sl, :].astype(F32) + extra[sl, :]
        x = hidden[sl, :].astype(F32)
        inv = lax.rsqrt(jnp.mean(x * x, axis=1, keepdims=True) + EPS)
        unit = x * inv
        d_unit = d_n * gain[...]
        mean = jnp.mean(d_unit * unit, axis=1, keepdims=True)
        rows_bf[sl, :] = (d_mixed[sl, :] + inv * (d_unit - unit * mean)).astype(BF)
        return carry

    lax.fori_loop(0, count // 16, body, 0)
    own_hidden = pltpu.make_async_copy(rows_bf, all_hidden.at[m], local_sem.at[1])
    own_hidden.start()
    hidden_chip = over_mp(7, rows_bf, all_hidden.at[m], chip)
    hidden_core = over_mp(8, rows_bf, all_hidden.at[m], core)
    arrive = []
    for s in range(2, n // 2 + 1):
        ring.step(s, 0)
        ring.step(s, 1)
        ring.step(s - 1, 2)
        if s == 2:
            result_chip.wait_recv()
            arrive.append(over_mp(9, all_result.at[far], all_result.at[far], core))
        if s == n // 2 - 1:
            hidden_chip.wait_recv()
            arrive.append(over_mp(10, all_hidden.at[far], all_hidden.at[far], core))
    ring.step(n // 2, 2)
    for copy in [result_core, hidden_core] + arrive:
        copy.wait_recv()
    own_result.wait()
    own_hidden.wait()
    for copy in sent:
        if copy is not gains_two:
            copy.wait_send()
    ring.end()


def last_exchange(grad_a, misc, gains, d_normed, extra, d_mixed, hidden, gain, result, cid):
    n = lax.axis_size("dp")
    rows, model = d_mixed.shape
    dma = pltpu.SemaphoreType.DMA
    every = jax.ShapeDtypeStruct((4, rows, model), BF)
    return pl.pallas_call(
        partial(last_kernel, n),
        out_shape=[jax.ShapeDtypeStruct(a.shape[1:], F32) for a in (grad_a, misc, gains)] + [every, every],
        in_specs=[VM] * 8 + [ANY],
        out_specs=[VM] * 3 + [ANY] * 2,
        scratch_shapes=[
            pltpu.VMEM(gains.shape, F32),
            pltpu.VMEM(gains.shape, F32),
            pltpu.VMEM(gains.shape, F32),
            pltpu.VMEM((2, rows, model), BF),
            pltpu.VMEM((rows, model), BF),
            pltpu.VMEM((rows, model), BF),
        ]
        + RingScatter.scratch(n, [grad_a, misc, gains])
        + [dma((11,)), dma((11,)), dma((2,))],
        compiler_params=pltpu.CompilerParams(
            collective_id=cid, has_side_effects=True, vmem_limit_bytes=56 * 1024 * 1024
        ),
    )(grad_a, misc, gains, d_normed, extra, d_mixed, hidden, gain, result)


def mp_scatter_kernel(x, out, from_core, from_chip, send_sem, recv_sem):
    m = lax.axis_index("mp")
    core, chip = mp_partners(m)
    mine, far = m, (m + 2) % 4
    beside = m + 1 - 2 * (m % 2)
    parts = [(pl.ds(start, size), size) for start, size in chunk_rows(0, out.shape[0])]
    greet([core, chip])
    first, last = [], []
    for slot, block in ((1, (beside + 2) % 4), (0, beside)):
        for i, (part, _) in enumerate(parts):
            copy = remote(
                x.at[block, part], from_core.at[slot, part], send_sem.at[slot, i], recv_sem.at[slot, i], core
            )
            copy.start()
            first.append(copy)
    for i, (part, size) in enumerate(parts):
        first[i].wait_recv()
        held = from_core.at[1, part]
        add_rows(held, [held, x.at[far, part]], size, x.dtype)
        copy = remote(held, from_chip.at[part], send_sem.at[2, i], recv_sem.at[2, i], chip)
        copy.start()
        last.append(copy)
    for i, (part, size) in enumerate(parts):
        first[len(parts) + i].wait_recv()
        last[i].wait_recv()
        add_rows(out.at[part], [x.at[mine, part], from_core.at[0, part], from_chip.at[part]], size, F32)
    for copy in first + last:
        copy.wait_send()


def scatter_mp(x, cid):
    rows, cols = x.shape[1:]
    count = len(chunk_rows(0, rows))
    return pl.pallas_call(
        mp_scatter_kernel,
        out_shape=jax.ShapeDtypeStruct((rows, cols), F32),
        in_specs=[VM],
        out_specs=VM,
        scratch_shapes=[
            pltpu.VMEM((2, rows, cols), x.dtype),
            pltpu.VMEM((rows, cols), x.dtype),
            pltpu.SemaphoreType.DMA((3, count)),
            pltpu.SemaphoreType.DMA((3, count)),
        ],
        compiler_params=pltpu.CompilerParams(
            collective_id=cid, has_side_effects=True, vmem_limit_bytes=32 * 1024 * 1024
        ),
    )(x)


def mp_gather_kernel(k, *refs):
    ins, outs = refs[:k], refs[k : 2 * k]
    local_sem, send_sem, recv_sem = refs[2 * k :]
    m = lax.axis_index("mp")
    core, chip = mp_partners(m)
    far = (m + 2) % 4
    greet([core, chip])
    copies, local, arrive = [], [], []
    for j in range(k):
        to_chip = remote(ins[j], outs[j].at[m], send_sem.at[0, j], recv_sem.at[0, j], chip)
        to_chip.start()
        to_core = remote(ins[j], outs[j].at[m], send_sem.at[1, j], recv_sem.at[1, j], core)
        to_core.start()
        own = pltpu.make_async_copy(ins[j], outs[j].at[m], local_sem.at[j])
        own.start()
        copies += [to_chip, to_core]
        arrive.append(to_chip)
        local.append(own)
    onward = []
    for j in range(k):
        arrive[j].wait_recv()
        copy = remote(outs[j].at[far], outs[j].at[far], send_sem.at[2, j], recv_sem.at[2, j], core)
        copy.start()
        onward.append(copy)
    for j in range(k):
        copies[2 * j + 1].wait_recv()
        onward[j].wait_recv()
        local[j].wait()
    for copy in copies + onward:
        copy.wait_send()


def gather_mp(arrays, cid):
    k = len(arrays)
    return pl.pallas_call(
        partial(mp_gather_kernel, k),
        out_shape=[jax.ShapeDtypeStruct((4,) + a.shape, a.dtype) for a in arrays],
        in_specs=[ANY] * k,
        out_specs=[ANY] * k,
        scratch_shapes=[
            pltpu.SemaphoreType.DMA((k,)),
            pltpu.SemaphoreType.DMA((3, k)),
            pltpu.SemaphoreType.DMA((3, k)),
        ],
        compiler_params=pltpu.CompilerParams(collective_id=cid, has_side_effects=True),
    )(*arrays)


class TokenGather:
    def __init__(self, n, both, x, out, sems):
        self.n, self.both, self.x, self.out = n, both, x, out
        self.local, self.ring_s, self.ring_r, self.core_s, self.core_r, self.chip_s, self.chip_r = sems
        self.d, self.m = lax.axis_index("dp"), lax.axis_index("mp")
        self.far = (self.m + 2) % 4
        self.core, self.chip = mp_partners(self.m)
        self.p, self.nxt, self.prv = ring_neighbours(n)
        self.pieces = [(0,) + c for c in chunk_rows(0, x.shape[0])] + [(1,) + c for c in chunk_rows(0, both)]
        self.sent, self.pending = [], {}
        self.ring, self.chips = {}, {}

    @staticmethod
    def scratch(n, rows, both):
        dma = pltpu.SemaphoreType.DMA
        own, far = len(chunk_rows(0, rows)), len(chunk_rows(0, both))
        steps = n // 2
        return [
            dma((3,)),
            dma((steps, own + far, 2)),
            dma((steps, own + far, 2)),
            dma((steps + 1, 2 * own + far, 2)),
            dma((steps + 1, 2 * own + far, 2)),
            dma((steps + 1, own, 2)),
            dma((steps + 1, own, 2)),
        ]

    def send(self, source, place, s_sem, r_sem, target):
        copy = remote(source, place, s_sem, r_sem, target)
        copy.start()
        self.sent.append(copy)
        return copy

    def begin(self):
        own = self.out.at[self.d, self.m]
        self.load = pltpu.make_async_copy(self.x, own, self.local.at[0])
        self.load.start()
        self.first = None
        if self.both:
            part = pl.ds(0, self.both)
            self.first = remote(
                self.x.at[part], own.at[part], self.local.at[1], self.local.at[2], self.chip
            )
            self.first.start()
            self.sent.append(self.first)

    def step(self, s, between=None):
        n, p = self.n, self.p
        for k, (is_far, start, rows) in enumerate(self.pieces):
            if k > 0 and between is not None:
                between()
            for way in range(2):
                origin = ring_device(n, (p + n - s) % n if way == 0 else (p + s) % n)
                place = self.far if is_far else self.m
                region = self.out.at[origin, place, pl.ds(start, rows)]
                source = region if s > 0 or is_far else self.x.at[pl.ds(start, rows)]
                if (s - 1, k, way) in self.ring:
                    self.ring[s - 1, k, way].wait_recv()
                elif s > 0:
                    continue
                elif is_far and self.first is not None:
                    self.first.wait_recv()
                    self.first = None
                if s + 1 < n // 2 or (s + 1 == n // 2 and k % 2 == way):
                    self.ring[s, k, way] = self.send(
                        source,
                        region,
                        self.ring_s.at[s, k, way],
                        self.ring_r.at[s, k, way],
                        self.nxt if way == 0 else self.prv,
                    )
                if s == 0 and way == 1:
                    continue
                self.pending.setdefault(s, []).append(
                    self.send(source, region, self.core_s.at[s, k, way], self.core_r.at[s, k, way], self.core)
                )
                if not is_far and start >= self.both:
                    self.chips[s, k, way] = (
                        self.send(
                            source, region, self.chip_s.at[s, k, way], self.chip_r.at[s, k, way], self.chip
                        ),
                        self.out.at[origin, self.far, pl.ds(start, rows)],
                    )

    def pass_on(self, s):
        total = len(self.pieces)
        for k in range(total):
            for way in range(2):
                if (s, k, way) in self.chips:
                    copy, region = self.chips[s, k, way]
                    copy.wait_recv()
                    at = (s, total + k, way)
                    self.pending.setdefault(s, []).append(
                        self.send(region, region, self.core_s.at[at], self.core_r.at[at], self.core)
                    )

    def blocks(self, s):
        n, p = self.n, self.p
        if s in (0, n // 2):
            return [ring_device(n, (p + s) % n)]
        return [ring_device(n, (p + n - s) % n), ring_device(n, (p + s) % n)]

    def complete(self, s):
        if s == 0:
            self.load.wait()
        for copy in self.pending.pop(s):
            copy.wait_recv()

    def end(self):
        for s in sorted(self.pending):
            self.complete(s)
        for copy in self.sent:
            copy.wait_send()


class SlotWork:
    def __init__(self, own, small, router, position, gates, slot_gates, earlier):
        self.own, self.small, self.router = own, small, router
        self.position, self.gates, self.slot_gates, self.earlier = position, gates, slot_gates, earlier
        self.first = (lax.axis_index("dp") * own).astype(F32)
        length = earlier.shape[0]
        row = lax.broadcasted_iota(jnp.int32, (length, length), 0)
        col = lax.broadcasted_iota(jnp.int32, (length, length), 1)
        earlier[...] = jnp.where(row < col, 1.0, 0.0).astype(BF)

    def named(self, block, first, count):
        length = self.earlier.shape[0]
        routes = self.small[block, :, 0:length].astype(F32)
        expert = lax.broadcasted_iota(jnp.int32, (count, length), 0).astype(F32) + first
        found = routes[1:2, :] == expert
        for k in range(2, TOPK + 1):
            found = found | (routes[k : k + 1, :] == expert)
        return found

    def place(self, block):
        named = self.named(block, self.first, 8)
        count = dot(jnp.where(named, 1.0, 0.0).astype(BF), self.earlier[...])
        self.position[block] = jnp.where(named, count, -1.0)[0 : self.own, :]

    def pick(self, block):
        return pick_matrix(self.position[block], self.own)

    def gate(self, block, rows, pick):
        own = self.own
        logits = dot(rows, self.router[...])
        named = jnp.where(self.named(block, 0.0, LANES), 1.0, 0.0).T > 0.5
        top = jnp.max(jnp.where(named, logits, MASKED), axis=1, keepdims=True)
        powers = jnp.where(named, jnp.exp(jnp.minimum(logits - top, 0.0)), 0.0)
        gate = powers / jnp.sum(powers, axis=1, keepdims=True)
        self.gates[block] = gate
        of_slot = dot(pick, jnp.concatenate(two_parts(gate), axis=1))
        of_slot = of_slot[:, 0:LANES] + of_slot[:, LANES : 2 * LANES]
        row = lax.broadcasted_iota(jnp.int32, of_slot.shape, 0)
        col = lax.broadcasted_iota(jnp.int32, of_slot.shape, 1)
        mine = col - lax.axis_index("dp") * own == row // CAP
        of_slot = jnp.sum(jnp.where(mine, of_slot, 0.0), axis=1, keepdims=True)
        of_slot = jnp.broadcast_to(of_slot, (own * CAP, LANES)).reshape(own, CAP, LANES)
        for e in range(own):
            self.slot_gates[e, block] = of_slot[e]


class RowStream:
    def __init__(self, source, target, in_buf, out_buf, load_sem, store_sem):
        self.source, self.target, self.in_buf, self.out_buf = source, target, in_buf, out_buf
        self.load_sem, self.store_sem = load_sem, store_sem
        self.loads, self.stores = [], []

    def load(self, block):
        at = len(self.loads) % 2
        copy = pltpu.make_async_copy(self.source.at[block], self.in_buf.at[at], self.load_sem.at[at])
        copy.start()
        self.loads.append(copy)

    def take(self, i, wait=True):
        if wait:
            self.loads[i].wait()
        held = self.in_buf[i % 2]
        return held.reshape(-1, held.shape[-1])

    def give(self, i, block, picked):
        if i > 1:
            self.stores[i - 2].wait()
        self.out_buf[i % 2] = picked.astype(BF).reshape(self.out_buf.shape[1:])
        copy = pltpu.make_async_copy(
            self.out_buf.at[i % 2], self.target.at[:, block], self.store_sem.at[i % 2]
        )
        copy.start()
        self.stores.append(copy)

    def end(self):
        for copy in self.stores[-2:]:
            copy.wait()


def token_gather_kernel(
    n,
    both,
    own,
    x,
    y,
    small,
    router,
    out,
    y_rows,
    x_rows,
    position,
    gates,
    slot_gates,
    earlier,
    y_in,
    y_out,
    x_in,
    x_out,
    stream_sem,
    *sems,
):
    gather = TokenGather(n, both, x, out, sems)
    work = SlotWork(own, small, router, position, gates, slot_gates, earlier)
    y_stream = RowStream(y, y_rows, y_in, y_out, stream_sem.at[0], stream_sem.at[1])
    x_stream = RowStream(out, x_rows, x_in, x_out, stream_sem.at[2], stream_sem.at[3])
    half = n // 2
    y_stream.load(0)
    greet([gather.core, gather.chip, gather.nxt, gather.prv])
    gather.begin()

    tasks = []

    def pick_y(b):
        held = {}

        def start():
            if b + 1 < n:
                y_stream.load(b + 1)
            held["pick"] = work.pick(b)

        def finish():
            y_stream.give(b, b, dot(held["pick"], y_stream.take(b)))

        return [start, finish]

    def pick_x(s):
        blocks = gather.blocks(s)
        held = {}

        def start():
            gather.complete(s)
            held["at"] = len(x_stream.loads)
            for block in blocks:
                x_stream.load(block)

        found = [start]
        for i, block in enumerate(blocks):

            def pick(i=i, block=block):
                held[i] = work.pick(block)
                x_stream.give(held["at"] + i, block, dot(held[i], x_stream.take(held["at"] + i)))

            def gate(i=i, block=block):
                work.gate(block, x_stream.take(held["at"] + i, False), held[i])

            found += [pick, gate]
        return found

    def between():
        for _ in range(2):
            if tasks:
                tasks.pop(0)()

    gather.step(0)
    for b in range(n):
        work.place(b)
        tasks += pick_y(b)
    for _ in range(4):
        tasks.pop(0)()
    for s in range(1, half + 1):
        gather.step(s, between)
        gather.pass_on(s - 1)
        tasks += pick_x(s - 1)
    gather.pass_on(half)
    tasks += pick_x(half)
    while tasks:
        tasks.pop(0)()
    gather.end()
    y_stream.end()
    x_stream.end()


def gather_tokens(x, y, small, router, own, cid):
    n, tokens, model = y.shape
    both = x.shape[0] // 2
    quarter = x.shape[0]
    picked = jax.ShapeDtypeStruct((own, n, CAP, model), BF)
    return pl.pallas_call(
        partial(token_gather_kernel, n, both, own),
        out_shape=[
            jax.ShapeDtypeStruct((n, 4) + x.shape, x.dtype),
            picked,
            picked,
            jax.ShapeDtypeStruct((n, own, tokens), F32),
            jax.ShapeDtypeStruct((n, tokens, LANES), F32),
            jax.ShapeDtypeStruct((own, n, CAP, LANES), F32),
        ],
        in_specs=[ANY, ANY, VM, VM],
        out_specs=[ANY, ANY, ANY, VM, VM, VM],
        scratch_shapes=[
            pltpu.VMEM((tokens, tokens), BF),
            pltpu.VMEM((2, tokens, model), BF),
            pltpu.VMEM((2, own, CAP, model), BF),
            pltpu.VMEM((2, 4, quarter, model), BF),
            pltpu.VMEM((2, own, CAP, model), BF),
            pltpu.SemaphoreType.DMA((4, 2)),
        ]
        + TokenGather.scratch(n, quarter, both),
        compiler_params=pltpu.CompilerParams(
            collective_id=cid, has_side_effects=True, vmem_limit_bytes=56 * 1024 * 1024
        ),
    )(x, y, small, router)


def first_kernel(n, k, *refs):
    ins, x = refs[:k], refs[k]
    outs, x_out = refs[k + 1 : 2 * k + 1], refs[2 * k + 1]
    ring = RingGather(n, ins, outs, refs[2 * k + 2 : 2 * k + 5])
    gather = TokenGather(n, 0, x, x_out, refs[2 * k + 5 :])
    greet([gather.core, gather.chip, gather.nxt, gather.prv])
    ring.begin()
    gather.begin()
    for s in range(n // 2 + 1):
        gather.step(s)
        ring.step(s)
        if s > 0:
            gather.pass_on(s - 1)
    gather.pass_on(n // 2)
    gather.end()
    ring.end()


def first_gather(arrays, x, cid):
    n, k = lax.axis_size("dp"), len(arrays)
    return pl.pallas_call(
        partial(first_kernel, n, k),
        out_shape=[jax.ShapeDtypeStruct((n,) + a.shape, a.dtype) for a in arrays]
        + [jax.ShapeDtypeStruct((n, 4) + x.shape, x.dtype)],
        in_specs=[ANY] * (k + 1),
        out_specs=[ANY] * (k + 1),
        scratch_shapes=RingGather.scratch(n, arrays) + TokenGather.scratch(n, x.shape[0], 0),
        compiler_params=pltpu.CompilerParams(collective_id=cid, has_side_effects=True),
    )(*arrays, x)


def token_scatter_kernel(
    n,
    x,
    out,
    from_core,
    slots,
    loads,
    far_loads,
    from_chip,
    to_chip,
    first,
    done,
    last_buf,
    load_sem,
    far_sem,
    core_send,
    core_recv,
    chip_send,
    chip_recv,
    send_sem,
    recv_sem,
    last_send,
    last_recv,
):
    m = lax.axis_index("mp")
    c, y = m % 2, m // 2
    core, chip = mp_partners(m)
    far = (m + 2) % 4
    beside = m + 1 - 2 * c
    p, nxt, prv = ring_neighbours(n)
    rows = out.shape[0]
    half, steps = rows // 2, n // 2
    greet([core, chip, nxt, prv])

    def block_of(i):
        s = (i + 1) // 2
        return ring_device(n, (p + steps - s) % n if i % 2 or i == 0 else (p + n - steps + s) % n)

    over, sent, loading, chips = {}, [], {}, {}
    loaded, summed = set(), set()
    upper, lower, whole = pl.ds(half, half), pl.ds(0, half), pl.ds(0, rows)

    def core_sends(i):
        if i >= n:
            return
        block = block_of(i)
        moves = [((beside + 2) % 4, 1 - y, upper), (beside, y, whole), ((beside + 2) % 4, 1 - y, lower)]
        for k, (theirs, piece, part) in enumerate(moves):
            copy = remote(
                x.at[block, theirs, part],
                from_core.at[block, piece, part],
                core_send.at[i, k],
                core_recv.at[i, k],
                core,
            )
            copy.start()
            over[i, k] = copy
            sent.append(copy)

    def start_pair(name, source, other, target, sems):
        loading[name] = []
        for k, ref in enumerate((source, other)):
            copy = pltpu.make_async_copy(ref, target.at[k], sems.at[k])
            copy.start()
            loading[name].append(copy)

    def load(i):
        if i >= n:
            return
        block = block_of(i)
        at = i % 4
        over[i, 1].wait_recv()
        start_pair(
            (i, 0), x.at[block, m], from_core.at[block, y], loads.at[at, :, whole], load_sem.at[at, 0]
        )
        over[i, 2].wait_recv()
        start_pair(
            (i, 1),
            x.at[block, far, lower],
            from_core.at[block, 1 - y, lower],
            loads.at[at, :, pl.ds(rows, half)],
            load_sem.at[at, 1],
        )

    def load_far(i):
        if i >= n:
            return
        block = block_of(i)
        over[i, 0].wait_recv()
        start_pair(
            (i, 2),
            x.at[block, far, upper],
            from_core.at[block, 1 - y, upper],
            far_loads.at[i % 2],
            far_sem.at[i % 2],
        )

    def to_other_chip(i):
        if i >= n:
            return
        for copy in loading[i, 2]:
            copy.wait()
        if i > 1:
            chips[i - 2].wait_send()
        add_rows(to_chip.at[i % 2], [far_loads.at[i % 2, 0], far_loads.at[i % 2, 1]], half, BF)
        copy = remote(to_chip.at[i % 2], from_chip.at[i], chip_send.at[i], chip_recv.at[i], chip)
        copy.start()
        chips[i] = copy

    chunks = chunk_rows(0, rows + half)
    count = len(chunks)
    order = [k for k in range(count) if chunks[k][0] >= rows]
    order += [k for k in range(count) if chunks[k][0] < rows]

    def pieces_of(i, k):
        start, size = chunks[k]
        area = pl.ds(start, size)
        if i not in loaded:
            loaded.add(i)
            for copy in loading[i, 0] + loading[i, 1]:
                copy.wait()
        found = [loads.at[i % 4, 0, area], loads.at[i % 4, 1, area]]
        if half <= start < rows:
            if i not in summed:
                summed.add(i)
                chips[i].wait_recv()
            found.append(from_chip.at[i, pl.ds(start - half, size)])
        return found

    for i in range(3):
        core_sends(i)
    load_far(0)
    load(0)
    load_far(1)
    to_other_chip(0)
    load_far(2)
    to_other_chip(1)
    core_sends(3)
    core_sends(4)
    load(1)
    to_other_chip(2)
    load(2)
    ring = {}
    for s in range(steps):
        for k, way in [(k, way) for k in order for way in range(2) if s > 0 or k % 2 == way]:
            start, size = chunks[k]
            area = pl.ds(start, size)
            if s == 0:
                target, pieces = first.at[area], pieces_of(0, k)
            else:
                target, pieces = slots.at[s - 1, way, area], pieces_of(2 * s - 1 + way, k)
                if (s - 1, k, way) in ring:
                    ring[s - 1, k, way].wait_recv()
                    pieces.append(target)
            add_rows(target, pieces, size, BF)
            copy = remote(
                target,
                slots.at[s, way, area],
                send_sem.at[s, k, way],
                recv_sem.at[s, k, way],
                nxt if way == 0 else prv,
            )
            copy.start()
            ring[s, k, way] = copy
        for i in (2 * s + 3, 2 * s + 4):
            load_far(i)
            core_sends(i + 2)
            to_other_chip(i)
            load(i)
    last = []
    for k in order:
        start, size = chunks[k]
        area = pl.ds(start, size)
        pieces = pieces_of(n - 1, k)
        for way in range(2):
            ring[steps - 1, k, way].wait_recv()
            pieces.append(slots.at[steps - 1, way, area])
        if start < rows:
            add_rows(out.at[area], pieces, size, F32)
            continue
        at = pl.ds(start - rows, size)
        add_rows(done.at[at], pieces, size, BF)
        copy = remote(done.at[at], last_buf.at[at], last_send.at[k], last_recv.at[k], chip)
        copy.start()
        last.append(copy)
    for copy in last:
        copy.wait_recv()
    add_rows(out.at[lower], [out.at[lower], last_buf], half, F32)
    for copy in sent + list(ring.values()) + last + [chips[n - 2], chips[n - 1]]:
        copy.wait_send()


def scatter_tokens(x, cid):
    n, _, rows, cols = x.shape
    half, steps = rows // 2, n // 2
    count = len(chunk_rows(0, rows + half))
    dma = pltpu.SemaphoreType.DMA
    out, _ = pl.pallas_call(
        partial(token_scatter_kernel, n),
        out_shape=[
            jax.ShapeDtypeStruct((rows, cols), F32),
            jax.ShapeDtypeStruct((n, 2, rows, cols), BF),
        ],
        in_specs=[ANY],
        out_specs=[VM, ANY],
        scratch_shapes=[
            pltpu.VMEM((steps, 2, rows + half, cols), BF),
            pltpu.VMEM((4, 2, rows + half, cols), BF),
            pltpu.VMEM((2, 2, half, cols), BF),
            pltpu.VMEM((n, half, cols), BF),
            pltpu.VMEM((2, half, cols), BF),
            pltpu.VMEM((rows + half, cols), BF),
            pltpu.VMEM((half, cols), BF),
            pltpu.VMEM((half, cols), BF),
            dma((4, 2, 2)),
            dma((2, 2)),
            dma((n, 3)),
            dma((n, 3)),
            dma((n,)),
            dma((n,)),
            dma((steps, count, 2)),
            dma((steps, count, 2)),
            dma((count,)),
            dma((count,)),
        ],
        compiler_params=pltpu.CompilerParams(
            collective_id=cid, has_side_effects=True, vmem_limit_bytes=56 * 1024 * 1024
        ),
    )(x)
    return out


def edge_kernel(n, part, slope, rim, total, ahead, mine, from_core, from_chip, edge, send_sem, recv_sem):
    d, m = lax.axis_index("dp"), lax.axis_index("mp")
    core, chip = mp_partners(m)
    before, after = {"dp": (d + n - 1) % n}, {"dp": (d + 1) % n}
    rows, cols = part.shape
    edge_rows, rim_cols = rim.shape
    greet([core, chip, before, after])

    def add(dst, pieces, dtype):
        add_rows(dst, pieces, rows, dtype)

    one = remote(part, from_core, send_sem.at[0], recv_sem.at[0], core)
    one.start()
    one.wait()
    add(mine, [part, from_core], BF)
    two = remote(mine, from_chip, send_sem.at[1], recv_sem.at[1], chip)
    two.start()
    two.wait_recv()
    add(total, [mine, from_chip], F32)
    edge[:, 0:rim_cols] = rim[...]
    edge[:, rim_cols : rim_cols + cols] = total[0:edge_rows, :] * slope[...]
    three = remote(edge, ahead, send_sem.at[2], recv_sem.at[2], before)

    @pl.when(d > 0)
    def _():
        three.start()

    @pl.when(d == n - 1)
    def _():
        ahead[...] = jnp.zeros_like(ahead)

    @pl.when(d < n - 1)
    def _():
        three.wait_recv()

    @pl.when(d > 0)
    def _():
        three.wait_send()

    two.wait_send()


def sum_and_edge(part, slope, rim, cid):
    rows, cols = part.shape
    edge_shape = (rim.shape[0], rim.shape[1] + cols)
    return pl.pallas_call(
        partial(edge_kernel, lax.axis_size("dp")),
        out_shape=[
            jax.ShapeDtypeStruct(part.shape, F32),
            jax.ShapeDtypeStruct(edge_shape, F32),
        ],
        in_specs=[VM] * 3,
        out_specs=[VM] * 2,
        scratch_shapes=[
            pltpu.VMEM((rows, cols), BF),
            pltpu.VMEM((rows, cols), F32),
            pltpu.VMEM((rows, cols), BF),
            pltpu.VMEM(edge_shape, F32),
            pltpu.SemaphoreType.DMA((3,)),
            pltpu.SemaphoreType.DMA((3,)),
        ],
        compiler_params=pltpu.CompilerParams(
            collective_id=cid, has_side_effects=True, vmem_limit_bytes=32 * 1024 * 1024
        ),
    )(part, slope, rim)


def head_pair(pair, first, second):
    lane = lax.broadcasted_iota(jnp.int32, first.shape, 1)
    return jnp.where(lane < LANES // 2, first, second)


def visible_pairs(seg_col, seg_row):
    length = seg_col.shape[0]
    row = lax.broadcasted_iota(jnp.int32, (length, length), 0)
    col = lax.broadcasted_iota(jnp.int32, (length, length), 1)
    return (row >= col) & (seg_col == seg_row)


def state_decay(entry, expand):
    last = entry[entry.shape[0] - 1 :, :]
    spread = jnp.broadcast_to(last, (LANES, LANES)).T
    return dot(expand, spread, ((0,), (0,)), HIGH)


def recur_kernel(
    pairs,
    values,
    write,
    read,
    cumul,
    cumul_t,
    step_t,
    entry,
    tail,
    seg_col,
    seg_row,
    expand,
    skip,
    start,
    out,
    kept,
    state,
):
    @pl.when(pl.program_id(0) == 0)
    def _():
        state[...] = start[...]

    held = state[...]
    kept[0] = held
    v, b, c = values[...], write[...], read[...]
    scores = dot(c, b, ((1,), (1,)), HIGH)
    visible = visible_pairs(seg_col[...], seg_row[...])
    entry_full = dot(entry[...], expand[...], precision=HIGH)
    tail_full = dot(tail[...], expand[...], precision=HIGH)
    carried = entry_full * dot(c, held, ((1,), (1,)), HIGH) + skip[...] * v
    cum, cum_t, st_t = cumul[...], cumul_t[...], step_t[...]
    for pair in range(pairs):
        cols = slice(pair * LANES, (pair + 1) * LANES)
        v2 = v[:, cols]
        found = []
        for h in (2 * pair, 2 * pair + 1):
            spread = jnp.where(visible, cum[:, h : h + 1] - cum_t[h : h + 1, :], MASKED)
            mixing = jnp.exp(spread) * (scores * st_t[h : h + 1, :])
            found.append(dot_three(mixing, v2, (1, 0)))
        out[:, cols] = head_pair(pair, found[0], found[1]) + carried[:, cols]
    state[...] = state_decay(entry[...], expand[...]) * held + dot(v * tail_full, b, ((0,), (0,)), HIGH)


def recur_specs(width, lengths):
    def rows(cols):
        return pl.BlockSpec((BLK, cols), lambda i: (lengths(i), 0))

    def flat(count):
        return pl.BlockSpec((count, BLK), lambda i: (0, lengths(i)))

    def whole(shape):
        return pl.BlockSpec(shape, lambda i: (0,) * len(shape))

    return rows, flat, whole


def recur_forward(v, b, c, cumul, cumul_t, step_t, entry, tail, seg_col, seg_row, expand, skip, start):
    total, width = v.shape
    blocks = total // BLK
    rows, flat, whole = recur_specs(width, lambda i: i)
    return pl.pallas_call(
        partial(recur_kernel, width // LANES),
        grid=(blocks,),
        out_shape=[
            jax.ShapeDtypeStruct((total, width), F32),
            jax.ShapeDtypeStruct((blocks, width, LANES), F32),
        ],
        in_specs=[
            rows(width),
            rows(LANES),
            rows(LANES),
            rows(LANES),
            flat(16),
            flat(16),
            rows(LANES),
            rows(LANES),
            rows(1),
            flat(1),
            whole((LANES, width)),
            whole((1, width)),
            whole((width, LANES)),
        ],
        out_specs=[
            rows(width),
            pl.BlockSpec((1, width, LANES), lambda i: (i, 0, 0)),
        ],
        scratch_shapes=[pltpu.VMEM((width, LANES), F32)],
        compiler_params=pltpu.CompilerParams(vmem_limit_bytes=48 * 1024 * 1024),
    )(v, b, c, cumul, cumul_t, step_t, entry, tail, seg_col, seg_row, expand, skip, start)


def adjoint_kernel(
    pairs,
    values,
    write,
    read,
    cumul,
    cumul_t,
    step_t,
    step,
    entry,
    tail_bare,
    seg_col,
    seg_row,
    expand,
    skip,
    kept,
    d_out,
    start,
    d_values,
    d_write,
    d_read,
    d_step,
    d_rate_step,
    d_skip,
    state,
    columns,
):
    @pl.when(pl.program_id(0) == 0)
    def _():
        state[...] = start[...]
        d_skip[...] = jnp.zeros_like(d_skip)
        columns[...] = jnp.zeros_like(columns)

    length = values.shape[0]
    lam, held = state[...], kept[0]
    v, b, c, dy = values[...], write[...], read[...], d_out[...]
    ex = expand[...]
    st = step[...]
    scores = dot(c, b, ((1,), (1,)), HIGH)
    visible = visible_pairs(seg_col[...], seg_row[...])
    entry_full = dot(entry[...], ex, precision=HIGH)
    tail = tail_bare[...] * st
    tail_full = dot(tail, ex, precision=HIGH)
    c_state = dot(c, held, ((1,), (1,)), HIGH)
    b_lam = dot(b, lam, ((1,), (1,)), HIGH)
    dy_in = dy * entry_full
    v_out = v * tail_full
    dc = dot(dy_in, held, precision=HIGH)
    db = dot(v_out, lam, precision=HIGH)
    reach = dot(dy_in * c_state, ex, ((1,), (1,)), HIGH)
    leave = dot(v * b_lam, ex, ((1,), (1,)), HIGH)
    d_skip[...] += jnp.sum(dy * v, axis=0, keepdims=True)
    dv_far = tail_full * b_lam + skip[...] * dy
    cum, cum_t, st_t = cumul[...], cumul_t[...], step_t[...]
    lane = lax.broadcasted_iota(jnp.int32, (length, LANES), 1)
    d_scores = jnp.zeros((length, length), F32)
    row_sums = jnp.zeros((length, LANES), F32)
    for pair in range(pairs):
        cols = slice(pair * LANES, (pair + 1) * LANES)
        v2, dy2 = v[:, cols], dy[:, cols]
        found = []
        for j in range(2):
            h = 2 * pair + j
            own = (lane < LANES // 2) if j == 0 else (lane >= LANES // 2)
            d_mix = dot_three(jnp.where(own, dy2, 0.0), v2, (1, 1))
            spread = jnp.where(visible, cum[:, h : h + 1] - cum_t[h : h + 1, :], MASKED)
            decay = jnp.exp(spread)
            decay_step = decay * st_t[h : h + 1, :]
            weighted = d_mix * scores * decay
            d_scores = d_scores + d_mix * decay_step
            columns[h : h + 1, :] = jnp.sum(weighted, axis=0, keepdims=True)
            per_row = jnp.sum(weighted * st_t[h : h + 1, :], axis=1, keepdims=True)
            row_sums = jnp.where(lane == h, per_row, row_sums)
            found.append(dot(scores * decay_step, dy2, ((0,), (0,))))
        d_values[:, cols] = head_pair(pair, found[0], found[1]) + dv_far[:, cols]
    d_read[...] = dc + dot(d_scores, b, precision=HIGH)
    d_write[...] = db + dot(d_scores, c, ((0,), (0,)), HIGH)
    col_sums = columns[...].T
    leave_step = tail * leave
    d_step[...] = col_sums + tail_bare[...] * leave
    d_cum = row_sums - st * col_sums + reach - leave_step
    row = lax.broadcasted_iota(jnp.int32, (length, length), 0)
    col = lax.broadcasted_iota(jnp.int32, (length, length), 1)
    upper = (col >= row).astype(F32)
    met = jnp.sum(dot(lam * held, ex, ((0,), (1,)), HIGH), axis=0, keepdims=True)
    at_end = jnp.sum(leave_step, axis=0, keepdims=True) + entry[length - 1 :, :] * met
    d_rate_step[...] = dot(upper, d_cum, precision=HIGH) + at_end
    state[...] = state_decay(entry[...], ex) * lam + dot(dy_in, c, ((0,), (0,)), HIGH)


def recur_backward(
    v, b, c, cumul, cumul_t, step_t, step, entry, tail_bare, seg_col, seg_row, expand, skip, kept, dy, start
):
    total, width = v.shape
    blocks = total // BLK
    rows, flat, whole = recur_specs(width, lambda i: blocks - 1 - i)
    return pl.pallas_call(
        partial(adjoint_kernel, width // LANES),
        grid=(blocks,),
        out_shape=[
            jax.ShapeDtypeStruct((total, width), F32),
            jax.ShapeDtypeStruct((total, LANES), F32),
            jax.ShapeDtypeStruct((total, LANES), F32),
            jax.ShapeDtypeStruct((total, LANES), F32),
            jax.ShapeDtypeStruct((total, LANES), F32),
            jax.ShapeDtypeStruct((1, width), F32),
        ],
        in_specs=[
            rows(width),
            rows(LANES),
            rows(LANES),
            rows(LANES),
            flat(16),
            flat(16),
            rows(LANES),
            rows(LANES),
            rows(LANES),
            rows(1),
            flat(1),
            whole((LANES, width)),
            whole((1, width)),
            pl.BlockSpec((1, width, LANES), lambda i: (blocks - 1 - i, 0, 0)),
            rows(width),
            whole((width, LANES)),
        ],
        out_specs=[
            rows(width),
            rows(LANES),
            rows(LANES),
            rows(LANES),
            rows(LANES),
            whole((1, width)),
        ],
        scratch_shapes=[pltpu.VMEM((width, LANES), F32), pltpu.VMEM((LANES, LANES), F32)],
        compiler_params=pltpu.CompilerParams(vmem_limit_bytes=48 * 1024 * 1024),
    )(v, b, c, cumul, cumul_t, step_t, step, entry, tail_bare, seg_col, seg_row, expand, skip, kept, dy, start)


def state_scan_kernel(
    n,
    reverse,
    mine,
    decay,
    expand,
    out,
    first,
    second,
    got_first,
    got_second,
    half,
    got_half,
    send_sem,
    recv_sem,
):
    d = lax.axis_index("dp")
    q = n - 1 - d if reverse else d
    zq, xq = q // 2, q % 2
    depth = n // 2
    rows = mine.shape[0] // 2
    xf = xq.astype(F32)
    sent_type = first.dtype

    def device(logical):
        return {"dp": n - 1 - logical if reverse else logical}

    beside = device(2 * zq + 1 - xq)
    others = [device(2 * ((zq + k) % depth) + xq) for k in range(1, depth)]
    own_rows = pl.ds(pl.multiple_of(rows * xq, 16), rows)
    other_rows = pl.ds(pl.multiple_of(rows * (1 - xq), 16), rows)
    own_lanes = pl.ds(pl.multiple_of(rows * xq, LANES), rows)
    tail = pl.ds(rows, 16)
    body = pl.ds(0, rows)
    row = lax.broadcasted_iota(jnp.int32, (16, LANES), 0)

    def spread(values):
        square = jnp.broadcast_to(values, (LANES, LANES)).T
        return dot(expand[:, own_lanes], square, ((0,), (0,)), HIGH)

    def two_terms(values):
        high = values.astype(sent_type).astype(F32)
        wide = jnp.where(row == 0, high, jnp.where(row == 1, values - high, 0.0))
        return wide.astype(sent_type)

    def one_term(block):
        return block[0:1, :].astype(F32) + block[1:2, :].astype(F32)

    for k in range(1, depth):

        @pl.when(zq < k)
        def _():
            got_second[k - 1] = jnp.zeros(got_second.shape[1:], sent_type)

    own_decay = decay[0:1, :]
    first[body, :] = mine[other_rows, :].astype(sent_type)
    first[tail, :] = two_terms(own_decay)
    greet([beside] + others)
    one = remote(first, got_first, send_sem.at[0], recv_sem.at[0], beside)
    one.start()
    one.wait_recv()
    own = mine[own_rows, :]
    got, got_decay = got_first[body, :].astype(F32), one_term(got_first[tail, :])
    early = own * (1.0 - xf) + got * xf
    early_decay = own_decay * (1.0 - xf) + got_decay * xf
    late = own * xf + got * (1.0 - xf)
    late_decay = own_decay * xf + got_decay * (1.0 - xf)
    second[body, :] = (spread(late_decay) * early + late).astype(sent_type)
    second[tail, :] = two_terms(early_decay * late_decay)
    sent = []
    for k in range(1, depth):
        copy = remote(
            second, got_second.at[k - 1], send_sem.at[k], recv_sem.at[k], device(2 * ((zq + k) % depth) + xq)
        )
        sent.append(copy)

        @pl.when(zq + k < depth)
        def _():
            copy.start()

    early_spread = spread(early_decay)
    total = jnp.zeros((rows, LANES), F32)
    for k in range(depth - 1, 0, -1):

        @pl.when(zq >= k)
        def _():
            sent[k - 1].wait_recv()

        got_k = got_second.at[k - 1]
        total = spread(one_term(got_k[tail, :])) * total + got_k[body, :].astype(F32)
    after = early_spread * total + early
    half[...] = (total * xf + after * (1.0 - xf)).astype(sent_type)
    last = remote(half, got_half, send_sem.at[depth], recv_sem.at[depth], beside)
    last.start()
    out[own_rows, :] = total * (1.0 - xf) + after * xf
    last.wait_recv()
    out[other_rows, :] = got_half[...].astype(F32)
    one.wait_send()
    last.wait_send()
    for k in range(1, depth):

        @pl.when(zq + k < depth)
        def _():
            sent[k - 1].wait_send()


def state_scan(mine, decay, expand, reverse, cid, sent_type):
    n = lax.axis_size("dp")
    half = mine.shape[0] // 2
    depth = n // 2
    message = (half + 16, LANES)
    return pl.pallas_call(
        partial(state_scan_kernel, n, reverse),
        out_shape=jax.ShapeDtypeStruct(mine.shape, F32),
        in_specs=[VM] * 3,
        out_specs=VM,
        scratch_shapes=[
            pltpu.VMEM(message, sent_type),
            pltpu.VMEM(message, sent_type),
            pltpu.VMEM(message, sent_type),
            pltpu.VMEM((depth - 1,) + message, sent_type),
            pltpu.VMEM((half, LANES), sent_type),
            pltpu.VMEM((half, LANES), sent_type),
            pltpu.SemaphoreType.DMA((depth + 1,)),
            pltpu.SemaphoreType.DMA((depth + 1,)),
        ],
        compiler_params=pltpu.CompilerParams(
            collective_id=cid, has_side_effects=True, vmem_limit_bytes=32 * 1024 * 1024
        ),
    )(mine, decay, expand)


def pick_matrix(position, own):
    length = position.shape[1]
    slot = lax.broadcasted_iota(jnp.int32, (CAP, length), 0).astype(F32)
    parts = [
        jnp.where(position[e : e + 1, :] == slot, 1.0, 0.0).astype(BF) for e in range(own)
    ]
    return jnp.concatenate(parts, axis=0)


def slot_spec(own, cols):
    return pl.BlockSpec((own, 1, CAP, cols), lambda s: (0, s, 0, 0))


def token_spec(rows, cols):
    return pl.BlockSpec((1, rows, cols), lambda s: (s, 0, 0))


BIG = pltpu.CompilerParams(vmem_limit_bytes=56 * 1024 * 1024)


def expert_kernel(
    own, rows, cot_rows, gate, w_in, w_out, grad_in, grad_out, d_rows, res, dots, wide, both
):
    e, part = pl.program_id(0), pl.program_id(1)
    model = rows.shape[2]
    units = w_out.shape[1]

    @pl.when(part == 0)
    def _():
        wide[...] = w_in[0].astype(F32)
        both[:, 0:units] = wide[pl.ds(0, model, stride=2), :].astype(BF)
        both[:, units : 2 * units] = wide[pl.ds(1, model, stride=2), :].astype(BF)
        grad_in[...] = jnp.zeros_like(grad_in)
        grad_out[...] = jnp.zeros_like(grad_out)

    x, c, g = rows[0], cot_rows[0], gate[0]
    mid = dot(x, both[...])
    mid_gate, mid_up = mid[:, 0:units], mid[:, units : 2 * units]
    sig = jax.nn.sigmoid(mid_gate)
    mid_silu = mid_gate * sig
    act = (mid_silu * mid_up).astype(BF).astype(F32)
    back = dot(c, w_out[0], ((1,), (1,)))
    dot_sum = jnp.sum(act * back, axis=1, keepdims=True)
    lane = lax.broadcasted_iota(jnp.int32, g.shape, 1)
    dots[0] = jnp.where(lane == lax.axis_index("dp") * own + e, dot_sum, 0.0).astype(BF)
    gated = (act * g).astype(BF)
    d_act = back * g
    d_gate = (d_act * mid_up * (sig * (1.0 + mid_gate * (1.0 - sig)))).astype(BF)
    d_mid = jnp.concatenate([d_gate, (d_act * mid_silu).astype(BF)], axis=1)
    grads = dot(x, d_mid, ((0,), (0,)))
    grad_in[0, pl.ds(0, model, stride=2), :] += grads[:, 0:units]
    grad_in[0, pl.ds(1, model, stride=2), :] += grads[:, units : 2 * units]
    grad_out[0] += dot(gated, c, ((0,), (0,)))
    d_rows[0] = dot(d_mid, both[...], ((1,), (1,))).astype(BF)
    res[0] = dot(gated, w_out[0]).astype(BF)


def run_experts(rows, cot_rows, gate, w_in, w_out):
    own, slots, model = rows.shape
    units = w_out.shape[1]
    part = min(slots, 512)

    def slot(cols):
        return pl.BlockSpec((1, part, cols), lambda e, j: (e, j, 0))

    def weight(a, b):
        return pl.BlockSpec((1, a, b), lambda e, j: (e, 0, 0))

    return pl.pallas_call(
        partial(expert_kernel, own),
        grid=(own, slots // part),
        out_shape=[
            jax.ShapeDtypeStruct((own, 2 * model, units), F32),
            jax.ShapeDtypeStruct((own, units, model), F32),
            jax.ShapeDtypeStruct((own, slots, model), BF),
            jax.ShapeDtypeStruct((own, slots, model), BF),
            jax.ShapeDtypeStruct((own, slots, LANES), BF),
        ],
        in_specs=[slot(model), slot(model), slot(LANES), weight(2 * model, units), weight(units, model)],
        out_specs=[weight(2 * model, units), weight(units, model), slot(model), slot(model), slot(LANES)],
        scratch_shapes=[pltpu.VMEM((2 * model, units), F32), pltpu.VMEM((model, 2 * units), BF)],
        compiler_params=BIG,
    )(rows, cot_rows, gate, w_in, w_out)


def put_kernel(own, k, position, *refs):
    out = refs[-1]
    put = pick_matrix(position[0], own)
    here = jnp.where(pl.program_id(0) == lax.axis_index("dp"), 1.0, 0.0)
    start = 0
    for i in range(k):
        rows, shared = refs[2 * i], refs[2 * i + 1]
        cols = shared.shape[1]
        total = dot(put, rows[...].reshape(own * CAP, cols), ((0,), (0,)))
        out[0, :, start : start + cols] = (total + here * shared[...]).astype(BF)
        start += cols
    if len(refs) > 2 * k + 1:
        extra = refs[2 * k]
        out[0, :, start : start + LANES] = dot(
            put, extra[...].reshape(own * CAP, LANES), ((0,), (0,))
        ).astype(BF)


def put_rows(position, parts, extra=None):
    n, own, tokens = position.shape
    args, specs, cols = [], [], 0
    for rows, shared in parts:
        model = shared.shape[1]
        args += [rows.reshape(own, n, CAP, model), shared]
        specs += [slot_spec(own, model), pl.BlockSpec((tokens, model), lambda s: (0, 0))]
        cols += model
    if extra is not None:
        args.append(extra.reshape(own, n, CAP, LANES))
        specs.append(slot_spec(own, LANES))
        cols += LANES
    return pl.pallas_call(
        partial(put_kernel, own, len(parts)),
        grid=(n,),
        out_shape=jax.ShapeDtypeStruct((n, tokens, cols), BF),
        in_specs=[token_spec(own, tokens)] + specs,
        out_specs=token_spec(tokens, cols),
        compiler_params=BIG,
    )(position, *args)


def grads_kernel(k, *refs):
    lefts, rights, out = refs[:k], refs[k : 2 * k], refs[2 * k]
    start = 0
    for left, right in zip(lefts, rights):
        cols = right.shape[1]
        out[:, start : start + cols] = dot(left[...], right[...], ((0,), (0,))).astype(BF)
        start += cols


def weight_grads(pairs):
    k = len(pairs)
    tokens, model = pairs[0][0].shape
    block = 256
    cols = sum(right.shape[1] for _, right in pairs)
    return pl.pallas_call(
        partial(grads_kernel, k),
        grid=(model // block,),
        out_shape=jax.ShapeDtypeStruct((model, cols), BF),
        in_specs=[pl.BlockSpec((tokens, block), lambda i: (0, i)) for _ in pairs]
        + [pl.BlockSpec(right.shape, lambda i: (0, 0)) for _, right in pairs],
        out_specs=pl.BlockSpec((block, cols), lambda i: (i, 0)),
        compiler_params=BIG,
    )(*[left for left, _ in pairs], *[right for _, right in pairs])


def combine_states(states, decays, expand, reverse):
    n = states.shape[0]
    place = lax.axis_index("dp")
    wide = dot(decays, expand, precision=HIGH)
    state = jnp.zeros(states.shape[1:], F32)
    for j in range(n):
        source = n - 1 - j if reverse else j
        use = source > place if reverse else source < place
        fresh = wide[source][:, None] * state + states[source]
        state = jnp.where(use, fresh, state)
    return state


def incoming_state(mine, decay, expand, reverse, cid):
    if lax.axis_size("dp") == 8:
        return state_scan(
            mine, jnp.broadcast_to(decay, (8, LANES)), expand, reverse, cid, BF if reverse else F32
        )
    rows = jnp.pad(decay, ((0, 31), (0, 0)))
    (gathered,) = gather_dp([jnp.concatenate([mine, rows], axis=0)], cid)
    width = mine.shape[0]
    return combine_states(gathered[:, :width], gathered[:, width], expand, reverse)


def per_device(
    hidden,
    segment_ids,
    routes,
    norm_gain,
    mixer_in,
    state_in,
    step_in,
    conv_value,
    conv_value_bias,
    conv_state,
    conv_state_bias,
    head_params,
    gated_gain,
    mixer_out,
    ffn_gain,
    router,
    shared_in,
    shared_out,
    expert_in,
    expert_out,
    cotangent,
):
    n = lax.axis_size("dp")
    place, mp_place = lax.axis_index("dp"), lax.axis_index("mp")
    tokens, model = hidden.shape
    shard = model // n
    inner = mixer_in.shape[2]
    state_cols = state_in.shape[1]
    taps = conv_value.shape[0]
    heads = head_params.shape[1]
    width = inner // heads
    own_experts = expert_in.shape[0]
    hidden_units = shared_out.shape[0]
    quarter = tokens // 4

    misc_parts = [
        conv_value.reshape(-1),
        conv_value_bias.reshape(-1),
        gated_gain.reshape(-1),
        conv_state.reshape(-1),
        conv_state_bias,
        norm_gain,
        ffn_gain,
    ]
    misc = jnp.concatenate(misc_parts)
    small = jnp.concatenate(
        [
            jnp.pad(misc, (0, model - misc.shape[0]))[None],
            jnp.pad(routes.T.astype(BF), ((0, 0), (0, model - tokens))),
            hidden[tokens - 15 + TOPK :],
        ],
        axis=0,
    )
    pack_a = jnp.concatenate(
        [
            mixer_in.reshape(shard, 2 * inner),
            state_in,
            jnp.pad(step_in, ((0, 0), (0, LANES - heads))),
        ],
        axis=1,
    )
    pack_b = jnp.concatenate(
        [
            mixer_out.T,
            shared_in.reshape(shard, 2 * hidden_units),
            shared_out.T,
            jnp.pad(router, ((0, 0), (0, LANES - EXPERTS))),
        ],
        axis=1,
    )
    mine_cot = lax.dynamic_slice_in_dim(cotangent, mp_place * quarter, quarter, 0)
    weight_a, small_all, cot_all = first_gather([pack_a, small], mine_cot, 0)
    weight_a = weight_a.reshape(model, -1)
    cot_all = cot_all.reshape(n, tokens, model)
    pack_b, small_all = lax.optimization_barrier((pack_b, small_all))
    weight_b = lax.all_gather(pack_b, "dp", axis=0, tiled=True)
    out_t = weight_b[:, :inner]
    shared_w = weight_b[:, inner : inner + 2 * hidden_units]
    shared_out_t = weight_b[:, inner + 2 * hidden_units : inner + 3 * hidden_units]
    router_w = weight_b[:, inner + 3 * hidden_units :]

    pieces = []
    start = 0
    for part in misc_parts:
        pieces.append(small_all[:, 0, start : start + part.shape[0]].astype(F32))
        start += part.shape[0]
    local_p = conv_value.shape[1]
    value_rows = jnp.concatenate(pieces[:3], axis=1).reshape(n, taps + 2, local_p, heads)
    value_rows = value_rows.transpose(1, 3, 0, 2).reshape(taps + 2, inner)
    state_rows = jnp.concatenate(pieces[3:5], axis=1).reshape(n, taps + 1, state_cols // n)
    state_rows = state_rows.transpose(1, 0, 2).reshape(taps + 1, state_cols)
    gain_first = pieces[5].reshape(1, model)
    gain_second = pieces[6].reshape(1, model)
    conv_taps = jnp.concatenate([value_rows[:taps], state_rows[:taps]], axis=1)
    conv_bias = jnp.concatenate([value_rows[taps], state_rows[taps]])[None]
    gated_row = value_rows[taps + 1][None]

    group_start = place * tokens
    seg_padded = jnp.concatenate([jnp.full((taps - 1,), -1, jnp.int32), segment_ids])
    seg_ext = lax.dynamic_slice_in_dim(seg_padded, group_start, tokens + taps - 1)
    segments = seg_ext[taps - 1 :]
    prev_seg = seg_ext[taps - 2]
    same = [
        (seg_ext[k : k + tokens] == segments).astype(F32)[:, None] for k in range(taps)
    ]
    blocks = tokens // BLK
    seg_blocks = segments.reshape(blocks, BLK)
    last_segs = seg_blocks[:, BLK - 1]
    prev_segs = jnp.concatenate([prev_seg[None], last_segs[:-1]])
    entry_ok = (seg_blocks == prev_segs[:, None]).astype(F32).reshape(tokens, 1)
    tail_ok = (seg_blocks == last_segs[:, None]).astype(F32).reshape(tokens, 1)
    group_entry_ok = (segments == prev_seg).astype(F32)[:, None]
    group_tail_ok = (segments == segments[tokens - 1]).astype(F32)[:, None]
    seg_f = segments.astype(F32)
    seg_col, seg_row = seg_f[:, None], seg_f[None, :]

    behind = lax.dynamic_index_in_dim(small_all, (place + n - 1) % n, 0, False)
    hidden_ext = jnp.concatenate([behind, hidden], axis=0).astype(F32)
    inv_ext = lax.rsqrt(jnp.mean(hidden_ext * hidden_ext, axis=1, keepdims=True) + EPS)
    normed_ext = (hidden_ext * inv_ext * gain_first).astype(BF)
    normed = normed_ext[16:]
    zx_ext = dot(normed_ext, weight_a)
    gate_z = zx_ext[16:, :inner]
    pre_ext = zx_ext[16 - taps + 1 :, inner : 2 * inner + state_cols]
    head_local = head_params.astype(F32)
    dt_lanes = zx_ext[16:, 2 * inner + state_cols :]
    conv = jnp.broadcast_to(conv_bias, (tokens, inner + state_cols))
    for k in range(taps):
        conv = conv + conv_taps[k][None] * pre_ext[k : k + tokens] * same[k]
    act = jax.nn.silu(conv)
    values = act[:, :inner]
    write = act[:, inner : inner + state_cols // 2]
    read = act[:, inner + state_cols // 2 :]

    live = (jnp.arange(LANES) < heads)[None]
    head_pad = jnp.pad(head_local, ((0, 0), (0, LANES - heads)))
    rate = jnp.where(live, -jnp.exp(head_pad[0:1]), 0.0)
    step = jnp.where(live, jax.nn.softplus(dt_lanes + head_pad[1:2]), 0.0)
    rated = (step * rate).reshape(blocks, BLK, LANES)
    lower = jnp.tril(jnp.ones((BLK, BLK), F32))
    cumul_b = jnp.einsum("ts,bsh->bth", lower, rated, precision=HIGH)
    totals = cumul_b[:, BLK - 1]
    zero_row = jnp.zeros((1, LANES), F32)
    before, after = [zero_row], [zero_row]
    for i in range(blocks - 1):
        before.append(before[-1] + totals[i][None])
        after.append(after[-1] + totals[blocks - 1 - i][None])
    before = jnp.stack(before)
    after = jnp.stack(after[::-1])
    cumul = cumul_b.reshape(tokens, LANES)
    to_end = totals[:, None] - cumul_b
    entry = jnp.exp(cumul) * entry_ok
    tail_bare = jnp.exp(to_end).reshape(tokens, LANES) * tail_ok
    tail = tail_bare * step
    group_entry = jnp.exp(cumul_b + before).reshape(tokens, LANES) * group_entry_ok
    group_tail = jnp.exp(to_end + after).reshape(tokens, LANES) * group_tail_ok * step
    cumul_t = cumul[:, :16].T
    step_t = step[:, :16].T
    expand = (jnp.arange(LANES)[:, None] == jnp.arange(inner)[None, :] // width).astype(F32)
    skip = dot(head_pad[2:3], expand, precision=HIGH)
    outgoing = dot(
        values * dot(group_tail, expand, precision=HIGH), write, ((0,), (0,)), HIGH
    )
    group_decay = group_entry[tokens - 1 :]
    incoming = incoming_state(outgoing, group_decay, expand, False, 1)
    ssd, kept = recur_forward(
        values, write, read, cumul, cumul_t, step_t, entry, tail, seg_col, seg_row, expand, skip, incoming
    )

    gate_act = jax.nn.silu(gate_z)
    gated = ssd * gate_act
    scaled = (gated * gated_row).astype(BF)
    proj_part = dot(scaled, out_t, ((1,), (1,)))
    square_part = jnp.sum(gated * gated, axis=1, keepdims=True)
    proj_pack = jnp.concatenate([proj_part, jnp.broadcast_to(square_part, (tokens, LANES))], axis=1)
    proj_sum = scatter_mp(proj_pack.reshape(4, quarter, -1), 2)
    proj = proj_sum[:, :model]
    square = proj_sum[:, model : model + 1]
    inv_gated = lax.rsqrt(square / DI + EPS)
    mine_hidden = lax.dynamic_slice_in_dim(hidden, mp_place * quarter, quarter, 0).astype(F32)
    mixed = mine_hidden + proj * inv_gated
    inv_second = lax.rsqrt(jnp.mean(mixed * mixed, axis=1, keepdims=True) + EPS)
    unit_second = mixed * inv_second
    ffn_mine = (unit_second * gain_second).astype(BF)

    first_expert = place * own_experts
    ffn_all, cot_rows, rows, position, gates, slot_gates = gather_tokens(
        ffn_mine, cot_all, small_all, router_w, own_experts, 3
    )
    ffn_all = ffn_all.reshape(n, tokens, model)

    slots = n * CAP
    grad_in_rows, grad_expert_out, d_rows, expert_res, slot_dots = run_experts(
        rows.reshape(own_experts, slots, model),
        cot_rows.reshape(own_experts, slots, model),
        slot_gates.reshape(own_experts, slots, LANES),
        expert_in.reshape(own_experts, 2 * model, -1),
        expert_out,
    )
    grad_expert_in = grad_in_rows.reshape(expert_in.shape)

    ffn_block = lax.dynamic_index_in_dim(ffn_all, place, 0, False)
    shared_mid = dot(ffn_block, shared_w)
    shared_gate, shared_up = shared_mid[:, :hidden_units], shared_mid[:, hidden_units:]
    shared_silu = jax.nn.silu(shared_gate)
    shared_act = (shared_silu * shared_up).astype(BF)
    shared_res = dot(shared_act, shared_out_t, ((1,), (1,)))
    d_shared_act = dot(cotangent, shared_out_t)
    d_shared_mid = jnp.concatenate(
        [d_shared_act * shared_up * silu_slope(shared_gate), d_shared_act * shared_silu], axis=1
    ).astype(BF)
    d_ffn_shared = dot(d_shared_mid, shared_w, ((1,), (1,)))

    if n > 8:
        d_ffn_pack = put_rows(position, [(d_rows, d_ffn_shared)], slot_dots)
        d_ffn_sum = scatter_tokens(d_ffn_pack.reshape(n, 4, quarter, -1), 4)
        expert_res, d_ffn_sum = lax.optimization_barrier((expert_res, d_ffn_sum))
        res_pack = put_rows(position, [(expert_res, shared_res)])
        res_sum = scatter_tokens(res_pack.reshape(n, 4, quarter, model), 10)
    else:
        pack = put_rows(position, [(expert_res, shared_res), (d_rows, d_ffn_shared)], slot_dots)
        both_sums = scatter_tokens(pack.reshape(n, 4, quarter, -1), 4)
        res_sum, d_ffn_sum = both_sums[:, :model], both_sums[:, model:]

    own_tokens_gates = lax.dynamic_slice(
        gates, (place, mp_place * quarter, 0), (1, quarter, LANES)
    ).reshape(quarter, LANES)
    dots = d_ffn_sum[:, model : model + LANES]
    share = jnp.sum(own_tokens_gates * dots, axis=1, keepdims=True)
    d_logits = (own_tokens_gates * (dots - share)).astype(BF)
    d_ffn = d_ffn_sum[:, :model] + dot(d_logits, router_w, ((1,), (1,)))
    mine_cot_f = mine_cot.astype(F32)
    grad_gain_second = jnp.sum(d_ffn * unit_second, axis=0)
    d_unit = d_ffn * gain_second
    d_mixed = mine_cot_f + inv_second * (
        d_unit - unit_second * jnp.mean(d_unit * unit_second, axis=1, keepdims=True)
    )
    d_proj_mine = (d_mixed * inv_gated).astype(BF)
    d_inv = jnp.sum(d_mixed * proj, axis=1, keepdims=True)
    d_square = d_inv * -0.5 * inv_gated * inv_gated * inv_gated / DI
    d_square_high = d_square.astype(BF)
    d_square_low = (d_square - d_square_high.astype(F32)).astype(BF)
    sent = jnp.concatenate(
        [
            d_proj_mine,
            d_logits[:, :EXPERTS],
            d_square_high,
            d_square_low,
            jnp.zeros((quarter, LANES - EXPERTS - 2), BF),
        ],
        axis=1,
    )
    (got,) = gather_mp([sent], 5)
    got = got.reshape(tokens, model + LANES)
    d_proj = got[:, :model]
    d_logits_all = jnp.pad(got[:, model : model + EXPERTS], ((0, 0), (0, LANES - EXPERTS)))
    d_square_all = got[:, model + EXPERTS : model + EXPERTS + 1].astype(F32) + got[
        :, model + EXPERTS + 1 : model + EXPERTS + 2
    ].astype(F32)

    rows0 = ((0,), (0,))
    grad_b = weight_grads(
        [
            (d_proj, scaled),
            (ffn_block, d_shared_mid),
            (cotangent, shared_act),
            (ffn_block, d_logits_all),
        ]
    )
    grad_b, d_proj = lax.optimization_barrier((grad_b, d_proj))
    sum_b = lax.psum_scatter(grad_b, "dp", scatter_dimension=0, tiled=True).astype(F32)
    d_scaled = dot(d_proj, out_t)
    grad_gated_row = jnp.sum(d_scaled * gated, axis=0)
    d_gated = d_scaled * gated_row + 2.0 * gated * d_square_all
    d_ssd = d_gated * gate_act
    d_gate_z = d_gated * ssd * silu_slope(gate_z)

    direct = dot(d_ssd * dot(group_entry, expand, precision=HIGH), read, rows0, HIGH)
    state_grad = incoming_state(direct, group_decay, expand, True, 6)
    d_values, d_write, d_read, d_step, d_rated, d_skip_row = recur_backward(
        values,
        write,
        read,
        cumul,
        cumul_t,
        step_t,
        step,
        entry,
        tail_bare,
        seg_col,
        seg_row,
        expand,
        skip,
        kept,
        d_ssd,
        state_grad,
    )
    d_rate = jnp.sum(d_rated * step, axis=0, keepdims=True)
    d_dt = jnp.where(
        live, (d_step + rate * d_rated) * jax.nn.sigmoid(dt_lanes + head_pad[1:2]), 0.0
    )
    d_skip = dot(d_skip_row, expand, ((1,), (1,)), HIGH)
    grad_head = jnp.concatenate(
        [d_rate * rate, jnp.sum(d_dt, axis=0, keepdims=True), d_skip], axis=0
    )[:, :heads]

    slope = silu_slope(conv)
    d_conv_values = d_values * slope[:, :inner]
    d_state_act, rim_ahead = sum_and_edge(
        jnp.concatenate([d_write, d_read], axis=1), slope[:16, inner:], d_conv_values[:16], 11
    )
    d_conv = jnp.concatenate([d_conv_values, d_state_act * slope[:, inner:]], axis=1)
    d_conv_ext = jnp.concatenate([d_conv, rim_ahead], axis=0)
    seg_after = lax.dynamic_slice_in_dim(
        jnp.concatenate([segment_ids, jnp.full((taps - 1,), -1, jnp.int32)]),
        group_start,
        tokens + taps - 1,
    )
    d_pre = jnp.zeros_like(d_conv)
    grad_rows = []
    for k in range(taps):
        ahead = taps - 1 - k
        ok = (seg_after[ahead : ahead + tokens] == segments).astype(F32)[:, None]
        d_pre = d_pre + conv_taps[k][None] * d_conv_ext[ahead : ahead + tokens] * ok
        grad_rows.append(jnp.sum(d_conv * pre_ext[k : k + tokens] * same[k], axis=0))
    grad_rows.append(jnp.sum(d_conv, axis=0))
    d_a = jnp.concatenate([d_gate_z, d_pre, d_dt], axis=1).astype(BF)

    d_state_mine = lax.dynamic_slice_in_dim(
        d_a[:, 2 * inner : 2 * inner + state_cols], mp_place * quarter, quarter, 0
    )
    d_normed_part = dot(d_a[:, : 2 * inner], weight_a[:, : 2 * inner], ((1,), (1,))) + dot(
        d_a[:, 2 * inner + state_cols :], weight_a[:, 2 * inner + state_cols :], ((1,), (1,))
    )
    d_state_rows = dot(
        d_state_mine, weight_a[:, 2 * inner : 2 * inner + state_cols], ((1,), (1,))
    )
    grad_a = dot(normed, d_a, rows0).astype(BF)
    unit_first = hidden_ext[16:] * inv_ext[16:]
    mine_unit = lax.dynamic_slice_in_dim(unit_first, mp_place * quarter, quarter, 0)
    grad_gain_first = jnp.sum(d_normed_part * unit_first, axis=0) + jnp.sum(
        d_state_rows * mine_unit, axis=0
    )

    value_grads = jnp.stack([g[:inner] for g in grad_rows] + [grad_gated_row])
    value_grads = value_grads.reshape(taps + 2, heads, n, local_p).transpose(2, 0, 3, 1)
    state_grads = jnp.stack([g[inner:] for g in grad_rows])
    state_grads = state_grads.reshape(taps + 1, n, state_cols // n).transpose(1, 0, 2)
    misc_grads = [
        value_grads.reshape(n, -1),
        state_grads.reshape(n, -1),
        jnp.broadcast_to(grad_head.reshape(1, -1), (n, 3 * heads)),
    ]
    sizes = [g.shape[1] for g in misc_grads]
    misc_grads = jnp.concatenate(misc_grads, axis=1)
    misc_grads = jnp.pad(misc_grads, ((0, 0), (0, 32 * LANES - misc_grads.shape[1])))
    gains = jnp.concatenate(
        [grad_gain_first.reshape(n, shard), grad_gain_second.reshape(n, shard)], axis=1
    )
    gains = jnp.pad(gains, ((0, 0), (0, 16 * LANES - 2 * shard)))
    mine_result = (mixed + res_sum).astype(BF)
    sum_a, misc_sum, gains_sum, hidden_all, result = last_exchange(
        grad_a.reshape(n, shard, -1),
        misc_grads.reshape(n, 32, LANES),
        gains.reshape(n, 16, LANES),
        d_normed_part.astype(BF).reshape(4, quarter, model),
        d_state_rows,
        d_mixed,
        mine_hidden,
        gain_first,
        mine_result,
        8,
    )
    result = result.reshape(tokens, model)
    misc_sum = misc_sum.reshape(-1)
    gains_sum = gains_sum.reshape(-1)
    cut = [0]
    for size in sizes:
        cut.append(cut[-1] + size)
    value_sum = misc_sum[: cut[1]].reshape(taps + 2, local_p, heads)
    state_sum = misc_sum[cut[1] : cut[2]].reshape(taps + 1, state_cols // n)
    head_sum = misc_sum[cut[2] : cut[3]].reshape(3, heads)

    b1, b2 = inner, inner + 2 * hidden_units
    b3 = b2 + hidden_units
    return (
        result,
        hidden_all.reshape(tokens, model).astype(F32),
        gains_sum[:shard],
        sum_a[:, : 2 * inner].reshape(shard, 2, inner),
        sum_a[:, 2 * inner : 2 * inner + state_cols],
        sum_a[:, 2 * inner + state_cols : 2 * inner + state_cols + heads],
        value_sum[:taps],
        value_sum[taps],
        state_sum[:taps],
        state_sum[taps],
        head_sum,
        value_sum[taps + 1],
        sum_b[:, :b1].T,
        gains_sum[shard : 2 * shard],
        sum_b[:, b3 : b3 + EXPERTS],
        sum_b[:, b1:b2].reshape(shard, 2, hidden_units),
        sum_b[:, b2:b3].T,
        grad_expert_in,
        grad_expert_out,
    )


def solution(mesh):
    placed = (
        P("dp", None),
        P(),
        P("dp", None),
        P("dp"),
        P("dp", None, "mp"),
        P("dp", None),
        P("dp", "mp"),
        P(None, "dp", "mp"),
        P("dp", "mp"),
        P(None, "dp"),
        P("dp"),
        P(None, "mp"),
        P("dp", "mp"),
        P("mp", "dp"),
        P("dp"),
        P("dp", None),
        P("dp", None, "mp"),
        P("mp", "dp"),
        P("dp", None, None, "mp"),
        P("dp", "mp", None),
        P("dp", None),
    )
    return jax.shard_map(
        per_device,
        mesh=mesh,
        in_specs=placed,
        out_specs=(
            P("dp", None),
            P("dp", None),
            P("dp"),
            P("dp", None, "mp"),
            P("dp", None),
            P("dp", "mp"),
            P(None, "dp", "mp"),
            P("dp", "mp"),
            P(None, "dp"),
            P("dp"),
            P(None, "mp"),
            P("dp", "mp"),
            P("mp", "dp"),
            P("dp"),
            P("dp", None),
            P("dp", None, "mp"),
            P("mp", "dp"),
            P("dp", None, None, "mp"),
            P("dp", "mp", None),
        ),
        check_vma=False,
    )
```

profile of v0, /device:TPU:0, one launch (start us, length us, event | category | flops | bytes accessed | tf_op | source)
XLA Modules:
  0.0 783.0 jit_solution(17389082508222220046)
XLA Ops:
  13.2 2.1 concatenate.77
  17.9 1.8 constant_dynamic-slice_fusion.refs_2_
  21.2 101.6 %shard_map.348 = (bf16[8,192,1920]{2,1,0:T(8,128)(2,1)}, bf16[8,16,1536]{2,1,0:T(8,128)(2,1)}, bf16[8,4,128,1536]{3,2,1,0:T(8,128)(2,1)}) custom-call(bf16[192,1920]{1,0:T(8,128)(2,1)} %fusion.34.refs_0_, bf16[16,1536]{1,0:T(8,128)(2,1)} %fusion.67.refs_1_, bf16[128,1536]{1,0:T(8,128)(2,1)} %constant_dynamic-slice_fusion.refs_2_), custom_call_target="tpu_custom_call" | custom-call | tf_op jit(solution)/shard_map/pallas_call | solution.py:808
  129.2 6.5 fusion.109
  135.9 1.8 copy-done.3
  142.2 1.4 fusion.77
  143.6 6.4 add_multiply_fusion
  150.6 1.4 slice.552.values
  155.0 2.6 fusion.24.mine
  157.7 41.6 %shard_map.349.start = f32[768,128]{1,0:T(8,128)S(1)} custom-call(f32[768,128]{1,0:T(8,128)S(1)} %fusion.24.mine, f32[8,128]{1,0:T(8,128)S(1)} %broadcast_in_dim.102.decay, f32[128,768]{1,0:T(8,128)S(1)} %fusion.45.expand), custom_call_target="tpu_custom_call" | custom-call | tf_op jit(solution)/shard_map/pallas_call | solution.py:1477
  199.5 10.0 %shard_map.350 = (f32[512,768]{1,0:T(8,128)S(1)}, f32[4,768,128]{2,1,0:T(8,128)S(1)}) custom-call(f32[512,768]{1,0:T(8,128)} %slice.552.values, f32[512,128]{1,0:T(8,128)S(1)} %get-tuple-element.199.write, f32[512,128]{1,0:T(8,128)S(1)} %get-tuple-element.198.read, f32[512,128]{1,0:T(8,128)S(1)} %bitcast.169, f32[16,512]{1,0:T(8,128)S(1)} %copy.89.cumul_t, ...), custom_call_target="tpu_custom_call" | custom-call | tf_op jit(solution)/shard_map/pallas_call | solution.py:1197
  209.5 3.0 multiply_convert_fusion.2
  213.9 2.5 all-gather.2.cloned.1.call-done
  216.4 3.1 fusion.12
  219.8 23.3 %shard_map.351 = f32[128,1664]{1,0:T(8,128)S(1)} custom-call(f32[4,128,1664]{2,1,0:T(8,128)S(1)} %bitcast.165), custom_call_target="tpu_custom_call" | custom-call | tf_op jit(solution)/shard_map/pallas_call | solution.py:404
  243.3 1.3 multiply_reduce_fusion.12
  245.5 1.8 slice.567.router
  247.2 85.6 %shard_map.352 = (bf16[8,4,128,1536]{3,2,1,0:T(8,128)(2,1)}, bf16[8,8,64,1536]{3,2,1,0:T(8,128)(2,1)}, bf16[8,8,64,1536]{3,2,1,0:T(8,128)(2,1)}, f32[8,8,512]{2,...) custom-call(bf16[128,1536]{1,0:T(8,128)(2,1)} %multiply_convert_fusion.4.x, ...), custom_call_target="tpu_custom_call" | custom-call | tf_op jit(solution)/shard_map/pallas_call | solution.py:761
  332.9 1.5 dynamic-slice_bitcast_fusion.refs_1_.refs_3_
  334.4 3.0 fusion.29
  337.4 1.8 multiply_convert_fusion.6
  340.1 33.1 %shard_map.353 = (f32[8,3072,128]{2,1,0:T(8,128)}, f32[8,128,1536]{2,1,0:T(8,128)}, bf16[8,512,1536]{2,1,0:T(8,128)(2,1)}, bf16[8,512,1536]{2,1,0:T(8,128)(2,1)}, bf16[8,512,128]{2,1,0:T(8,128)(2,1)}) custom-call(bf16[8,512,1536]{2,1,0:T(8,128)(2,1)} %bitcast.178, bf16[8,512,1536]{2,1,0:T(8,128)(2,1)} %bitcast.177, f32[8,512,128]{2,1,0:T(8,128)} %bitcast.187, ...), custom_call_target="tpu_custom_call" | custom-call | tf_op jit(solution)/shard_map/pallas_call | solution.py:1566
  373.1 4.1 fusion.27.refs_3_
  377.3 3.4 fusion.36.refs_1_
  380.7 25.8 %shard_map.354 = bf16[8,512,3200]{2,1,0:T(8,128)(2,1)} custom-call(f32[8,8,512]{2,1,0:T(8,128)} %get-tuple-element.59.position, bf16[8,8,64,1536]{3,2,1,0:T(8,128)(2,1)} %bitcast.176, f32[512,1536]{1,0:T(8,128)} %fusion.36.refs_1_, bf16[8,8,64,1536]{3,2,1,0:T(8,128)(2,1)} %bitcast.175, f32[512,1536]{1,0:T(8,128)} %fusion.27.refs_3_, ...), custom_call_target="tpu_custom_call" | custom-call | tf_op jit(solution)/shard_map/pallas_call | solution.py:1613
  406.5 125.2 %shard_map.355 = (f32[128,3200]{1,0:T(8,128)}, bf16[8,2,128,3200]{3,2,1,0:T(8,128)(2,1)}) custom-call(bf16[8,4,128,3200]{3,2,1,0:T(8,128)(2,1)} %bitcast.174), custom_call_target="tpu_custom_call" | custom-call | tf_op jit(solution)/shard_map/pallas_call | solution.py:1016
  533.6 2.6 multiply_reduce_fusion.8
  539.7 14.7 %shard_map.356 = bf16[4,128,1664]{2,1,0:T(8,128)(2,1)} custom-call(bf16[128,1664]{1,0:T(8,128)(2,1)} %concatenate.88.refs_0_), custom_call_target="tpu_custom_call" | custom-call | tf_op jit(solution)/shard_map/pallas_call | solution.py:455
  554.5 2.7 slice.573.refs_0_
  558.7 8.7 %shard_map.357 = bf16[1536,1664]{1,0:T(8,128)(2,1)} custom-call(bf16[512,1536]{1,0:T(8,128)(2,1)} %slice.573.refs_0_, bf16[512,1536]{1,0:T(8,128)(2,1)} %copy-done.11, bf16[512,1536]{1,0:T(8,128)(2,1)} %refs_2_.1, bf16[512,1536]{1,0:T(8,128)(2,1)} %copy-done.11, bf16[512,768]{1,0:T(8,128)(2,1)} %copy-done.16, bf16[512,512]{1,0:T(8,128)(2,1)} %pad_maximum_fusion.5.refs_5_, ...), custom_call_target="tpu_custom_call" | custom-call | tf_op jit(solution)/shard_map/pallas_call | solution.py:1637
  569.0 2.0 dynamic-slice_convert_fusion.hidden
  572.2 1.7 multiply_reduce_fusion.14
  573.9 5.5 multiply_convert_fusion.1
  580.5 3.6 fusion.21.mine
  584.1 33.2 %shard_map.358.start = f32[768,128]{1,0:T(8,128)S(1)} custom-call(f32[768,128]{1,0:T(8,128)S(1)} %fusion.21.mine, f32[8,128]{1,0:T(8,128)S(1)} %broadcast_in_dim.102.decay, f32[128,768]{1,0:T(8,128)S(1)} %fusion.45.expand), custom_call_target="tpu_custom_call" | custom-call | tf_op jit(solution)/shard_map/pallas_call | solution.py:1477
  617.3 24.0 %shard_map.359 = (f32[512,768]{1,0:T(8,128)S(1)}, f32[512,128]{1,0:T(8,128)S(1)}, f32[512,128]{1,0:T(8,128)S(1)}, f32[512,128]{1,0:T(8,128)S(1)}, f32[512,128]{1,0:T(8,128)S(1)}, /*index=5*/f32[1,768]{1,0:T(1,128)S(1)}) custom-call(f32[512,768]{1,0:T(8,128)} %slice.552.values, f32[512,128]{1,0:T(8,128)S(1)} %get-tuple-element.199.write, ...), custom_call_target="tpu_custom_call" | custom-call | tf_op jit(solution)/shard_map/pallas_call | solution.py:1324
  641.6 16.2 %shard_map.360 = (f32[512,256]{1,0:T(8,128)S(1)}, f32[16,1024]{1,0:T(8,128)S(1)}) custom-call(f32[512,256]{1,0:T(8,128)S(1)} %pad_maximum_fusion.6.part, f32[16,256]{1,0:T(8,128)S(1)} %slice.578.slope, f32[16,768]{1,0:T(8,128)S(1)} %slice.579.rim), custom_call_target="tpu_custom_call" | custom-call | tf_op jit(solution)/shard_map/pallas_call | solution.py:1096
  658.3 1.8 fusion.5
  660.9 2.6 fusion
  663.6 1.8 multiply_reduce_fusion.1
  668.0 5.2 multiply_reduce_fusion.2
  675.8 6.9 convolution_convert_fusion
  682.7 73.4 %shard_map.361 = (f32[192,1920]{1,0:T(8,128)}, f32[32,128]{1,0:T(8,128)}, f32[16,128]{1,0:T(8,128)}, bf16[4,128,1536]{2,1,0:T(8,128)(2,1)}, bf16[4,128,1536]{2,1,0:T(8,128)(2,1)}) custom-call(bf16[8,192,1920]{2,1,0:T(8,128)(2,1)} %bitcast.185, f32[8,32,128]{2,1,0:T(8,128)} %bitcast.195, f32[8,16,128]{2,1,0:T(8,128)} %bitcast.199, ...), custom_call_target="tpu_custom_call" | custom-call | tf_op jit(solution)/shard_map/pallas_call | solution.py:350
  756.1 1.4 slice.521
  757.5 1.7 slice.522
  760.9 1.8 reshape.491
  766.7 1.4 fusion.107
  768.1 2.2 bitcast_convert_fusion
  (258 shorter events, 57.2 us)
Async XLA Ops:
  7.2 12.4 %copy-start.27 = (bf16[192,256]{1,0:T(8,128)(2,1)S(1)}, bf16[192,256]{1,0:T(8,128)(2,1)}, u32[]{:S(2)}) copy-start(bf16[192,256]{1,0:T(8,128)(2,1)} %param.26) | copy-start | bytes 294916
  7.2 209.2 %all-gather.2.cloned.1.call-start = ((), (), s32[]{:S(2)}) async-start(), calls=%async_computation.1 | async-start | bytes 5750784 | tf_op jit(solution)/shard_map/all_gather | solution.py:1748
  9.2 113.6 %copy-start.26 = (bf16[768,192]{0,1:T(8,128)(2,1)S(1)}, bf16[768,192]{0,1:T(8,128)(2,1)}, u32[]{:S(2)}) copy-start(bf16[768,192]{0,1:T(8,128)(2,1)} %param.34) | copy-start | bytes 884740
  9.2 113.6 %copy-start.28 = (bf16[256,192]{0,1:T(8,128)(2,1)S(1)}, bf16[256,192]{0,1:T(8,128)(2,1)}, u32[]{:S(2)}) copy-start(bf16[256,192]{0,1:T(8,128)(2,1)} %param.38) | copy-start | bytes 294916
  19.6 108.6 %copy-start.7 = (bf16[512,1536]{1,0:T(8,128)(2,1)S(1)}, bf16[512,1536]{1,0:T(8,128)(2,1)}, u32[]{:S(2)}) copy-start(bf16[512,1536]{1,0:T(8,128)(2,1)} %param.21) | copy-start | bytes 4718596
  122.8 5.9 copy-start.35
  123.8 646.5 %reduce-scatter.2.cloned.1.call-start = ((), (), s32[]{:S(2)}) async-start(), calls=%async_computation.2 | async-start | bytes 5750784 | tf_op jit(solution)/shard_map/reduce_scatter | solution.py:1943
  124.0 11.7 %copy-start.33 = (pred[128]{0:T(512)(128)(4,1)}, pred[128]{0:T(512)(128)(4,1)S(1)}, u32[]{:S(2)}) copy-start(pred[128]{0:T(512)(128)(4,1)S(1)} %iota_compare_fusion.12) | copy-start | bytes 388
  129.2 6.5 copy-start.20
  135.7 2.0 copy-start.3
  135.7 4.5 copy-start.30
  150.5 1.8 copy-start.9
  153.3 0.7 copy-start.24
  153.3 1.7 copy-start.10
  209.5 3.0 copy-start
  209.5 3.0 copy-start.1
  212.6 1.2 copy-start.14
  212.6 6.9 copy-start.16
  243.3 89.6 %copy-start.31 = (f32[128]{0:T(128)}, f32[128]{0:T(128)S(1)}, u32[]{:S(2)}) copy-start(f32[128]{0:T(128)S(1)} %fusion.65) | copy-start | bytes 1540
  334.4 3.0 copy-start.11
  334.4 3.0 copy-start.15
  339.2 38.1 %copy-start.23 = (bf16[512,256]{1,0:T(8,128)(2,1)}, bf16[512,256]{1,0:T(8,128)(2,1)S(1)}, u32[]{:S(2)}) copy-start(bf16[512,256]{1,0:T(8,128)(2,1)S(1)} %get-tuple-element.202.refs_6_) | copy-start | bytes 786436
  536.2 1.4 copy-start.32
  567.4 3.6 copy-start.25
  568.2 3.6 copy-start.8
  571.0 2.9 copy-start.4
  571.8 2.1 copy-start.2
  579.4 1.1 copy-start.13
  617.3 24.1 %copy-start.12 = (f32[512,1024]{1,0:T(8,128)S(1)}, f32[512,1024]{1,0:T(8,128)}, u32[]{:S(2)}) copy-start(f32[512,1024]{1,0:T(8,128)} %get-tuple-element.176) | copy-start | bytes 6291460
  641.6 16.7 %copy-start.5 = (f32[512,768]{1,0:T(8,128)}, f32[512,768]{1,0:T(8,128)S(1)}, u32[]{:S(2)}) copy-start(f32[512,768]{1,0:T(8,128)S(1)} %slice_multiply_fusion.4) | copy-start | bytes 4718596
  657.9 2.3 slice-start.1
  658.3 1.8 copy-start.34
  658.3 2.5 slice-start.2
  658.3 2.7 copy-start.36
  660.1 3.5 copy-start.18
  663.6 1.9 slice-start
  665.4 2.6 copy-start.6
  673.2 2.6 copy-start.19
  673.2 2.6 copy-start.37
  756.1 4.0 copy-start.29
  757.5 10.6 %copy-start.22 = (bf16[4,128,1536]{2,1,0:T(8,128)(2,1)S(1)}, bf16[4,128,1536]{2,1,0:T(8,128)(2,1)}, u32[]{:S(2)}) copy-start(bf16[4,128,1536]{2,1,0:T(8,128)(2,1)} %get-tuple-element.80) | copy-start | bytes 4718596
  770.3 2.8 copy-start.17
  771.5 3.3 copy-start.21
Sparse Core Ops, SparseCore 0:
  123.9 92.4 all-gather.1
  567.5 110.0 reduce-scatter.1
where the time goes:
time: 788 us; the launch traced here: 783 us
  Pallas kernels  616 us (78%)
  local copies, waits for them, and re-layouts  55.8 us (7%)
  matrix products  51.2 us (6%)
  other arithmetic  41.5 us (5%)
  between operations  15.4 us (2%)
    pallas_call x1, Pallas kernels, scatter_tokens(): pl.pallas_call(partial(token_scatter_kernel, n), out_shape=[jax.ShapeDtyp...  125 us
    pallas_call x1, Pallas kernels, first_gather(): pl.pallas_call(partial(first_kernel, n, k), out_shape=[jax.ShapeDtypeStru...  102 us
    pallas_call x1, Pallas kernels, gather_tokens(): pl.pallas_call(partial(token_gather_kernel, n, both, own), out_shape=[jax...  85.6 us
    pallas_call x2, Pallas kernels, state_scan(): pl.pallas_call(partial(state_scan_kernel, n, reverse), out_shape=jax.Shap...  74.8 us
    pallas_call x1, Pallas kernels, last_exchange(): pl.pallas_call(partial(last_kernel, n), out_shape=[jax.ShapeDtypeStruct(a...  73.4 us
    dot_general x18, matrix products, dot(): lax.dot_general(a, b, (dims, ((), ())), precision=precision, preferred_el...  50.8 us
    pallas_call x1, Pallas kernels, run_experts(): pl.pallas_call(partial(expert_kernel, own), grid=(own, slots // part), ou...  33.1 us
    pallas_call x1, Pallas kernels, put_rows(): pl.pallas_call(partial(put_kernel, own, len(parts)), grid=(n,), out_shape...  25.8 us
  transfers between devices with their start and end apart: 2, of which 1 were waited for; matrix products, arithmetic and copies ran while one was open for 11% of the time, Pallas kernels for 25%

commit v1 on v0

--- a/solution.py
+++ b/solution.py
@@ -197,8 +197,13 @@
             if s == n // 2:
                 for way in range(2):
                     self.copies[s - 1, j, i, way].wait_recv()
-                mine = array.at[ring_device(n, p), part]
-                add_rows(out.at[part], [mine, slots.at[s - 1, 0, part], slots.at[s - 1, 1, part]], size, F32)
+                start_col = 0
+                for ref in out:
+                    cols = pl.ds(start_col, ref.shape[1])
+                    start_col += ref.shape[1]
+                    pieces = [array.at[ring_device(n, p), part, cols]]
+                    pieces += [slots.at[s - 1, way, part, cols] for way in range(2)]
+                    add_rows(ref.at[part], pieces, size, F32)
                 continue
             for way in range(2):
                 if s == 0 and i % 2 != way:
@@ -237,7 +242,9 @@
     hidden,
     gain,
     result,
-    out_a,
+    out_zx,
+    out_state,
+    out_dt,
     out_misc,
     out_gains,
     all_hidden,
@@ -264,7 +271,7 @@
     ring = RingScatter(
         n,
         [grad_a, misc, gains_mine],
-        [out_a, out_misc, out_gains],
+        [(out_zx, out_state, out_dt), (out_misc,), (out_gains,)],
         [slots_a, slots_misc, slots_gains],
         [ring_send, ring_recv],
     )
@@ -342,16 +349,19 @@
     ring.end()
 
 
-def last_exchange(grad_a, misc, gains, d_normed, extra, d_mixed, hidden, gain, result, cid):
+def last_exchange(grad_a, misc, gains, d_normed, extra, d_mixed, hidden, gain, result, cols, cid):
     n = lax.axis_size("dp")
+    shard = grad_a.shape[1]
     rows, model = d_mixed.shape
     dma = pltpu.SemaphoreType.DMA
     every = jax.ShapeDtypeStruct((4, rows, model), BF)
     return pl.pallas_call(
         partial(last_kernel, n),
-        out_shape=[jax.ShapeDtypeStruct(a.shape[1:], F32) for a in (grad_a, misc, gains)] + [every, every],
+        out_shape=[jax.ShapeDtypeStruct((shard, c), F32) for c in cols]
+        + [jax.ShapeDtypeStruct(a.shape[1:], F32) for a in (misc, gains)]
+        + [every, every],
         in_specs=[VM] * 8 + [ANY],
-        out_specs=[VM] * 3 + [ANY] * 2,
+        out_specs=[VM] * 5 + [ANY] * 2,
         scratch_shapes=[
             pltpu.VMEM(gains.shape, F32),
             pltpu.VMEM(gains.shape, F32),
@@ -468,13 +478,16 @@
 
 class TokenGather:
     def __init__(self, n, both, x, out, sems):
-        self.n, self.both, self.x, self.out = n, both, x, out
+        self.n, self.both, self.out = n, both, out
         self.local, self.ring_s, self.ring_r, self.core_s, self.core_r, self.chip_s, self.chip_r = sems
         self.d, self.m = lax.axis_index("dp"), lax.axis_index("mp")
         self.far = (self.m + 2) % 4
         self.core, self.chip = mp_partners(self.m)
         self.p, self.nxt, self.prv = ring_neighbours(n)
-        self.pieces = [(0,) + c for c in chunk_rows(0, x.shape[0])] + [(1,) + c for c in chunk_rows(0, both)]
+        rows = out.shape[2]
+        base = pl.multiple_of(self.m * rows, rows) if x.shape[0] > rows else 0
+        self.x = x.at[pl.ds(base, rows)]
+        self.pieces = [(0,) + c for c in chunk_rows(0, rows)] + [(1,) + c for c in chunk_rows(0, both)]
         self.sent, self.pending = [], {}
         self.ring, self.chips = {}, {}
 
@@ -582,17 +595,22 @@
 
 
 class SlotWork:
-    def __init__(self, own, small, router, position, gates, slot_gates, earlier):
-        self.own, self.small, self.router = own, small, router
-        self.position, self.gates, self.slot_gates, self.earlier = position, gates, slot_gates, earlier
+    def __init__(self, own, small, position):
+        self.own, self.small, self.position = own, small, position
         self.first = (lax.axis_index("dp") * own).astype(F32)
-        length = earlier.shape[0]
-        row = lax.broadcasted_iota(jnp.int32, (length, length), 0)
-        col = lax.broadcasted_iota(jnp.int32, (length, length), 1)
+        self.length = position.shape[2]
+
+    def count_with(self, earlier):
+        self.earlier = earlier
+        row = lax.broadcasted_iota(jnp.int32, earlier.shape, 0)
+        col = lax.broadcasted_iota(jnp.int32, earlier.shape, 1)
         earlier[...] = jnp.where(row < col, 1.0, 0.0).astype(BF)
 
+    def gate_with(self, router, gates, slot_gates):
+        self.router, self.gates, self.slot_gates = router, gates, slot_gates
+
     def named(self, block, first, count):
-        length = self.earlier.shape[0]
+        length = self.length
         routes = self.small[block, :, 0:length].astype(F32)
         expert = lax.broadcasted_iota(jnp.int32, (count, length), 0).astype(F32) + first
         found = routes[1:2, :] == expert
@@ -634,7 +652,7 @@
         self.loads, self.stores = [], []
 
     def load(self, block):
-        at = len(self.loads) % 2
+        at = len(self.loads) % self.in_buf.shape[0]
         copy = pltpu.make_async_copy(self.source.at[block], self.in_buf.at[at], self.load_sem.at[at])
         copy.start()
         self.loads.append(copy)
@@ -642,7 +660,7 @@
     def take(self, i, wait=True):
         if wait:
             self.loads[i].wait()
-        held = self.in_buf[i % 2]
+        held = self.in_buf[i % self.in_buf.shape[0]]
         return held.reshape(-1, held.shape[-1])
 
     def give(self, i, block, picked):
@@ -664,47 +682,62 @@
     n,
     both,
     own,
+    units,
     x,
-    y,
+    position,
     small,
-    router,
+    weights,
+    cot,
     out,
-    y_rows,
     x_rows,
-    position,
     gates,
     slot_gates,
-    earlier,
-    y_in,
-    y_out,
+    block,
+    act,
+    d_mid,
+    shared_res,
+    shared_d,
     x_in,
     x_out,
+    mid,
     stream_sem,
     *sems,
 ):
+    inner = weights.shape[1] - 3 * units - LANES
+    shared_in = pl.ds(inner, 2 * units)
+    shared_out = pl.ds(inner + 2 * units, units)
+    router = weights.at[:, pl.ds(inner + 3 * units, LANES)]
     gather = TokenGather(n, both, x, out, sems)
-    work = SlotWork(own, small, router, position, gates, slot_gates, earlier)
-    y_stream = RowStream(y, y_rows, y_in, y_out, stream_sem.at[0], stream_sem.at[1])
-    x_stream = RowStream(out, x_rows, x_in, x_out, stream_sem.at[2], stream_sem.at[3])
+    work = SlotWork(own, small, position)
+    work.gate_with(router, gates, slot_gates)
+    x_stream = RowStream(out, x_rows, x_in, x_out, stream_sem.at[0], stream_sem.at[1])
     half = n // 2
-    y_stream.load(0)
     greet([gather.core, gather.chip, gather.nxt, gather.prv])
     gather.begin()
-
     tasks = []
 
-    def pick_y(b):
-        held = {}
-
-        def start():
-            if b + 1 < n:
-                y_stream.load(b + 1)
-            held["pick"] = work.pick(b)
-
-        def finish():
-            y_stream.give(b, b, dot(held["pick"], y_stream.take(b)))
-
-        return [start, finish]
+    def shared(held):
+        def first():
+            block[...] = x_stream.take(held["at"])
+            mid[...] = dot(block[...], weights[:, shared_in])
+
+        def second():
+            gate, up = mid[:, 0:units], mid[:, units : 2 * units]
+            sig = jax.nn.sigmoid(gate)
+            silu = gate * sig
+            act[...] = (silu * up).astype(BF)
+            d_act = dot(cot[...], weights[:, shared_out])
+            slope = sig * (1.0 + gate * (1.0 - sig))
+            d_mid[:, 0:units] = (d_act * up * slope).astype(BF)
+            d_mid[:, units : 2 * units] = (d_act * silu).astype(BF)
+
+        def third():
+            shared_res[...] = dot(act[...], weights[:, shared_out], ((1,), (1,)))
+
+        def fourth():
+            shared_d[...] = dot(d_mid[...], weights[:, shared_in], ((1,), (1,)))
+
+        return [first, second, third, fourth]
 
     def pick_x(s):
         blocks = gather.blocks(s)
@@ -717,11 +750,14 @@
                 x_stream.load(block)
 
         found = [start]
+        if s == 0:
+            found += shared(held)
         for i, block in enumerate(blocks):
 
             def pick(i=i, block=block):
                 held[i] = work.pick(block)
-                x_stream.give(held["at"] + i, block, dot(held[i], x_stream.take(held["at"] + i)))
+                rows = x_stream.take(held["at"] + i, s > 0)
+                x_stream.give(held["at"] + i, block, dot(held[i], rows))
 
             def gate(i=i, block=block):
                 work.gate(block, x_stream.take(held["at"] + i, False), held[i])
@@ -730,59 +766,81 @@
         return found
 
     def between():
-        for _ in range(2):
+        for _ in range(1 if len(tasks) < 6 else 2):
             if tasks:
                 tasks.pop(0)()
 
     gather.step(0)
-    for b in range(n):
-        work.place(b)
-        tasks += pick_y(b)
-    for _ in range(4):
-        tasks.pop(0)()
     for s in range(1, half + 1):
         gather.step(s, between)
         gather.pass_on(s - 1)
         tasks += pick_x(s - 1)
+    final = pick_x(half)
+    while len(tasks) > 4:
+        tasks.pop(0)()
     gather.pass_on(half)
-    tasks += pick_x(half)
-    while tasks:
-        tasks.pop(0)()
+    tasks.pop(0)()
+    tasks.pop(0)()
+    final.pop(0)()
+    for task in tasks + final:
+        task()
     gather.end()
-    y_stream.end()
     x_stream.end()
 
 
-def gather_tokens(x, y, small, router, own, cid):
-    n, tokens, model = y.shape
-    both = x.shape[0] // 2
-    quarter = x.shape[0]
-    picked = jax.ShapeDtypeStruct((own, n, CAP, model), BF)
+def gather_tokens(x, position, small, weights, cot, units, cid):
+    n, own, tokens = position.shape
+    quarter, model = x.shape
+    both = quarter // 2
     return pl.pallas_call(
-        partial(token_gather_kernel, n, both, own),
+        partial(token_gather_kernel, n, both, own, units),
         out_shape=[
             jax.ShapeDtypeStruct((n, 4) + x.shape, x.dtype),
-            picked,
-            picked,
-            jax.ShapeDtypeStruct((n, own, tokens), F32),
+            jax.ShapeDtypeStruct((own, n, CAP, model), BF),
             jax.ShapeDtypeStruct((n, tokens, LANES), F32),
             jax.ShapeDtypeStruct((own, n, CAP, LANES), F32),
+            jax.ShapeDtypeStruct((tokens, model), BF),
+            jax.ShapeDtypeStruct((tokens, units), BF),
+            jax.ShapeDtypeStruct((tokens, 2 * units), BF),
+            jax.ShapeDtypeStruct((tokens, model), F32),
+            jax.ShapeDtypeStruct((tokens, model), F32),
         ],
-        in_specs=[ANY, ANY, VM, VM],
-        out_specs=[ANY, ANY, ANY, VM, VM, VM],
+        in_specs=[ANY, VM, VM, VM, VM],
+        out_specs=[ANY, ANY] + [VM] * 7,
         scratch_shapes=[
-            pltpu.VMEM((tokens, tokens), BF),
-            pltpu.VMEM((2, tokens, model), BF),
+            pltpu.VMEM((3, 4, quarter, model), BF),
             pltpu.VMEM((2, own, CAP, model), BF),
-            pltpu.VMEM((2, 4, quarter, model), BF),
-            pltpu.VMEM((2, own, CAP, model), BF),
-            pltpu.SemaphoreType.DMA((4, 2)),
+            pltpu.VMEM((tokens, 2 * units), F32),
+            pltpu.SemaphoreType.DMA((2, 3)),
         ]
         + TokenGather.scratch(n, quarter, both),
         compiler_params=pltpu.CompilerParams(
             collective_id=cid, has_side_effects=True, vmem_limit_bytes=56 * 1024 * 1024
         ),
-    )(x, y, small, router)
+    )(x, position, small, weights, cot)
+
+
+def slots_kernel(own, y, small, y_rows, position, earlier):
+    work = SlotWork(own, small, position)
+    work.count_with(earlier)
+    work.place(0)
+    y_rows[...] = dot(work.pick(0), y[0]).astype(BF).reshape(y_rows.shape)
+
+
+def slots_of(y, small, own):
+    n, tokens, model = y.shape
+    return pl.pallas_call(
+        partial(slots_kernel, own),
+        grid=(n,),
+        out_shape=[
+            jax.ShapeDtypeStruct((own, n, CAP, model), BF),
+            jax.ShapeDtypeStruct((n, own, tokens), F32),
+        ],
+        in_specs=[token_spec(tokens, model), token_spec(small.shape[1], small.shape[2])],
+        out_specs=[slot_spec(own, model), token_spec(own, tokens)],
+        scratch_shapes=[pltpu.VMEM((tokens, tokens), BF)],
+        compiler_params=BIG,
+    )(y, small)
 
 
 def first_kernel(n, k, *refs):
@@ -805,13 +863,14 @@
 
 def first_gather(arrays, x, cid):
     n, k = lax.axis_size("dp"), len(arrays)
+    rows, cols = x.shape[0] // 4, x.shape[1]
     return pl.pallas_call(
         partial(first_kernel, n, k),
         out_shape=[jax.ShapeDtypeStruct((n,) + a.shape, a.dtype) for a in arrays]
-        + [jax.ShapeDtypeStruct((n, 4) + x.shape, x.dtype)],
+        + [jax.ShapeDtypeStruct((n, 4, rows, cols), x.dtype)],
         in_specs=[ANY] * (k + 1),
         out_specs=[ANY] * (k + 1),
-        scratch_shapes=RingGather.scratch(n, arrays) + TokenGather.scratch(n, x.shape[0], 0),
+        scratch_shapes=RingGather.scratch(n, arrays) + TokenGather.scratch(n, rows, 0),
         compiler_params=pltpu.CompilerParams(collective_id=cid, has_side_effects=True),
     )(*arrays, x)
 
@@ -1048,6 +1107,278 @@
     return out
 
 
+def put_scatter_kernel(
+    n,
+    own,
+    position,
+    slot_a,
+    slot_b,
+    slot_c,
+    shared_a,
+    shared_b,
+    out,
+    from_core,
+    made,
+    in_a,
+    in_b,
+    in_c,
+    slots,
+    loads,
+    far_loads,
+    from_chip,
+    to_chip,
+    first,
+    done,
+    last_buf,
+    slot_sem,
+    load_sem,
+    far_sem,
+    core_send,
+    core_recv,
+    chip_send,
+    chip_recv,
+    send_sem,
+    recv_sem,
+    last_send,
+    last_recv,
+):
+    m = lax.axis_index("mp")
+    c, y = m % 2, m // 2
+    core, chip = mp_partners(m)
+    far = (m + 2) % 4
+    beside = m + 1 - 2 * c
+    p, nxt, prv = ring_neighbours(n)
+    rows = out.shape[0]
+    model = shared_a.shape[1]
+    half, steps = rows // 2, n // 2
+
+    def block_of(i):
+        s = (i + 1) // 2
+        return ring_device(n, (p + steps - s) % n if i % 2 or i == 0 else (p + n - steps + s) % n)
+
+    over, sent, loading, chips, arriving = {}, [], {}, {}, {}
+    loaded, summed = set(), set()
+    upper, lower, whole = pl.ds(half, half), pl.ds(0, half), pl.ds(0, rows)
+
+    def slot_load(i):
+        if i >= n:
+            return
+        arriving[i] = []
+        for k, (source, target) in enumerate(((slot_a, in_a), (slot_b, in_b), (slot_c, in_c))):
+            copy = pltpu.make_async_copy(source.at[:, block_of(i)], target.at[i % 2], slot_sem.at[i % 2, k])
+            copy.start()
+            arriving[i].append(copy)
+
+    def make(i):
+        if i >= n:
+            return
+        slot_load(i + 1)
+        if i >= 4:
+            for k in range(3):
+                over[i - 4, k].wait_send()
+        pick = pick_matrix(position[block_of(i)], own)
+        for copy in arriving[i]:
+            copy.wait()
+        start = 0
+        for target, shared in ((in_a, shared_a), (in_b, shared_b), (in_c, None)):
+            cols = target.shape[3]
+            total = dot(pick, target[i % 2].reshape(own * CAP, cols), ((0,), (0,)))
+            if i == n - 1 and shared is not None:
+                total = total + shared[...]
+            made[i % 4, :, :, start : start + cols] = total.astype(BF).reshape(4, rows, cols)
+            start += cols
+
+    def core_sends(i):
+        if i >= n:
+            return
+        block = block_of(i)
+        moves = [((beside + 2) % 4, 1 - y, upper), (beside, y, whole), ((beside + 2) % 4, 1 - y, lower)]
+        for k, (theirs, piece, part) in enumerate(moves):
+            copy = remote(
+                made.at[i % 4, theirs, part],
+                from_core.at[block, piece, part],
+                core_send.at[i, k],
+                core_recv.at[i, k],
+                core,
+            )
+            copy.start()
+            over[i, k] = copy
+            if i >= n - 4:
+                sent.append(copy)
+
+    def load(i):
+        if i >= n:
+            return
+        block = block_of(i)
+        loading[i] = []
+        for k, (piece, part, at) in enumerate(((y, whole, 0), (1 - y, lower, rows))):
+            over[i, k + 1].wait_recv()
+            copy = pltpu.make_async_copy(
+                from_core.at[block, piece, part],
+                loads.at[i % 4, pl.ds(at, rows if k == 0 else half)],
+                load_sem.at[i % 4, k],
+            )
+            copy.start()
+            loading[i].append(copy)
+
+    def to_other_chip(i):
+        if i >= n:
+            return
+        over[i, 0].wait_recv()
+        copy = pltpu.make_async_copy(
+            from_core.at[block_of(i), 1 - y, upper], far_loads.at[i % 2], far_sem.at[i % 2]
+        )
+        copy.start()
+        load(i)
+        if i > 1:
+            chips[i - 2].wait_send()
+        copy.wait()
+        add_rows(to_chip.at[i % 2], [far_loads.at[i % 2], made.at[i % 4, far, upper]], half, BF)
+        copy = remote(to_chip.at[i % 2], from_chip.at[i], chip_send.at[i], chip_recv.at[i], chip)
+        copy.start()
+        chips[i] = copy
+
+    chunks = chunk_rows(0, rows + half)
+    order = [k for k in range(len(chunks)) if chunks[k][0] >= rows]
+    order += [k for k in range(len(chunks)) if chunks[k][0] < rows]
+
+    def pieces_of(i, k):
+        start, size = chunks[k]
+        area = pl.ds(start, size)
+        if i not in loaded:
+            loaded.add(i)
+            for copy in loading[i]:
+                copy.wait()
+        found = [loads.at[i % 4, area]]
+        if start < rows:
+            found.append(made.at[i % 4, m, area])
+        else:
+            found.append(made.at[i % 4, far, pl.ds(start - rows, size)])
+        if half <= start < rows:
+            if i not in summed:
+                summed.add(i)
+                chips[i].wait_recv()
+            found.append(from_chip.at[i, pl.ds(start - half, size)])
+        return found
+
+    slot_load(0)
+    make(0)
+    greet([core, chip, nxt, prv])
+    core_sends(0)
+    make(1)
+    core_sends(1)
+    to_other_chip(0)
+    ring = {}
+    for s in range(steps):
+        for k, way in [(k, way) for k in order for way in range(2) if s > 0 or k % 2 == way]:
+            start, size = chunks[k]
+            area = pl.ds(start, size)
+            if s == 0:
+                if start == half:
+                    make(2)
+                    core_sends(2)
+                target, pieces = first.at[area], pieces_of(0, k)
+            else:
+                target, pieces = slots.at[s - 1, way, area], pieces_of(2 * s - 1 + way, k)
+                if (s - 1, k, way) in ring:
+                    ring[s - 1, k, way].wait_recv()
+                    pieces.append(target)
+            add_rows(target, pieces, size, BF)
+            copy = remote(
+                target,
+                slots.at[s, way, area],
+                send_sem.at[s, k, way],
+                recv_sem.at[s, k, way],
+                nxt if way == 0 else prv,
+            )
+            copy.start()
+            ring[s, k, way] = copy
+        if s == 0:
+            to_other_chip(1)
+            to_other_chip(2)
+        for i in (2 * s + 3, 2 * s + 4):
+            make(i)
+            core_sends(i)
+        for i in (2 * s + 3, 2 * s + 4):
+            to_other_chip(i)
+    last = []
+    for k in order:
+        start, size = chunks[k]
+        area = pl.ds(start, size)
+        pieces = pieces_of(n - 1, k)
+        for way in range(2):
+            ring[steps - 1, k, way].wait_recv()
+            pieces.append(slots.at[steps - 1, way, area])
+        if start < rows:
+            add_rows(out.at[area], pieces, size, F32)
+            continue
+        at = pl.ds(start - rows, size)
+        add_rows(done.at[at], pieces, size, BF)
+        copy = remote(done.at[at], last_buf.at[at], last_send.at[k], last_recv.at[k], chip)
+        copy.start()
+        last.append(copy)
+    for copy in last:
+        copy.wait_recv()
+    add_rows(out.at[lower], [out.at[lower], last_buf], half, F32)
+    for copy in sent + list(ring.values()) + last + [chips[n - 2], chips[n - 1]]:
+        copy.wait_send()
+
+
+def put_scatter(position, rows_a, rows_b, rows_c, shared_a, shared_b, cid):
+    n, own, tokens = position.shape
+    model = shared_a.shape[1]
+    quarter = tokens // 4
+    cols = 2 * model + LANES
+    half, steps = quarter // 2, n // 2
+    count = len(chunk_rows(0, quarter + half))
+    dma = pltpu.SemaphoreType.DMA
+    out, _ = pl.pallas_call(
+        partial(put_scatter_kernel, n, own),
+        out_shape=[
+            jax.ShapeDtypeStruct((quarter, cols), F32),
+            jax.ShapeDtypeStruct((n, 2, quarter, cols), BF),
+        ],
+        in_specs=[VM, ANY, ANY, ANY, VM, VM],
+        out_specs=[VM, ANY],
+        scratch_shapes=[
+            pltpu.VMEM((4, 4, quarter, cols), BF),
+            pltpu.VMEM((2, own, CAP, model), BF),
+            pltpu.VMEM((2, own, CAP, model), BF),
+            pltpu.VMEM((2, own, CAP, LANES), BF),
+            pltpu.VMEM((steps, 2, quarter + half, cols), BF),
+            pltpu.VMEM((4, quarter + half, cols), BF),
+            pltpu.VMEM((2, half, cols), BF),
+            pltpu.VMEM((n, half, cols), BF),
+            pltpu.VMEM((2, half, cols), BF),
+            pltpu.VMEM((quarter + half, cols), BF),
+            pltpu.VMEM((half, cols), BF),
+            pltpu.VMEM((half, cols), BF),
+            dma((2, 3)),
+            dma((4, 2)),
+            dma((2,)),
+            dma((n, 3)),
+            dma((n, 3)),
+            dma((n,)),
+            dma((n,)),
+            dma((steps, count, 2)),
+            dma((steps, count, 2)),
+            dma((count,)),
+            dma((count,)),
+        ],
+        compiler_params=pltpu.CompilerParams(
+            collective_id=cid, has_side_effects=True, vmem_limit_bytes=60 * 1024 * 1024
+        ),
+    )(
+        position,
+        rows_a.reshape(own, n, CAP, model),
+        rows_b.reshape(own, n, CAP, model),
+        rows_c.reshape(own, n, CAP, LANES),
+        shared_a,
+        shared_b,
+    )
+    return out
+
+
 def edge_kernel(n, part, slope, rim, total, ahead, mine, from_core, from_chip, edge, send_sem, recv_sem):
     d, m = lax.axis_index("dp"), lax.axis_index("mp")
     core, chip = mp_partners(m)
@@ -1363,22 +1694,35 @@
     )(v, b, c, cumul, cumul_t, step_t, step, entry, tail_bare, seg_col, seg_row, expand, skip, kept, dy, start)
 
 
-def state_scan_kernel(
-    n,
-    reverse,
-    mine,
-    decay,
-    expand,
-    out,
-    first,
-    second,
-    got_first,
-    got_second,
-    half,
-    got_half,
-    send_sem,
-    recv_sem,
-):
+def state_scan_kernel(n, own, *refs):
+    reverse = own == 0
+    if reverse:
+        mine, decay, expand, out = refs[:4]
+        refs = refs[4:]
+    else:
+        mine, decay, expand, y, small, out, y_rows, position = refs[:8]
+        refs = refs[8:]
+    first, second, got_first, got_second, half, got_half, send_sem, recv_sem = refs[:8]
+
+    def work(blocks):
+        pass
+
+    if not reverse:
+        earlier, y_in, y_out, stream_sem = refs[8:]
+        slots = SlotWork(own, small, position)
+        stream = RowStream(y, y_rows, y_in, y_out, stream_sem.at[0], stream_sem.at[1])
+        stream.load(0)
+
+        def work(blocks):
+            for b in blocks:
+                if b + 1 < n:
+                    stream.load(b + 1)
+                if b == 0:
+                    slots.count_with(earlier)
+                    for block in range(n):
+                        slots.place(block)
+                stream.give(b, b, dot(slots.pick(b), stream.take(b)))
+
     d = lax.axis_index("dp")
     q = n - 1 - d if reverse else d
     zq, xq = q // 2, q % 2
@@ -1423,12 +1767,13 @@
     greet([beside] + others)
     one = remote(first, got_first, send_sem.at[0], recv_sem.at[0], beside)
     one.start()
+    work(range(0, 2))
     one.wait_recv()
-    own = mine[own_rows, :]
+    own_part = mine[own_rows, :]
     got, got_decay = got_first[body, :].astype(F32), one_term(got_first[tail, :])
-    early = own * (1.0 - xf) + got * xf
+    early = own_part * (1.0 - xf) + got * xf
     early_decay = own_decay * (1.0 - xf) + got_decay * xf
-    late = own * xf + got * (1.0 - xf)
+    late = own_part * xf + got * (1.0 - xf)
     late_decay = own_decay * xf + got_decay * (1.0 - xf)
     second[body, :] = (spread(late_decay) * early + late).astype(sent_type)
     second[tail, :] = two_terms(early_decay * late_decay)
@@ -1444,6 +1789,7 @@
             copy.start()
 
     early_spread = spread(early_decay)
+    work(range(2, n - 1))
     total = jnp.zeros((rows, LANES), F32)
     for k in range(depth - 1, 0, -1):
 
@@ -1458,6 +1804,7 @@
     last = remote(half, got_half, send_sem.at[depth], recv_sem.at[depth], beside)
     last.start()
     out[own_rows, :] = total * (1.0 - xf) + after * xf
+    work(range(n - 1, n))
     last.wait_recv()
     out[other_rows, :] = got_half[...].astype(F32)
     one.wait_send()
@@ -1468,17 +1815,37 @@
         def _():
             sent[k - 1].wait_send()
 
-
-def state_scan(mine, decay, expand, reverse, cid, sent_type):
+    if not reverse:
+        stream.end()
+
+
+def state_scan(mine, decay, expand, cid, sent_type, y=None, small=None, own=0):
     n = lax.axis_size("dp")
     half = mine.shape[0] // 2
     depth = n // 2
     message = (half + 16, LANES)
+    out_shape, out_specs = [jax.ShapeDtypeStruct(mine.shape, F32)], [VM]
+    args, in_specs, more = [mine, decay, expand], [VM] * 3, []
+    if own:
+        tokens, model = y.shape[1:]
+        args += [y, small]
+        in_specs += [ANY, VM]
+        out_shape += [
+            jax.ShapeDtypeStruct((own, n, CAP, model), BF),
+            jax.ShapeDtypeStruct((n, own, tokens), F32),
+        ]
+        out_specs += [ANY, VM]
+        more = [
+            pltpu.VMEM((tokens, tokens), BF),
+            pltpu.VMEM((2, tokens, model), BF),
+            pltpu.VMEM((2, own, CAP, model), BF),
+            pltpu.SemaphoreType.DMA((2, 2)),
+        ]
     return pl.pallas_call(
-        partial(state_scan_kernel, n, reverse),
-        out_shape=jax.ShapeDtypeStruct(mine.shape, F32),
-        in_specs=[VM] * 3,
-        out_specs=VM,
+        partial(state_scan_kernel, n, own),
+        out_shape=out_shape,
+        in_specs=in_specs,
+        out_specs=out_specs,
         scratch_shapes=[
             pltpu.VMEM(message, sent_type),
             pltpu.VMEM(message, sent_type),
@@ -1488,11 +1855,12 @@
             pltpu.VMEM((half, LANES), sent_type),
             pltpu.SemaphoreType.DMA((depth + 1,)),
             pltpu.SemaphoreType.DMA((depth + 1,)),
-        ],
+        ]
+        + more,
         compiler_params=pltpu.CompilerParams(
-            collective_id=cid, has_side_effects=True, vmem_limit_bytes=32 * 1024 * 1024
+            collective_id=cid, has_side_effects=True, vmem_limit_bytes=48 * 1024 * 1024
         ),
-    )(mine, decay, expand)
+    )(*args)
 
 
 def pick_matrix(position, own):
@@ -1516,7 +1884,7 @@
 
 
 def expert_kernel(
-    own, rows, cot_rows, gate, w_in, w_out, grad_in, grad_out, d_rows, res, dots, wide, both
+    own, parts, rows, cot_rows, gate, w_in, w_out, grad_in, grad_out, d_rows, res, dots, wide, both
 ):
     e, part = pl.program_id(0), pl.program_id(1)
     model = rows.shape[2]
@@ -1527,8 +1895,9 @@
         wide[...] = w_in[0].astype(F32)
         both[:, 0:units] = wide[pl.ds(0, model, stride=2), :].astype(BF)
         both[:, units : 2 * units] = wide[pl.ds(1, model, stride=2), :].astype(BF)
-        grad_in[...] = jnp.zeros_like(grad_in)
-        grad_out[...] = jnp.zeros_like(grad_out)
+        if parts > 1:
+            grad_in[...] = jnp.zeros_like(grad_in)
+            grad_out[...] = jnp.zeros_like(grad_out)
 
     x, c, g = rows[0], cot_rows[0], gate[0]
     mid = dot(x, both[...])
@@ -1545,9 +1914,15 @@
     d_gate = (d_act * mid_up * (sig * (1.0 + mid_gate * (1.0 - sig)))).astype(BF)
     d_mid = jnp.concatenate([d_gate, (d_act * mid_silu).astype(BF)], axis=1)
     grads = dot(x, d_mid, ((0,), (0,)))
-    grad_in[0, pl.ds(0, model, stride=2), :] += grads[:, 0:units]
-    grad_in[0, pl.ds(1, model, stride=2), :] += grads[:, units : 2 * units]
-    grad_out[0] += dot(gated, c, ((0,), (0,)))
+    grads_down = dot(gated, c, ((0,), (0,)))
+    if parts > 1:
+        grad_in[0, pl.ds(0, model, stride=2), :] += grads[:, 0:units]
+        grad_in[0, pl.ds(1, model, stride=2), :] += grads[:, units : 2 * units]
+        grad_out[0] += grads_down
+    else:
+        grad_in[0, pl.ds(0, model, stride=2), :] = grads[:, 0:units]
+        grad_in[0, pl.ds(1, model, stride=2), :] = grads[:, units : 2 * units]
+        grad_out[0] = grads_down
     d_rows[0] = dot(d_mid, both[...], ((1,), (1,))).astype(BF)
     res[0] = dot(gated, w_out[0]).astype(BF)
 
@@ -1564,7 +1939,7 @@
         return pl.BlockSpec((1, a, b), lambda e, j: (e, 0, 0))
 
     return pl.pallas_call(
-        partial(expert_kernel, own),
+        partial(expert_kernel, own, slots // part),
         grid=(own, slots // part),
         out_shape=[
             jax.ShapeDtypeStruct((own, 2 * model, units), F32),
@@ -1631,7 +2006,7 @@
 
 def weight_grads(pairs):
     k = len(pairs)
-    tokens, model = pairs[0][0].shape
+    tokens, model = pairs[1][0].shape
     block = 256
     cols = sum(right.shape[1] for _, right in pairs)
     return pl.pallas_call(
@@ -1658,11 +2033,7 @@
     return state
 
 
-def incoming_state(mine, decay, expand, reverse, cid):
-    if lax.axis_size("dp") == 8:
-        return state_scan(
-            mine, jnp.broadcast_to(decay, (8, LANES)), expand, reverse, cid, BF if reverse else F32
-        )
+def ring_state(mine, decay, expand, reverse, cid):
     rows = jnp.pad(decay, ((0, 31), (0, 0)))
     (gathered,) = gather_dp([jnp.concatenate([mine, rows], axis=0)], cid)
     width = mine.shape[0]
@@ -1741,14 +2112,12 @@
         axis=1,
     )
     mine_cot = lax.dynamic_slice_in_dim(cotangent, mp_place * quarter, quarter, 0)
-    weight_a, small_all, cot_all = first_gather([pack_a, small], mine_cot, 0)
+    weight_a, small_all, cot_all = first_gather([pack_a, small], cotangent, 0)
     weight_a = weight_a.reshape(model, -1)
     cot_all = cot_all.reshape(n, tokens, model)
     pack_b, small_all = lax.optimization_barrier((pack_b, small_all))
     weight_b = lax.all_gather(pack_b, "dp", axis=0, tiled=True)
     out_t = weight_b[:, :inner]
-    shared_w = weight_b[:, inner : inner + 2 * hidden_units]
-    shared_out_t = weight_b[:, inner + 2 * hidden_units : inner + 3 * hidden_units]
     router_w = weight_b[:, inner + 3 * hidden_units :]
 
     pieces = []
@@ -1834,7 +2203,13 @@
         values * dot(group_tail, expand, precision=HIGH), write, ((0,), (0,)), HIGH
     )
     group_decay = group_entry[tokens - 1 :]
-    incoming = incoming_state(outgoing, group_decay, expand, False, 1)
+    if n == 8:
+        incoming, cot_rows, position = state_scan(
+            outgoing, jnp.broadcast_to(group_decay, (8, LANES)), expand, 1, F32, cot_all, small_all, own_experts
+        )
+    else:
+        incoming = ring_state(outgoing, group_decay, expand, False, 1)
+        cot_rows, position = slots_of(cot_all, small_all, own_experts)
     ssd, kept = recur_forward(
         values, write, read, cumul, cumul_t, step_t, entry, tail, seg_col, seg_row, expand, skip, incoming
     )
@@ -1856,10 +2231,17 @@
     ffn_mine = (unit_second * gain_second).astype(BF)
 
     first_expert = place * own_experts
-    ffn_all, cot_rows, rows, position, gates, slot_gates = gather_tokens(
-        ffn_mine, cot_all, small_all, router_w, own_experts, 3
-    )
-    ffn_all = ffn_all.reshape(n, tokens, model)
+    (
+        _,
+        rows,
+        gates,
+        slot_gates,
+        ffn_block,
+        shared_act,
+        d_shared_mid,
+        shared_res,
+        d_ffn_shared,
+    ) = gather_tokens(ffn_mine, position, small_all, weight_b, cotangent, hidden_units, 3)
 
     slots = n * CAP
     grad_in_rows, grad_expert_out, d_rows, expert_res, slot_dots = run_experts(
@@ -1871,18 +2253,6 @@
     )
     grad_expert_in = grad_in_rows.reshape(expert_in.shape)
 
-    ffn_block = lax.dynamic_index_in_dim(ffn_all, place, 0, False)
-    shared_mid = dot(ffn_block, shared_w)
-    shared_gate, shared_up = shared_mid[:, :hidden_units], shared_mid[:, hidden_units:]
-    shared_silu = jax.nn.silu(shared_gate)
-    shared_act = (shared_silu * shared_up).astype(BF)
-    shared_res = dot(shared_act, shared_out_t, ((1,), (1,)))
-    d_shared_act = dot(cotangent, shared_out_t)
-    d_shared_mid = jnp.concatenate(
-        [d_shared_act * shared_up * silu_slope(shared_gate), d_shared_act * shared_silu], axis=1
-    ).astype(BF)
-    d_ffn_shared = dot(d_shared_mid, shared_w, ((1,), (1,)))
-
     if n > 8:
         d_ffn_pack = put_rows(position, [(d_rows, d_ffn_shared)], slot_dots)
         d_ffn_sum = scatter_tokens(d_ffn_pack.reshape(n, 4, quarter, -1), 4)
@@ -1890,8 +2260,7 @@
         res_pack = put_rows(position, [(expert_res, shared_res)])
         res_sum = scatter_tokens(res_pack.reshape(n, 4, quarter, model), 10)
     else:
-        pack = put_rows(position, [(expert_res, shared_res), (d_rows, d_ffn_shared)], slot_dots)
-        both_sums = scatter_tokens(pack.reshape(n, 4, quarter, -1), 4)
+        both_sums = put_scatter(position, expert_res, d_rows, slot_dots, shared_res, d_ffn_shared, 4)
         res_sum, d_ffn_sum = both_sums[:, :model], both_sums[:, model:]
 
     own_tokens_gates = lax.dynamic_slice(
@@ -1933,13 +2302,14 @@
     rows0 = ((0,), (0,))
     grad_b = weight_grads(
         [
-            (d_proj, scaled),
+            (got, scaled),
             (ffn_block, d_shared_mid),
             (cotangent, shared_act),
             (ffn_block, d_logits_all),
         ]
     )
-    grad_b, d_proj = lax.optimization_barrier((grad_b, d_proj))
+    grad_b, got = lax.optimization_barrier((grad_b, got))
+    d_proj = got[:, :model]
     sum_b = lax.psum_scatter(grad_b, "dp", scatter_dimension=0, tiled=True).astype(F32)
     d_scaled = dot(d_proj, out_t)
     grad_gated_row = jnp.sum(d_scaled * gated, axis=0)
@@ -1948,7 +2318,10 @@
     d_gate_z = d_gated * ssd * silu_slope(gate_z)
 
     direct = dot(d_ssd * dot(group_entry, expand, precision=HIGH), read, rows0, HIGH)
-    state_grad = incoming_state(direct, group_decay, expand, True, 6)
+    if n == 8:
+        (state_grad,) = state_scan(direct, jnp.broadcast_to(group_decay, (8, LANES)), expand, 6, BF)
+    else:
+        state_grad = ring_state(direct, group_decay, expand, True, 6)
     d_values, d_write, d_read, d_step, d_rated, d_skip_row = recur_backward(
         values,
         write,
@@ -2031,7 +2404,7 @@
     )
     gains = jnp.pad(gains, ((0, 0), (0, 16 * LANES - 2 * shard)))
     mine_result = (mixed + res_sum).astype(BF)
-    sum_a, misc_sum, gains_sum, hidden_all, result = last_exchange(
+    sum_zx, sum_state, sum_dt, misc_sum, gains_sum, hidden_all, result = last_exchange(
         grad_a.reshape(n, shard, -1),
         misc_grads.reshape(n, 32, LANES),
         gains.reshape(n, 16, LANES),
@@ -2041,6 +2414,7 @@
         mine_hidden,
         gain_first,
         mine_result,
+        (2 * inner, state_cols, LANES),
         8,
     )
     result = result.reshape(tokens, model)
@@ -2059,9 +2433,9 @@
         result,
         hidden_all.reshape(tokens, model).astype(F32),
         gains_sum[:shard],
-        sum_a[:, : 2 * inner].reshape(shard, 2, inner),
-        sum_a[:, 2 * inner : 2 * inner + state_cols],
-        sum_a[:, 2 * inner + state_cols : 2 * inner + state_cols + heads],
+        sum_zx.reshape(shard, 2, inner),
+        sum_state,
+        sum_dt[:, :heads],
         value_sum[:taps],
         value_sum[taps],
         state_sum[:taps],

time: 788 us -> 750 us (0.952)
  Pallas kernels: 616 us -> 587 us
  matrix products: 51.2 us -> 39.3 us
  waiting for transfers between devices: 2.5 us -> 11.8 us
    pallas_call x7 -> x6, Pallas kernels: 418 us -> 389 us  [the longest x1 129 us: put_scatter(): pl.pallas_call(partial(put_scatter_kernel, n, own), out_shape=[jax.ShapeD...]
    dot_general x18 -> x14, matrix products: 50.8 us -> 38.9 us  [dot(): lax.dot_general(a, b, (dims, ((), ())), precision=precision, preferred_el...]
    all_gather x1, waiting for transfers between devices: 2.46 us -> 11.7 us  [per_device(): weight_b = lax.all_gather(pack_b, 'dp', axis=0, tiled=True)]
    slice x5 -> x0, local copies, waits for them, and re-layouts: 8.41 us -> none  [the longest x1 2.65 us: per_device(): d_proj = got[:, :model]]
  transfers between devices with their start and end apart: 2 -> 2, of which waited for: 1 -> 1; matrix products, arithmetic and copies ran while one was open for 11% -> 12% of each run, Pallas kernels for 25% -> 26%
where the time goes in v1:
time: 750 us; the launch traced here: 745 us
  Pallas kernels  587 us (78%)
  local copies, waits for them, and re-layouts  51 us (7%)
  other arithmetic  39.7 us (5%)
  matrix products  39.3 us (5%)
  between operations  16 us (2%)
  waiting for transfers between devices  11.8 us (2%)
    pallas_call x1, Pallas kernels, put_scatter(): pl.pallas_call(partial(put_scatter_kernel, n, own), out_shape=[jax.ShapeD...  129 us
    pallas_call x1, Pallas kernels, first_gather(): pl.pallas_call(partial(first_kernel, n, k), out_shape=[jax.ShapeDtypeStru...  102 us
    pallas_call x1, Pallas kernels, gather_tokens(): pl.pallas_call(partial(token_gather_kernel, n, both, own, units), out_sha...  81.7 us
    pallas_call x1, Pallas kernels, last_exchange(): pl.pallas_call(partial(last_kernel, n), out_shape=[jax.ShapeDtypeStruct((...  73 us
    pallas_call x2, Pallas kernels, state_scan(): pl.pallas_call(partial(state_scan_kernel, n, own), out_shape=out_shape, i...  70.7 us
    dot_general x14, matrix products, dot(): lax.dot_general(a, b, (dims, ((), ())), precision=precision, preferred_el...  38.9 us
    pallas_call x1, Pallas kernels, run_experts(): pl.pallas_call(partial(expert_kernel, own, slots // part), grid=(own, slo...  33.7 us
    pallas_call x1, Pallas kernels, recur_backward(): pl.pallas_call(partial(adjoint_kernel, width // LANES), grid=(blocks,), o...  24.1 us
  transfers between devices with their start and end apart: 2, of which 1 were waited for; matrix products, arithmetic and copies ran while one was open for 12% of the time, Pallas kernels for 26%

profile of v1, /device:TPU:0, one launch (start us, length us, event | category | flops | bytes accessed | tf_op | source)
XLA Modules:
  0.0 745.1 jit_solution(17922675145110470672)
XLA Ops:
  9.9 1.1 copy.98
  15.8 2.1 concatenate.73
  17.9 1.8 fusion.31.refs_0_
  20.3 101.6 %shard_map.348 = (bf16[8,192,1920]{2,1,0:T(8,128)(2,1)}, bf16[8,16,1536]{2,1,0:T(8,128)(2,1)}, bf16[8,4,128,1536]{3,2,1,0:T(8,128)(2,1)}) custom-call(bf16[192,1920]{1,0:T(8,128)(2,1)} %fusion.31.refs_0_, bf16[16,1536]{1,0:T(8,128)(2,1)} %fusion.61.refs_1_, bf16[512,1536]{1,0:T(8,128)(2,1)} %refs_2_.3), custom_call_target="tpu_custom_call" | custom-call | tf_op jit(solution)/shard_map/pallas_call | solution.py:867
  131.2 2.0 fusion.71
  133.7 6.4 fusion.102
  140.2 3.2 add_multiply_fusion
  144.0 1.5 slice.528.values
  148.7 2.6 fusion.25.refs_0_
  151.3 37.8 %shard_map.349 = (f32[768,128]{1,0:T(8,128)S(1)}, bf16[8,8,64,1536]{3,2,1,0:T(8,128)(2,1)}, f32[8,8,512]{2,1,0:T(8,128)S(1)}) custom-call(f32[768,128]{1,0:T(8,128)S(1)} %fusion.25.refs_0_, f32[8,128]{1,0:T(8,128)S(1)} %broadcast_in_dim.102.refs_1_, f32[128,768]{1,0:T(8,128)S(1)} %fusion.39.refs_2_.expand, bf16[8,512,1536]{2,1,0:T(8,128)(2,1)} %bitcast.165, ...), custom_call_target="tpu_custom_call" | custom-call | tf_op jit(solution)/shard_map/pallas_call | solution.py:1844
  189.4 10.0 %shard_map.350 = (f32[512,768]{1,0:T(8,128)S(1)}, f32[4,768,128]{2,1,0:T(8,128)S(1)}) custom-call(f32[512,768]{1,0:T(8,128)} %slice.528.values, f32[512,128]{1,0:T(8,128)S(1)} %get-tuple-element.213.write, f32[512,128]{1,0:T(8,128)S(1)} %get-tuple-element.212.read, f32[512,128]{1,0:T(8,128)S(1)} %bitcast.160, f32[16,512]{1,0:T(8,128)S(1)} %copy.80.cumul_t, ...), custom_call_target="tpu_custom_call" | custom-call | tf_op jit(solution)/shard_map/pallas_call | solution.py:1528
  199.4 3.0 multiply_convert_fusion.2
  202.5 1.1 copy-done.19
  203.8 11.7 %all-gather.2.cloned.1.call-done.weights = bf16[1536,1664]{1,0:T(8,128)(2,1)} async-done(((bf16[192,1664]{1,0:T(8,128)(2,1)}), bf16[1536,1664]{1,0:T(8,128)(2,1)}) %all-gather.2.cloned.1.call-update) | async-done | bytes 5111824 | tf_op jit(solution)/shard_map/all_gather | solution.py:2119
  215.5 3.1 fusion.12
  219.0 23.1 %shard_map.351 = f32[128,1664]{1,0:T(8,128)S(1)} custom-call(f32[4,128,1664]{2,1,0:T(8,128)S(1)} %bitcast.156), custom_call_target="tpu_custom_call" | custom-call | tf_op jit(solution)/shard_map/pallas_call | solution.py:414
  242.2 1.3 multiply_reduce_fusion.12
  245.3 81.7 %shard_map.352 = (bf16[8,4,128,1536]{3,2,1,0:T(8,128)(2,1)}, bf16[8,8,64,1536]{3,2,1,0:T(8,128)(2,1)}, f32[8,512,128]{2,1,0:T(8,128)}, f32[8,8,64,128]{3,2,1,0:T...) custom-call(bf16[128,1536]{1,0:T(8,128)(2,1)} %multiply_convert_fusi, ...), custom_call_target="tpu_custom_call" | custom-call | tf_op jit(solution)/shard_map/pallas_call | solution.py:795
  327.0 33.7 %shard_map.353 = (f32[8,3072,128]{2,1,0:T(8,128)}, f32[8,128,1536]{2,1,0:T(8,128)}, bf16[8,512,1536]{2,1,0:T(8,128)(2,1)}, bf16[8,512,1536]{2,1,0:T(8,128)(2,1)}, bf16[8,512,128]{2,1,0:T(8,128)(2,1)}) custom-call(bf16[8,512,1536]{2,1,0:T(8,128)(2,1)} %bitcast.167, bf16[8,512,1536]{2,1,0:T(8,128)(2,1)} %bitcast.166, f32[8,512,128]{2,1,0:T(8,128)} %bitcast.178, ...), custom_call_target="tpu_custom_call" | custom-call | tf_op jit(solution)/shard_map/pallas_call | solution.py:1941
  360.7 129.5 %shard_map.354 = (f32[128,3200]{1,0:T(8,128)}, bf16[8,2,128,3200]{3,2,1,0:T(8,128)(2,1)}) custom-call(f32[8,8,512]{2,1,0:T(8,128)} %copy-done.4, bf16[8,8,64,1536]{3,2,1,0:T(8,128)(2,1)} %bitcast.169, bf16[8,8,64,1536]{3,2,1,0:T(8,128)(2,1)} %bitcast.168, bf16[8,8,64,128]{3,2,1,0:T(8,128)(2,1)} %bitcast.182, f32[512,1536]{1,0:T(8,128)} %get-tuple-element.74.shared_a, ...), custom_call_target="tpu_custom_call" | custom-call | tf_op jit(solution)/shard_map/pallas_call | solution.py:1335
  492.2 3.5 multiply_reduce_fusion.8
  495.7 1.4 multiply_reduce_fusion.10
  499.7 1.9 concatenate.83.refs_0_
  501.5 15.2 %shard_map.355 = bf16[4,128,1664]{2,1,0:T(8,128)(2,1)} custom-call(bf16[128,1664]{1,0:T(8,128)(2,1)} %concatenate.83.refs_0_), custom_call_target="tpu_custom_call" | custom-call | tf_op jit(solution)/shard_map/pallas_call | solution.py:465
  518.3 8.7 %shard_map.356 = bf16[1536,1664]{1,0:T(8,128)(2,1)} custom-call(bf16[512,1664]{1,0:T(8,128)(2,1)} %bitcast.171, bf16[512,1536]{1,0:T(8,128)(2,1)} %get-tuple-element.78.refs_1_.refs_3_, bf16[512,1536]{1,0:T(8,128)(2,1)} %refs_2_.3, bf16[512,1536]{1,0:T(8,128)(2,1)} %get-tuple-element.78.refs_1_.refs_3_, bf16[512,768]{1,0:T(8,128)(2,1)} %copy-done.20, ...), custom_call_target="tpu_custom_call" | custom-call | tf_op jit(solution)/shard_map/pallas_call | solution.py:2012
  529.3 2.0 dynamic-slice_convert_fusion.hidden
  532.2 2.1 maximum_convert_fusion
  534.3 1.4 multiply_reduce_fusion.14
  535.7 5.4 multiply_convert_fusion.1
  541.2 3.7 fusion.21.refs_0_
  544.9 32.9 %shard_map.357.start = f32[768,128]{1,0:T(8,128)S(1)} custom-call(f32[768,128]{1,0:T(8,128)S(1)} %fusion.21.refs_0_, f32[8,128]{1,0:T(8,128)S(1)} %broadcast_in_dim.102.refs_1_, f32[128,768]{1,0:T(8,128)S(1)} %fusion.39.refs_2_.expand), custom_call_target="tpu_custom_call" | custom-call | tf_op jit(solution)/shard_map/pallas_call | solution.py:1844
  577.8 24.1 %shard_map.358 = (f32[512,768]{1,0:T(8,128)S(1)}, f32[512,128]{1,0:T(8,128)S(1)}, f32[512,128]{1,0:T(8,128)S(1)}, f32[512,128]{1,0:T(8,128)S(1)}, f32[512,128]{1,0:T(8,128)S(1)}, /*index=5*/f32[1,768]{1,0:T(1,128)S(1)}) custom-call(f32[512,768]{1,0:T(8,128)} %slice.528.values, f32[512,128]{1,0:T(8,128)S(1)} %get-tuple-element.213.write, ...), custom_call_target="tpu_custom_call" | custom-call | tf_op jit(solution)/shard_map/pallas_call | solution.py:1655
  602.3 15.7 %shard_map.359 = (f32[512,256]{1,0:T(8,128)S(1)}, f32[16,1024]{1,0:T(8,128)S(1)}) custom-call(f32[512,256]{1,0:T(8,128)S(1)} %pad_maximum_fusion.5.part, f32[16,256]{1,0:T(8,128)S(1)} %slice.549.slope, f32[16,768]{1,0:T(8,128)S(1)} %slice.550.rim), custom_call_target="tpu_custom_call" | custom-call | tf_op jit(solution)/shard_map/pallas_call | solution.py:1427
  618.1 1.9 multiply_reduce_fusion.2
  621.9 1.3 copy.89
  623.4 1.7 fusion.90
  627.9 1.5 fusion.5
  630.4 2.6 fusion
  633.1 1.9 multiply_reduce_fusion.1
  635.0 1.3 multiply_reduce_fusion.9
  637.1 6.4 convolution_convert_fusion
  643.5 73.0 %shard_map.360 = (f32[192,1536]{1,0:T(8,128)}, f32[192,256]{1,0:T(8,128)}, f32[192,128]{1,0:T(8,128)}, f32[32,128]{1,0:T(8,128)}, f32[16,128]{1,0:T(8,128)}, /*i...) custom-call(bf16[8,192,1920]{2,1,0:T(8,128)(2,1)} %bitcast.176, f32[8,32,128]{2,1,0:T(8,128)} %bitcast.186, ...), custom_call_target="tpu_custom_call" | custom-call | tf_op jit(solution)/shard_map/pallas_call | solution.py:358
  718.1 1.3 slice.563
  720.1 3.0 reshape.483
  727.9 1.4 fusion.100
  729.3 2.2 bitcast_convert_fusion
  731.4 1.2 convert_element_type.226
  736.0 1.1 copy.121
  (316 shorter events, 50.9 us)
Async XLA Ops:
  7.2 208.3 %all-gather.2.cloned.1.call-start = ((), (), s32[]{:S(2)}) async-start(), calls=%async_computation.1 | async-start | bytes 5750784 | tf_op jit(solution)/shard_map/all_gather | solution.py:2119
  11.0 111.0 %copy-start.32 = (bf16[768,192]{0,1:T(8,128)(2,1)S(1)}, bf16[768,192]{0,1:T(8,128)(2,1)}, u32[]{:S(2)}) copy-start(bf16[768,192]{0,1:T(8,128)(2,1)} %param.34) | copy-start | bytes 884740
  11.0 111.0 %copy-start.34 = (bf16[256,192]{0,1:T(8,128)(2,1)S(1)}, bf16[256,192]{0,1:T(8,128)(2,1)}, u32[]{:S(2)}) copy-start(bf16[256,192]{0,1:T(8,128)(2,1)} %param.38) | copy-start | bytes 294916
  121.9 6.5 copy-start
  122.0 6.7 copy-start.59
  122.0 7.2 copy-start.9
  122.9 608.5 %reduce-scatter.2.cloned.1.call-start = ((), (), s32[]{:S(2)}) async-start(), calls=%async_computation.2 | async-start | bytes 5750784 | tf_op jit(solution)/shard_map/reduce_scatter | solution.py:2313
  124.2 9.5 %copy-start.36 = (f32[8,192]{1,0:T(8,128)}, f32[8,192]{1,0:T(8,128)S(1)}, u32[]{:S(2)}) copy-start(f32[8,192]{1,0:T(8,128)S(1)} %get-tuple-element.185) | copy-start | bytes 18436
  128.4 5.3 copy-start.28
  131.2 8.9 %copy-start.51 = (f32[512]{0:T(512)}, f32[512]{0:T(512)S(1)}, u32[]{:S(2)}) copy-start(f32[512]{0:T(512)S(1)} %get-tuple-element.252) | copy-start | bytes 6148
  131.2 8.9 %copy-start.53 = (f32[512]{0:T(512)}, f32[512]{0:T(512)S(1)}, u32[]{:S(2)}) copy-start(f32[512]{0:T(512)S(1)} %get-tuple-element.253) | copy-start | bytes 6148
  131.2 8.9 %copy-start.49 = (f32[528]{0:T(1024)}, f32[528]{0:T(1024)S(1)}, u32[]{:S(2)}) copy-start(f32[528]{0:T(1024)S(1)} %add_rsqrt_fusion.1) | copy-start | bytes 6340
  133.2 6.9 copy-start.55
  133.2 6.9 copy-start.40
  133.2 6.9 copy-start.42
  133.2 6.9 copy-start.44
  133.2 6.9 copy-start.46
  133.7 6.4 copy-start.24
  140.1 5.4 copy-start.5
  146.6 52.8 %copy-start.57 = (f32[768]{0:T(1024)}, f32[768]{0:T(1024)S(1)}, u32[]{:S(2)}) copy-start(f32[768]{0:T(1024)S(1)} %mul.487) | copy-start | bytes 9220
  146.7 42.4 %copy-start.38 = (s32[768]{0:T(1024)}, s32[768]{0:T(1024)S(1)}, u32[]{:S(2)}) copy-start(s32[768]{0:T(1024)S(1)} %add_select_fusion) | copy-start | bytes 9220
  189.1 10.3 %copy-start.4 = (f32[8,8,512]{2,1,0:T(8,128)}, f32[8,8,512]{2,1,0:T(8,128)S(1)}, u32[]{:S(2)}) copy-start(f32[8,8,512]{2,1,0:T(8,128)S(1)} %get-tuple-element.67.position) | copy-start | bytes 393220
  199.4 3.0 copy-start.1
  199.4 3.0 copy-start.2
  202.5 16.1 %copy-start.20 = (bf16[512,768]{1,0:T(8,128)(2,1)}, bf16[512,768]{1,0:T(8,128)(2,1)S(1)}, u32[]{:S(2)}) copy-start(bf16[512,768]{1,0:T(8,128)(2,1)S(1)} %get-tuple-element.198.refs_4_) | copy-start | bytes 2359300
  490.2 5.5 copy-start.15
  527.1 4.2 copy-start.39
  527.7 4.4 copy-start.29
  528.5 3.6 copy-start.10
  531.3 4.4 copy-start.6
  532.1 3.6 copy-start.3
  532.1 3.6 copy-start.58
  541.2 36.7 %copy-start.18 = (f32[512,768]{1,0:T(8,128)}, f32[512,768]{1,0:T(8,128)S(1)}, u32[]{:S(2)}) copy-start(f32[512,768]{1,0:T(8,128)S(1)} %get-tuple-element.209.d_out) | copy-start | bytes 4718596
  577.8 24.1 %copy-start.16 = (f32[512,1024]{1,0:T(8,128)S(1)}, f32[512,1024]{1,0:T(8,128)}, u32[]{:S(2)}) copy-start(f32[512,1024]{1,0:T(8,128)} %get-tuple-element.190) | copy-start | bytes 6291460
  602.2 17.8 %copy-start.7 = (f32[512,768]{1,0:T(8,128)}, f32[512,768]{1,0:T(8,128)S(1)}, u32[]{:S(2)}) copy-start(f32[512,768]{1,0:T(8,128)S(1)} %slice_multiply_fusion.4) | copy-start | bytes 4718596
  602.2 15.8 %copy-start.52 = (f32[512]{0:T(512)S(1)}, f32[512]{0:T(512)}, u32[]{:S(2)}) copy-start(f32[512]{0:T(512)} %copy-done.51) | copy-start | bytes 6148
  602.2 15.8 %copy-start.54 = (f32[512]{0:T(512)S(1)}, f32[512]{0:T(512)}, u32[]{:S(2)}) copy-start(f32[512]{0:T(512)} %copy-done.53) | copy-start | bytes 6148
  602.2 15.8 %copy-start.56 = (f32[512]{0:T(512)S(1)}, f32[512]{0:T(512)}, u32[]{:S(2)}) copy-start(f32[512]{0:T(512)} %copy-done.55) | copy-start | bytes 6148
  618.1 5.3 copy-start.66
  618.1 5.3 copy-start.68
  618.1 5.3 copy-start.70
  620.0 7.1 copy-start.48
  620.0 7.2 copy-start.8
  629.5 3.6 copy-start.22
  716.5 6.6 copy-start.35
  716.5 12.7 %copy-start.27 = (bf16[4,128,1536]{2,1,0:T(8,128)(2,1)S(1)}, bf16[4,128,1536]{2,1,0:T(8,128)(2,1)}, u32[]{:S(2)}) copy-start(bf16[4,128,1536]{2,1,0:T(8,128)(2,1)} %get-tuple-element.92) | copy-start | bytes 4718596
  731.4 2.8 copy-start.21
  732.7 3.3 copy-start.26
  (30 other events, 41.5 us)
Sparse Core Ops, SparseCore 0:
  123.0 92.4 all-gather.1
  527.2 109.3 reduce-scatter.1

commit v2 on v1

--- a/solution.py
+++ b/solution.py
@@ -487,14 +487,16 @@
         rows = out.shape[2]
         base = pl.multiple_of(self.m * rows, rows) if x.shape[0] > rows else 0
         self.x = x.at[pl.ds(base, rows)]
-        self.pieces = [(0,) + c for c in chunk_rows(0, rows)] + [(1,) + c for c in chunk_rows(0, both)]
+        self.pieces = [(0,) + c for c in chunk_rows(0, both) + chunk_rows(both, rows - both)]
+        self.pieces += [(1,) + c for c in chunk_rows(0, both)]
         self.sent, self.pending = [], {}
         self.ring, self.chips = {}, {}
 
     @staticmethod
     def scratch(n, rows, both):
         dma = pltpu.SemaphoreType.DMA
-        own, far = len(chunk_rows(0, rows)), len(chunk_rows(0, both))
+        far = len(chunk_rows(0, both))
+        own = far + len(chunk_rows(both, rows - both))
         steps = n // 2
         return [
             dma((3,)),
@@ -791,7 +793,7 @@
 def gather_tokens(x, position, small, weights, cot, units, cid):
     n, own, tokens = position.shape
     quarter, model = x.shape
-    both = quarter // 2
+    both = quarter // 128 * 48
     return pl.pallas_call(
         partial(token_gather_kernel, n, both, own, units),
         out_shape=[
@@ -2117,8 +2119,6 @@
     cot_all = cot_all.reshape(n, tokens, model)
     pack_b, small_all = lax.optimization_barrier((pack_b, small_all))
     weight_b = lax.all_gather(pack_b, "dp", axis=0, tiled=True)
-    out_t = weight_b[:, :inner]
-    router_w = weight_b[:, inner + 3 * hidden_units :]
 
     pieces = []
     start = 0
@@ -2217,6 +2217,14 @@
     gate_act = jax.nn.silu(gate_z)
     gated = ssd * gate_act
     scaled = (gated * gated_row).astype(BF)
+    unit_first = hidden_ext[16:] * inv_ext[16:]
+    mine_unit = lax.dynamic_slice_in_dim(unit_first, mp_place * quarter, quarter, 0)
+    entry_wide = dot(group_entry, expand, precision=HIGH)
+    unit_first, mine_unit, entry_wide, weight_b = lax.optimization_barrier(
+        (unit_first, mine_unit, entry_wide, weight_b)
+    )
+    out_t = weight_b[:, :inner]
+    router_w = weight_b[:, inner + 3 * hidden_units :]
     proj_part = dot(scaled, out_t, ((1,), (1,)))
     square_part = jnp.sum(gated * gated, axis=1, keepdims=True)
     proj_pack = jnp.concatenate([proj_part, jnp.broadcast_to(square_part, (tokens, LANES))], axis=1)
@@ -2310,14 +2318,14 @@
     )
     grad_b, got = lax.optimization_barrier((grad_b, got))
     d_proj = got[:, :model]
-    sum_b = lax.psum_scatter(grad_b, "dp", scatter_dimension=0, tiled=True).astype(F32)
+    sum_b = lax.psum_scatter(grad_b, "dp", scatter_dimension=0, tiled=True)
     d_scaled = dot(d_proj, out_t)
     grad_gated_row = jnp.sum(d_scaled * gated, axis=0)
     d_gated = d_scaled * gated_row + 2.0 * gated * d_square_all
     d_ssd = d_gated * gate_act
     d_gate_z = d_gated * ssd * silu_slope(gate_z)
 
-    direct = dot(d_ssd * dot(group_entry, expand, precision=HIGH), read, rows0, HIGH)
+    direct = dot(d_ssd * entry_wide, read, rows0, HIGH)
     if n == 8:
         (state_grad,) = state_scan(direct, jnp.broadcast_to(group_decay, (8, LANES)), expand, 6, BF)
     else:
@@ -2381,8 +2389,6 @@
         d_state_mine, weight_a[:, 2 * inner : 2 * inner + state_cols], ((1,), (1,))
     )
     grad_a = dot(normed, d_a, rows0).astype(BF)
-    unit_first = hidden_ext[16:] * inv_ext[16:]
-    mine_unit = lax.dynamic_slice_in_dim(unit_first, mp_place * quarter, quarter, 0)
     grad_gain_first = jnp.sum(d_normed_part * unit_first, axis=0) + jnp.sum(
         d_state_rows * mine_unit, axis=0
     )
@@ -2442,11 +2448,11 @@
         state_sum[taps],
         head_sum,
         value_sum[taps + 1],
-        sum_b[:, :b1].T,
+        sum_b[:, :b1].T.astype(F32),
         gains_sum[shard : 2 * shard],
-        sum_b[:, b3 : b3 + EXPERTS],
-        sum_b[:, b1:b2].reshape(shard, 2, hidden_units),
-        sum_b[:, b2:b3].T,
+        sum_b[:, b3 : b3 + EXPERTS].astype(F32),
+        sum_b[:, b1:b2].reshape(shard, 2, hidden_units).astype(F32),
+        sum_b[:, b2:b3].T.astype(F32),
         grad_expert_in,
         grad_expert_out,
     )

time: 750 us -> 750 us (level)
    unnamed x171 -> x105, local copies, waits for them, and re-layouts: 14.7 us -> 17.1 us
where the time goes in v2:
time: 750 us; the launch traced here: 745 us
  Pallas kernels  589 us (79%)
  local copies, waits for them, and re-layouts  52.7 us (7%)
  matrix products  41.1 us (5%)
  other arithmetic  40.3 us (5%)
  between operations  15.5 us (2%)
    pallas_call x1, Pallas kernels, put_scatter(): pl.pallas_call(partial(put_scatter_kernel, n, own), out_shape=[jax.ShapeD...  132 us
    pallas_call x1, Pallas kernels, first_gather(): pl.pallas_call(partial(first_kernel, n, k), out_shape=[jax.ShapeDtypeStru...  102 us
    pallas_call x1, Pallas kernels, gather_tokens(): pl.pallas_call(partial(token_gather_kernel, n, both, own, units), out_sha...  80.5 us
    pallas_call x1, Pallas kernels, last_exchange(): pl.pallas_call(partial(last_kernel, n), out_shape=[jax.ShapeDtypeStruct((...  73 us
    pallas_call x2, Pallas kernels, state_scan(): pl.pallas_call(partial(state_scan_kernel, n, own), out_shape=out_shape, i...  70.6 us
    dot_general x14, matrix products, dot(): lax.dot_general(a, b, (dims, ((), ())), precision=precision, preferred_el...  40.7 us
    pallas_call x1, Pallas kernels, run_experts(): pl.pallas_call(partial(expert_kernel, own, slots // part), grid=(own, slo...  33.6 us
    pallas_call x1, Pallas kernels, recur_backward(): pl.pallas_call(partial(adjoint_kernel, width // LANES), grid=(blocks,), o...  24.4 us
  transfers between devices with their start and end apart: 2, of which 1 were waited for; matrix products, arithmetic and copies ran while one was open for 12% of the time, Pallas kernels for 26%

profile of v2, /device:TPU:0, one launch (start us, length us, event | category | flops | bytes accessed | tf_op | source)
XLA Modules:
  0.0 744.7 jit_solution(44519098890634461)
XLA Ops:
  15.7 2.1 concatenate.73
  17.9 1.8 fusion.31.refs_0_
  20.3 101.6 %shard_map.348 = (bf16[8,192,1920]{2,1,0:T(8,128)(2,1)}, bf16[8,16,1536]{2,1,0:T(8,128)(2,1)}, bf16[8,4,128,1536]{3,2,1,0:T(8,128)(2,1)}) custom-call(bf16[192,1920]{1,0:T(8,128)(2,1)} %fusion.31.refs_0_, bf16[16,1536]{1,0:T(8,128)(2,1)} %fusion.61.refs_1_, bf16[512,1536]{1,0:T(8,128)(2,1)} %refs_2_.3), custom_call_target="tpu_custom_call" | custom-call | tf_op jit(solution)/shard_map/pallas_call | solution.py:869
  130.9 1.4 fusion.71
  133.1 6.3 fusion.103
  139.4 3.2 add_multiply_fusion
  143.2 1.4 slice.528.values
  147.7 2.6 fusion.25.refs_0_
  150.4 37.6 %shard_map.349 = (f32[768,128]{1,0:T(8,128)S(1)}, bf16[8,8,64,1536]{3,2,1,0:T(8,128)(2,1)}, f32[8,8,512]{2,1,0:T(8,128)S(1)}) custom-call(f32[768,128]{1,0:T(8,128)S(1)} %fusion.25.refs_0_, f32[8,128]{1,0:T(8,128)S(1)} %broadcast_in_dim.102.refs_1_, f32[128,768]{1,0:T(8,128)S(1)} %fusion.39.refs_2_.expand, bf16[8,512,1536]{2,1,0:T(8,128)(2,1)} %bitcast.165, ...), custom_call_target="tpu_custom_call" | custom-call | tf_op jit(solution)/shard_map/pallas_call | solution.py:1846
  188.6 10.0 %shard_map.350 = (f32[512,768]{1,0:T(8,128)S(1)}, f32[4,768,128]{2,1,0:T(8,128)S(1)}) custom-call(f32[512,768]{1,0:T(8,128)} %slice.528.values, f32[512,128]{1,0:T(8,128)S(1)} %get-tuple-element.220.write, f32[512,128]{1,0:T(8,128)S(1)} %get-tuple-element.219.read, f32[512,128]{1,0:T(8,128)S(1)} %bitcast.160, f32[16,512]{1,0:T(8,128)S(1)} %copy.80.cumul_t, ...), custom_call_target="tpu_custom_call" | custom-call | tf_op jit(solution)/shard_map/pallas_call | solution.py:1530
  198.7 3.0 multiply_convert_fusion.2
  201.8 1.2 copy-done.19
  204.7 1.7 copy-done.12
  207.3 2.0 fusion.36
  209.3 6.3 all-gather.2.cloned.1.call-done.weights
  215.5 3.1 fusion.12
  219.0 23.1 %shard_map.351 = f32[128,1664]{1,0:T(8,128)S(1)} custom-call(f32[4,128,1664]{2,1,0:T(8,128)S(1)} %bitcast.156), custom_call_target="tpu_custom_call" | custom-call | tf_op jit(solution)/shard_map/pallas_call | solution.py:414
  242.2 1.3 multiply_reduce_fusion.12
  245.3 80.5 %shard_map.352 = (bf16[8,4,128,1536]{3,2,1,0:T(8,128)(2,1)}, bf16[8,8,64,1536]{3,2,1,0:T(8,128)(2,1)}, f32[8,512,128]{2,1,0:T(8,128)}, f32[8,8,64,128]{3,2,1,0:T...) custom-call(bf16[128,1536]{1,0:T(8,128)(2,1)} %multiply_convert_fusi, ...), custom_call_target="tpu_custom_call" | custom-call | tf_op jit(solution)/shard_map/pallas_call | solution.py:797
  325.8 33.6 %shard_map.353 = (f32[8,3072,128]{2,1,0:T(8,128)}, f32[8,128,1536]{2,1,0:T(8,128)}, bf16[8,512,1536]{2,1,0:T(8,128)(2,1)}, bf16[8,512,1536]{2,1,0:T(8,128)(2,1)}, bf16[8,512,128]{2,1,0:T(8,128)(2,1)}) custom-call(bf16[8,512,1536]{2,1,0:T(8,128)(2,1)} %bitcast.167, bf16[8,512,1536]{2,1,0:T(8,128)(2,1)} %bitcast.166, f32[8,512,128]{2,1,0:T(8,128)} %bitcast.178, ...), custom_call_target="tpu_custom_call" | custom-call | tf_op jit(solution)/shard_map/pallas_call | solution.py:1943
  359.4 132.2 %shard_map.354 = (f32[128,3200]{1,0:T(8,128)}, bf16[8,2,128,3200]{3,2,1,0:T(8,128)(2,1)}) custom-call(f32[8,8,512]{2,1,0:T(8,128)} %copy-done.3, bf16[8,8,64,1536]{3,2,1,0:T(8,128)(2,1)} %bitcast.169, bf16[8,8,64,1536]{3,2,1,0:T(8,128)(2,1)} %bitcast.168, bf16[8,8,64,128]{3,2,1,0:T(8,128)(2,1)} %bitcast.182, f32[512,1536]{1,0:T(8,128)} %get-tuple-element.79.shared_a, ...), custom_call_target="tpu_custom_call" | custom-call | tf_op jit(solution)/shard_map/pallas_call | solution.py:1337
  493.7 2.9 multiply_reduce_fusion.8
  496.5 1.4 multiply_reduce_fusion.10
  499.9 1.9 concatenate.83.refs_0_
  501.7 15.9 %shard_map.355 = bf16[4,128,1664]{2,1,0:T(8,128)(2,1)} custom-call(bf16[128,1664]{1,0:T(8,128)(2,1)} %concatenate.83.refs_0_), custom_call_target="tpu_custom_call" | custom-call | tf_op jit(solution)/shard_map/pallas_call | solution.py:465
  519.2 8.7 %shard_map.356 = bf16[1536,1664]{1,0:T(8,128)(2,1)} custom-call(bf16[512,1664]{1,0:T(8,128)(2,1)} %bitcast.171, bf16[512,1536]{1,0:T(8,128)(2,1)} %get-tuple-element.83.refs_1_.refs_3_, bf16[512,1536]{1,0:T(8,128)(2,1)} %refs_2_.3, bf16[512,1536]{1,0:T(8,128)(2,1)} %get-tuple-element.83.refs_1_.refs_3_, bf16[512,768]{1,0:T(8,128)(2,1)} %copy-done.21, ...), custom_call_target="tpu_custom_call" | custom-call | tf_op jit(solution)/shard_map/pallas_call | solution.py:2014
  529.4 2.0 dynamic-slice_convert_fusion.hidden
  531.4 1.2 multiply_reduce_fusion.14
  532.6 6.8 multiply_convert_fusion.1
  539.4 3.8 fusion.21.refs_0_
  543.2 33.0 %shard_map.357.start = f32[768,128]{1,0:T(8,128)S(1)} custom-call(f32[768,128]{1,0:T(8,128)S(1)} %fusion.21.refs_0_, f32[8,128]{1,0:T(8,128)S(1)} %broadcast_in_dim.102.refs_1_, f32[128,768]{1,0:T(8,128)S(1)} %fusion.39.refs_2_.expand), custom_call_target="tpu_custom_call" | custom-call | tf_op jit(solution)/shard_map/pallas_call | solution.py:1846
  576.2 24.4 %shard_map.358 = (f32[512,768]{1,0:T(8,128)S(1)}, f32[512,128]{1,0:T(8,128)S(1)}, f32[512,128]{1,0:T(8,128)S(1)}, f32[512,128]{1,0:T(8,128)S(1)}, f32[512,128]{1,0:T(8,128)S(1)}, /*index=5*/f32[1,768]{1,0:T(1,128)S(1)}) custom-call(f32[512,768]{1,0:T(8,128)} %slice.528.values, f32[512,128]{1,0:T(8,128)S(1)} %get-tuple-element.220.write, ...), custom_call_target="tpu_custom_call" | custom-call | tf_op jit(solution)/shard_map/pallas_call | solution.py:1657
  601.0 14.7 %shard_map.359 = (f32[512,256]{1,0:T(8,128)S(1)}, f32[16,1024]{1,0:T(8,128)S(1)}) custom-call(f32[512,256]{1,0:T(8,128)S(1)} %pad_maximum_fusion.5.part, f32[16,256]{1,0:T(8,128)S(1)} %slice.548.slope, f32[16,768]{1,0:T(8,128)S(1)} %slice.549.rim), custom_call_target="tpu_custom_call" | custom-call | tf_op jit(solution)/shard_map/pallas_call | solution.py:1429
  615.9 1.9 multiply_reduce_fusion.2
  619.7 1.3 copy.89
  621.2 1.7 fusion.90
  624.6 1.6 fusion.5
  627.7 1.3 multiply_reduce_fusion.9
  629.0 2.6 fusion
  631.7 1.7 fusion.95
  634.2 6.5 convolution_convert_fusion
  640.7 73.0 %shard_map.360 = (f32[192,1536]{1,0:T(8,128)}, f32[192,256]{1,0:T(8,128)}, f32[192,128]{1,0:T(8,128)}, f32[32,128]{1,0:T(8,128)}, f32[16,128]{1,0:T(8,128)}, /*i...) custom-call(bf16[8,192,1920]{2,1,0:T(8,128)(2,1)} %bitcast.176, f32[8,32,128]{2,1,0:T(8,128)} %bitcast.186, ...), custom_call_target="tpu_custom_call" | custom-call | tf_op jit(solution)/shard_map/pallas_call | solution.py:358
  715.3 1.3 slice.561
  717.4 3.0 reshape.483
  725.1 1.4 fusion.101
  726.5 2.2 bitcast_convert_fusion
  732.3 1.9 convert_bitcast_fusion
  734.2 1.6 convert_bitcast_fusion.1
  (250 shorter events, 53.7 us)
Async XLA Ops:
  7.2 208.3 %all-gather.2.cloned.1.call-start = ((), (), s32[]{:S(2)}) async-start(), calls=%async_computation.1 | async-start | bytes 5750784 | tf_op jit(solution)/shard_map/all_gather | solution.py:2121
  11.0 110.9 %copy-start.31 = (bf16[768,192]{0,1:T(8,128)(2,1)S(1)}, bf16[768,192]{0,1:T(8,128)(2,1)}, u32[]{:S(2)}) copy-start(bf16[768,192]{0,1:T(8,128)(2,1)} %param.34) | copy-start | bytes 884740
  11.0 110.9 %copy-start.33 = (bf16[256,192]{0,1:T(8,128)(2,1)S(1)}, bf16[256,192]{0,1:T(8,128)(2,1)}, u32[]{:S(2)}) copy-start(bf16[256,192]{0,1:T(8,128)(2,1)} %param.38) | copy-start | bytes 294916
  20.3 107.2 %copy-start.35 = (s32[4096]{0:T(1024)S(1)}, s32[4096]{0:T(1024)}, u32[]{:S(2)}) copy-start(s32[4096]{0:T(1024)} %param.22) | copy-start | bytes 49156
  121.9 7.4 copy-start
  122.0 7.4 copy-start.8
  122.9 605.8 %reduce-scatter.2.cloned.1.call-start = ((), (), s32[]{:S(2)}) async-start(), calls=%async_computation.2 | async-start | bytes 5750784 | tf_op jit(solution)/shard_map/reduce_scatter | solution.py:2321
  133.1 6.3 copy-start.25
  139.3 5.3 copy-start.4
  143.2 2.0 copy-start.10
  143.2 1.4 copy-start.38
  144.6 1.4 copy-start.36
  146.1 1.6 copy-start.11
  188.0 0.7 copy-start.3
  198.7 3.1 copy-start.1
  198.7 3.1 copy-start.2
  201.8 1.2 copy-start.19
  201.8 13.8 %copy-start.21 = (bf16[512,768]{1,0:T(8,128)(2,1)}, bf16[512,768]{1,0:T(8,128)(2,1)S(1)}, u32[]{:S(2)}) copy-start(bf16[512,768]{1,0:T(8,128)(2,1)S(1)} %get-tuple-element.204.refs_4_) | copy-start | bytes 2359300
  201.8 2.3 copy-start.9
  204.7 1.7 copy-start.12
  243.5 0.9 copy-start.14
  491.6 4.9 copy-start.15
  497.9 0.9 copy-start.17
  532.6 6.8 copy-start.20
  539.4 36.8 %copy-start.18 = (f32[512,768]{1,0:T(8,128)}, f32[512,768]{1,0:T(8,128)S(1)}, u32[]{:S(2)}) copy-start(f32[512,768]{1,0:T(8,128)S(1)} %get-tuple-element.215.d_out) | copy-start | bytes 4718596
  576.2 24.5 %copy-start.16 = (f32[512,1024]{1,0:T(8,128)S(1)}, f32[512,1024]{1,0:T(8,128)}, u32[]{:S(2)}) copy-start(f32[512,1024]{1,0:T(8,128)} %get-tuple-element.196) | copy-start | bytes 6291460
  600.7 15.2 %copy-start.5 = (f32[528,1920]{1,0:T(8,128)S(1)}, f32[528,1920]{1,0:T(8,128)}, u32[]{:S(2)}) copy-start(f32[528,1920]{1,0:T(8,128)} %copy-done.4) | copy-start | bytes 12165124
  600.9 16.9 %copy-start.6 = (f32[512,768]{1,0:T(8,128)}, f32[512,768]{1,0:T(8,128)S(1)}, u32[]{:S(2)}) copy-start(f32[512,768]{1,0:T(8,128)S(1)} %slice_multiply_fusion.4) | copy-start | bytes 4718596
  615.9 5.3 copy-start.37
  617.8 6.5 copy-start.7
  619.0 0.7 copy-start.30
  624.3 2.2 slice-start
  624.6 2.2 copy-start.22
  624.6 3.1 slice-start.1
  626.2 5.4 copy-start.23
  626.2 2.8 copy-start.39
  629.0 2.7 copy-start.13
  629.0 2.7 copy-start.29
  631.6 2.6 copy-start.24
  631.7 2.6 copy-start.26
  713.7 6.6 copy-start.34
  713.7 12.8 %copy-start.28 = (bf16[4,128,1536]{2,1,0:T(8,128)(2,1)S(1)}, bf16[4,128,1536]{2,1,0:T(8,128)(2,1)}, u32[]{:S(2)}) copy-start(bf16[4,128,1536]{2,1,0:T(8,128)(2,1)} %get-tuple-element.100) | copy-start | bytes 4718596
  728.7 7.0 copy-start.27
  732.3 4.6 copy-start.32
Sparse Core Ops, SparseCore 0:
  123.0 92.4 all-gather.1
  528.1 108.7 reduce-scatter.1

commit v3 on v2

--- a/solution.py
+++ b/solution.py
@@ -2289,9 +2289,8 @@
     d_square = d_inv * -0.5 * inv_gated * inv_gated * inv_gated / DI
     d_square_high = d_square.astype(BF)
     d_square_low = (d_square - d_square_high.astype(F32)).astype(BF)
-    sent = jnp.concatenate(
+    side = jnp.concatenate(
         [
-            d_proj_mine,
             d_logits[:, :EXPERTS],
             d_square_high,
             d_square_low,
@@ -2299,26 +2298,22 @@
         ],
         axis=1,
     )
-    (got,) = gather_mp([sent], 5)
-    got = got.reshape(tokens, model + LANES)
-    d_proj = got[:, :model]
-    d_logits_all = jnp.pad(got[:, model : model + EXPERTS], ((0, 0), (0, LANES - EXPERTS)))
-    d_square_all = got[:, model + EXPERTS : model + EXPERTS + 1].astype(F32) + got[
-        :, model + EXPERTS + 1 : model + EXPERTS + 2
-    ].astype(F32)
+    d_proj, side = gather_mp([d_proj_mine, side], 5)
+    d_proj = d_proj.reshape(tokens, model)
+    side = side.reshape(tokens, LANES)
+    d_square_all = side[:, EXPERTS : EXPERTS + 1].astype(F32) + side[:, EXPERTS + 1 : EXPERTS + 2].astype(F32)
 
     rows0 = ((0,), (0,))
     grad_b = weight_grads(
         [
-            (got, scaled),
+            (d_proj, scaled),
             (ffn_block, d_shared_mid),
             (cotangent, shared_act),
-            (ffn_block, d_logits_all),
+            (ffn_block, side),
         ]
     )
-    grad_b, got = lax.optimization_barrier((grad_b, got))
-    d_proj = got[:, :model]
-    sum_b = lax.psum_scatter(grad_b, "dp", scatter_dimension=0, tiled=True)
+    grad_b, d_proj = lax.optimization_barrier((grad_b, d_proj))
+    sum_b = lax.psum_scatter(grad_b, "dp", scatter_dimension=0, tiled=True).astype(F32)
     d_scaled = dot(d_proj, out_t)
     grad_gated_row = jnp.sum(d_scaled * gated, axis=0)
     d_gated = d_scaled * gated_row + 2.0 * gated * d_square_all
@@ -2448,11 +2443,11 @@
         state_sum[taps],
         head_sum,
         value_sum[taps + 1],
-        sum_b[:, :b1].T.astype(F32),
+        sum_b[:, :b1].T,
         gains_sum[shard : 2 * shard],
-        sum_b[:, b3 : b3 + EXPERTS].astype(F32),
-        sum_b[:, b1:b2].reshape(shard, 2, hidden_units).astype(F32),
-        sum_b[:, b2:b3].T.astype(F32),
+        sum_b[:, b3 : b3 + EXPERTS],
+        sum_b[:, b1:b2].reshape(shard, 2, hidden_units),
+        sum_b[:, b2:b3].T,
         grad_expert_in,
         grad_expert_out,
     )

time: 750 us -> 740 us (0.987)
    unnamed x105 -> x109, local copies, waits for them, and re-layouts: 17.1 us -> 17 us
where the time goes in v3:
time: 740 us; the launch traced here: 735 us
  Pallas kernels  585 us (79%)
  local copies, waits for them, and re-layouts  50.8 us (7%)
  matrix products  41.1 us (6%)
  other arithmetic  36 us (5%)
  between operations  15.5 us (2%)
    pallas_call x1, Pallas kernels, put_scatter(): pl.pallas_call(partial(put_scatter_kernel, n, own), out_shape=[jax.ShapeD...  132 us
    pallas_call x1, Pallas kernels, first_gather(): pl.pallas_call(partial(first_kernel, n, k), out_shape=[jax.ShapeDtypeStru...  102 us
    pallas_call x1, Pallas kernels, gather_tokens(): pl.pallas_call(partial(token_gather_kernel, n, both, own, units), out_sha...  80.6 us
    pallas_call x1, Pallas kernels, last_exchange(): pl.pallas_call(partial(last_kernel, n), out_shape=[jax.ShapeDtypeStruct((...  70.6 us
    pallas_call x2, Pallas kernels, state_scan(): pl.pallas_call(partial(state_scan_kernel, n, own), out_shape=out_shape, i...  70.3 us
    dot_general x14, matrix products, dot(): lax.dot_general(a, b, (dims, ((), ())), precision=precision, preferred_el...  40.7 us
    pallas_call x1, Pallas kernels, run_experts(): pl.pallas_call(partial(expert_kernel, own, slots // part), grid=(own, slo...  33.7 us
    pallas_call x1, Pallas kernels, recur_backward(): pl.pallas_call(partial(adjoint_kernel, width // LANES), grid=(blocks,), o...  24.4 us
  transfers between devices with their start and end apart: 2, of which 1 were waited for; matrix products, arithmetic and copies ran while one was open for 12% of the time, Pallas kernels for 26%

profile of v3, /device:TPU:0, one launch (start us, length us, event | category | flops | bytes accessed | tf_op | source)
XLA Modules:
  0.0 735.1 jit_solution(8554613865765662246)
XLA Ops:
  9.9 1.1 copy.98
  15.7 2.1 concatenate.73
  17.9 1.8 fusion.30.refs_0_
  20.3 101.6 %shard_map.348 = (bf16[8,192,1920]{2,1,0:T(8,128)(2,1)}, bf16[8,16,1536]{2,1,0:T(8,128)(2,1)}, bf16[8,4,128,1536]{3,2,1,0:T(8,128)(2,1)}) custom-call(bf16[192,1920]{1,0:T(8,128)(2,1)} %fusion.30.refs_0_, bf16[16,1536]{1,0:T(8,128)(2,1)} %fusion.60.refs_1_, bf16[512,1536]{1,0:T(8,128)(2,1)} %refs_2_.3), custom_call_target="tpu_custom_call" | custom-call | tf_op jit(solution)/shard_map/pallas_call | solution.py:869
  130.9 1.4 fusion.70
  133.1 6.3 fusion.102
  139.4 3.2 add_multiply_fusion
  143.2 1.4 slice.520.values
  147.8 2.6 fusion.24.refs_0_
  150.4 37.6 %shard_map.349 = (f32[768,128]{1,0:T(8,128)S(1)}, bf16[8,8,64,1536]{3,2,1,0:T(8,128)(2,1)}, f32[8,8,512]{2,1,0:T(8,128)S(1)}) custom-call(f32[768,128]{1,0:T(8,128)S(1)} %fusion.24.refs_0_, f32[8,128]{1,0:T(8,128)S(1)} %broadcast_in_dim.102.refs_1_, f32[128,768]{1,0:T(8,128)S(1)} %fusion.38.refs_2_.expand, bf16[8,512,1536]{2,1,0:T(8,128)(2,1)} %bitcast.167, ...), custom_call_target="tpu_custom_call" | custom-call | tf_op jit(solution)/shard_map/pallas_call | solution.py:1846
  188.7 10.0 %shard_map.350 = (f32[512,768]{1,0:T(8,128)S(1)}, f32[4,768,128]{2,1,0:T(8,128)S(1)}) custom-call(f32[512,768]{1,0:T(8,128)} %slice.520.values, f32[512,128]{1,0:T(8,128)S(1)} %get-tuple-element.224.write, f32[512,128]{1,0:T(8,128)S(1)} %get-tuple-element.223.read, f32[512,128]{1,0:T(8,128)S(1)} %bitcast.162, f32[16,512]{1,0:T(8,128)S(1)} %copy.80.cumul_t, ...), custom_call_target="tpu_custom_call" | custom-call | tf_op jit(solution)/shard_map/pallas_call | solution.py:1530
  198.7 3.0 multiply_convert_fusion.2
  201.8 1.2 copy-done.19
  204.8 1.7 copy-done.12
  207.4 2.0 fusion.35
  209.3 6.2 all-gather.2.cloned.1.call-done.weights
  215.5 3.1 fusion.12
  219.0 23.1 %shard_map.351 = f32[128,1664]{1,0:T(8,128)S(1)} custom-call(f32[4,128,1664]{2,1,0:T(8,128)S(1)} %bitcast.158), custom_call_target="tpu_custom_call" | custom-call | tf_op jit(solution)/shard_map/pallas_call | solution.py:414
  242.2 1.3 multiply_reduce_fusion.12
  245.3 80.6 %shard_map.352 = (bf16[8,4,128,1536]{3,2,1,0:T(8,128)(2,1)}, bf16[8,8,64,1536]{3,2,1,0:T(8,128)(2,1)}, f32[8,512,128]{2,1,0:T(8,128)}, f32[8,8,64,128]{3,2,1,0:T...) custom-call(bf16[128,1536]{1,0:T(8,128)(2,1)} %multiply_convert_fusi, ...), custom_call_target="tpu_custom_call" | custom-call | tf_op jit(solution)/shard_map/pallas_call | solution.py:797
  325.9 33.7 %shard_map.353 = (f32[8,3072,128]{2,1,0:T(8,128)}, f32[8,128,1536]{2,1,0:T(8,128)}, bf16[8,512,1536]{2,1,0:T(8,128)(2,1)}, bf16[8,512,1536]{2,1,0:T(8,128)(2,1)}, bf16[8,512,128]{2,1,0:T(8,128)(2,1)}) custom-call(bf16[8,512,1536]{2,1,0:T(8,128)(2,1)} %bitcast.169, bf16[8,512,1536]{2,1,0:T(8,128)(2,1)} %bitcast.168, f32[8,512,128]{2,1,0:T(8,128)} %bitcast.176, ...), custom_call_target="tpu_custom_call" | custom-call | tf_op jit(solution)/shard_map/pallas_call | solution.py:1943
  359.6 132.1 %shard_map.354 = (f32[128,3200]{1,0:T(8,128)}, bf16[8,2,128,3200]{3,2,1,0:T(8,128)(2,1)}) custom-call(f32[8,8,512]{2,1,0:T(8,128)} %copy-done.3, bf16[8,8,64,1536]{3,2,1,0:T(8,128)(2,1)} %bitcast.171, bf16[8,8,64,1536]{3,2,1,0:T(8,128)(2,1)} %bitcast.170, bf16[8,8,64,128]{3,2,1,0:T(8,128)(2,1)} %bitcast.184, f32[512,1536]{1,0:T(8,128)} %get-tuple-element.81.shared_a, ...), custom_call_target="tpu_custom_call" | custom-call | tf_op jit(solution)/shard_map/pallas_call | solution.py:1337
  491.7 1.1 fusion.52
  493.7 2.9 multiply_reduce_fusion.8
  496.6 1.4 multiply_reduce_fusion.10
  500.6 16.0 %shard_map.355 = (bf16[4,128,1536]{2,1,0:T(8,128)(2,1)}, bf16[4,128,128]{2,1,0:T(8,128)(2,1)}) custom-call(bf16[128,1536]{1,0:T(8,128)(2,1)} %multiply_convert_fusion.3.refs_0_, bf16[128,128]{1,0:T(8,128)(2,1)} %maximum_maximum_fusion.refs_1_), custom_call_target="tpu_custom_call" | custom-call | tf_op jit(solution)/shard_map/pallas_call | solution.py:465
  516.6 8.8 %shard_map.356 = bf16[1536,1664]{1,0:T(8,128)(2,1)} custom-call(bf16[512,1536]{1,0:T(8,128)(2,1)} %bitcast.177, bf16[512,1536]{1,0:T(8,128)(2,1)} %get-tuple-element.86.refs_1_.refs_3_, bf16[512,1536]{1,0:T(8,128)(2,1)} %refs_2_.3, bf16[512,1536]{1,0:T(8,128)(2,1)} %get-tuple-element.86.refs_1_.refs_3_, bf16[512,768]{1,0:T(8,128)(2,1)} %copy-done.21, ...), custom_call_target="tpu_custom_call" | custom-call | tf_op jit(solution)/shard_map/pallas_call | solution.py:2014
  526.9 2.0 dynamic-slice_convert_fusion.hidden
  529.1 6.9 multiply_convert_fusion.1
  536.0 3.7 fusion.21.refs_0_
  539.7 32.7 %shard_map.357.start = f32[768,128]{1,0:T(8,128)S(1)} custom-call(f32[768,128]{1,0:T(8,128)S(1)} %fusion.21.refs_0_, f32[8,128]{1,0:T(8,128)S(1)} %broadcast_in_dim.102.refs_1_, f32[128,768]{1,0:T(8,128)S(1)} %fusion.38.refs_2_.expand), custom_call_target="tpu_custom_call" | custom-call | tf_op jit(solution)/shard_map/pallas_call | solution.py:1846
  572.4 24.4 %shard_map.358 = (f32[512,768]{1,0:T(8,128)S(1)}, f32[512,128]{1,0:T(8,128)S(1)}, f32[512,128]{1,0:T(8,128)S(1)}, f32[512,128]{1,0:T(8,128)S(1)}, f32[512,128]{1,0:T(8,128)S(1)}, /*index=5*/f32[1,768]{1,0:T(1,128)S(1)}) custom-call(f32[512,768]{1,0:T(8,128)} %slice.520.values, f32[512,128]{1,0:T(8,128)S(1)} %get-tuple-element.224.write, ...), custom_call_target="tpu_custom_call" | custom-call | tf_op jit(solution)/shard_map/pallas_call | solution.py:1657
  597.2 14.0 %shard_map.359 = (f32[512,256]{1,0:T(8,128)S(1)}, f32[16,1024]{1,0:T(8,128)S(1)}) custom-call(f32[512,256]{1,0:T(8,128)S(1)} %pad_maximum_fusion.5.part, f32[16,256]{1,0:T(8,128)S(1)} %slice.539.slope, f32[16,768]{1,0:T(8,128)S(1)} %slice.540.rim), custom_call_target="tpu_custom_call" | custom-call | tf_op jit(solution)/shard_map/pallas_call | solution.py:1429
  611.3 1.9 multiply_reduce_fusion.2
  615.2 1.3 copy.89
  616.7 1.7 fusion.89
  620.1 1.6 fusion.5
  623.1 1.3 multiply_reduce_fusion.9
  624.4 2.6 fusion
  627.1 1.7 fusion.94
  629.6 6.4 convolution_convert_fusion
  636.1 70.6 %shard_map.360 = (f32[192,1536]{1,0:T(8,128)}, f32[192,256]{1,0:T(8,128)}, f32[192,128]{1,0:T(8,128)}, f32[32,128]{1,0:T(8,128)}, f32[16,128]{1,0:T(8,128)}, /*i...) custom-call(bf16[8,192,1920]{2,1,0:T(8,128)(2,1)} %bitcast.174, f32[8,32,128]{2,1,0:T(8,128)} %bitcast.188, ...), custom_call_target="tpu_custom_call" | custom-call | tf_op jit(solution)/shard_map/pallas_call | solution.py:358
  708.3 1.3 slice.552
  710.3 3.0 reshape.487
  718.1 1.4 fusion.100
  719.5 2.2 bitcast_convert_fusion
  721.6 1.2 convert_element_type.224
  726.2 1.1 copy.121
  (254 shorter events, 49.4 us)
Async XLA Ops:
  7.2 208.3 %all-gather.2.cloned.1.call-start = ((), (), s32[]{:S(2)}) async-start(), calls=%async_computation.1 | async-start | bytes 5750784 | tf_op jit(solution)/shard_map/all_gather | solution.py:2121
  11.0 110.9 %copy-start.33 = (bf16[768,192]{0,1:T(8,128)(2,1)S(1)}, bf16[768,192]{0,1:T(8,128)(2,1)}, u32[]{:S(2)}) copy-start(bf16[768,192]{0,1:T(8,128)(2,1)} %param.34) | copy-start | bytes 884740
  11.0 110.9 %copy-start.35 = (bf16[256,192]{0,1:T(8,128)(2,1)S(1)}, bf16[256,192]{0,1:T(8,128)(2,1)}, u32[]{:S(2)}) copy-start(bf16[256,192]{0,1:T(8,128)(2,1)} %param.38) | copy-start | bytes 294916
  20.3 107.2 %copy-start.37 = (s32[4096]{0:T(1024)S(1)}, s32[4096]{0:T(1024)}, u32[]{:S(2)}) copy-start(s32[4096]{0:T(1024)} %param.22) | copy-start | bytes 49156
  121.9 7.4 %copy-start = (bf16[8,16,1536]{2,1,0:T(8,128)(2,1)S(1)}, bf16[8,16,1536]{2,1,0:T(8,128)(2,1)}, u32[]{:S(2)}) copy-start(bf16[8,16,1536]{2,1,0:T(8,128)(2,1)} %get-tuple-element.67.refs_4_.small) | copy-start | bytes 1179652
  122.0 7.4 %copy-start.8 = (bf16[512,1536]{1,0:T(8,128)(2,1)S(1)}, bf16[512,1536]{1,0:T(8,128)(2,1)}, u32[]{:S(2)}) copy-start(bf16[512,1536]{1,0:T(8,128)(2,1)} %param.21) | copy-start | bytes 4718596
  122.9 598.8 %reduce-scatter.2.cloned.1.call-start = ((), (), s32[]{:S(2)}) async-start(), calls=%async_computation.2 | async-start | bytes 5750784 | tf_op jit(solution)/shard_map/reduce_scatter | solution.py:2316
  133.1 6.3 copy-start.26
  139.3 5.3 copy-start.4
  143.2 2.0 copy-start.10
  143.2 1.4 copy-start.40
  144.6 0.9 copy-start.38
  146.2 1.6 copy-start.11
  188.0 0.7 copy-start.3
  198.7 3.1 copy-start.1
  198.7 3.1 copy-start.2
  201.8 1.2 copy-start.19
  201.8 13.7 %copy-start.21 = (bf16[512,768]{1,0:T(8,128)(2,1)}, bf16[512,768]{1,0:T(8,128)(2,1)S(1)}, u32[]{:S(2)}) copy-start(bf16[512,768]{1,0:T(8,128)(2,1)S(1)} %get-tuple-element.208.refs_4_) | copy-start | bytes 2359300
  201.8 2.3 copy-start.9
  204.8 1.7 copy-start.12
  243.5 0.9 copy-start.14
  491.7 4.9 copy-start.15
  498.0 0.9 copy-start.17
  525.5 3.4 copy-start.30
  529.1 6.9 copy-start.20
  536.0 36.4 %copy-start.18 = (f32[512,768]{1,0:T(8,128)}, f32[512,768]{1,0:T(8,128)S(1)}, u32[]{:S(2)}) copy-start(f32[512,768]{1,0:T(8,128)S(1)} %get-tuple-element.219.d_out) | copy-start | bytes 4718596
  572.4 24.5 %copy-start.16 = (f32[512,1024]{1,0:T(8,128)S(1)}, f32[512,1024]{1,0:T(8,128)}, u32[]{:S(2)}) copy-start(f32[512,1024]{1,0:T(8,128)} %get-tuple-element.200) | copy-start | bytes 6291460
  596.9 14.4 %copy-start.5 = (f32[528,1920]{1,0:T(8,128)S(1)}, f32[528,1920]{1,0:T(8,128)}, u32[]{:S(2)}) copy-start(f32[528,1920]{1,0:T(8,128)} %copy-done.4) | copy-start | bytes 12165124
  597.1 16.1 %copy-start.6 = (f32[512,768]{1,0:T(8,128)}, f32[512,768]{1,0:T(8,128)S(1)}, u32[]{:S(2)}) copy-start(f32[512,768]{1,0:T(8,128)S(1)} %slice_multiply_fusion.4) | copy-start | bytes 4718596
  611.3 5.3 copy-start.39
  613.3 6.5 copy-start.7
  614.5 0.7 copy-start.32
  619.7 2.2 slice-start
  620.0 2.2 copy-start.22
  620.1 3.0 slice-start.1
  621.6 5.4 copy-start.24
  621.7 2.7 copy-start.41
  624.4 2.7 copy-start.13
  624.4 2.7 copy-start.31
  627.1 2.6 copy-start.25
  627.1 2.6 copy-start.27
  706.7 6.6 copy-start.36
  706.7 12.7 %copy-start.29 = (bf16[4,128,1536]{2,1,0:T(8,128)(2,1)S(1)}, bf16[4,128,1536]{2,1,0:T(8,128)(2,1)}, u32[]{:S(2)}) copy-start(bf16[4,128,1536]{2,1,0:T(8,128)(2,1)} %get-tuple-element.104) | copy-start | bytes 4718596
  721.6 2.8 copy-start.23
  722.9 3.3 copy-start.28
  725.2 2.1 copy-start.34
Sparse Core Ops, SparseCore 0:
  123.0 92.4 all-gather.1
  525.6 107.7 reduce-scatter.1
